TPU v7x, 512 devices: a whole 4x8x8 slice. The times are simulated.
512 devices in a mesh: lon: 32 (over y, z_lo), lat: 16 (over x, z_hi, core).
Axes of the slice: x: 4, y: 8, z: 8 (z_hi: 2, z_lo: 4; z = z_hi * 4 + z_lo), core: 2. Of those that a mesh axis runs over, the one named last changes fastest.
Arguments:
- state: float32 [4, 40, 128, 4096], P(None, None, 'lat', 'lon'), may hold values from -6 to 6
- mixing: float32 [40, 128, 4096], P(None, 'lat', 'lon'), may hold values from 0.02 to 5
- wet_levels: int32 [128, 4096], P('lat', 'lon'), may hold values from 0 to 40, as said below
Outputs:
- new_state: float32 [4, 40, 128, 4096], P(None, None, 'lat', 'lon')
Inputs may be any that keep to these rules, and one draw needn't show every extreme that they name: `wet_levels`: 0 marks a land column; whole tiles of 8 x 128 columns may be land, except in the top 8 rows of the grid, where every column has at least one wet level.
All inputs are finite; a program needn't handle non-finite values.
Results may differ from a plain program's by a relative error of at most 0.0003.
Values sent between devices are 32-bit elements; how exact they have to be, the bound alone decides.
No kernel may reach another device: no remote copies, remote signals or barrier semaphores. Data moves between devices by JAX's collectives and lax.ppermute only.
A program may use at most 128 MiB of HBM per device.

v0:
```python
import math

import jax
import jax.numpy as jnp
from jax import lax
from jax.sharding import PartitionSpec as P

STEPS = 3


ADVECT = 0.15
DIFFUSE = 0.12
VISCOSITY = 0.1
PRESSURE = 0.03
CORIOLIS = 0.3
EXPAND_HEAT = 0.6
EXPAND_SALT = 0.8
TAPER_SCALE = 1.0


def with_halo(cells, sides, width, closed):
    for axis, dim in sides:
        count = lax.axis_size(axis)
        ends = count if closed else count - 1
        head = lax.slice_in_dim(cells, 0, width, axis=dim)
        tail = lax.slice_in_dim(cells, cells.shape[dim] - width, cells.shape[dim], axis=dim)
        cells = jnp.concatenate(
            [
                lax.ppermute(tail, axis, [(i, (i + 1) % count) for i in range(ends)]),
                cells,
                lax.ppermute(head, axis, [((i + 1) % count, i) for i in range(ends)]),
            ],
            axis=dim,
        )
    return cells


def slab_cut(array, lower_end, upper_end, direction):
    return lax.slice_in_dim(array, lower_end, upper_end, axis=direction)


def minmod(first_diff, second_diff):
    smaller = jnp.where(jnp.abs(first_diff) < jnp.abs(second_diff), first_diff, second_diff)
    return jnp.where(first_diff * second_diff > 0.0, smaller, 0.0)


def vertical_grad(array):
    padded = jnp.pad(array, ((0, 0), (1, 1), (0, 0), (0, 0)))
    return 0.5 * (padded[:, 2:] - padded[:, :-2])


def advect_div(tracer, speed, wetness, direction, length):
    diffs = (
        slab_cut(tracer, 1, length + 4, direction) - slab_cut(tracer, 0, length + 3, direction)
    ) * (slab_cut(wetness, 1, length + 4, direction) * slab_cut(wetness, 0, length + 3, direction))
    slopes = minmod(
        slab_cut(diffs, 1, length + 3, direction), slab_cut(diffs, 0, length + 2, direction)
    )
    left_value = slab_cut(tracer, 1, length + 2, direction) + 0.5 * slab_cut(
        slopes, 0, length + 1, direction
    )
    right_value = slab_cut(tracer, 2, length + 3, direction) - 0.5 * slab_cut(
        slopes, 1, length + 2, direction
    )
    face_wet = slab_cut(wetness, 1, length + 2, direction) * slab_cut(
        wetness, 2, length + 3, direction
    )
    face_speed = (
        0.5
        * (slab_cut(speed, 1, length + 2, direction) + slab_cut(speed, 2, length + 3, direction))
        * face_wet
    )
    fluxes = jnp.maximum(face_speed, 0.0) * left_value + jnp.minimum(face_speed, 0.0) * right_value
    return slab_cut(fluxes, 1, length + 1, direction) - slab_cut(fluxes, 0, length, direction)


def laplace_div(field, wetness, direction, length):
    face_wet = slab_cut(wetness, 0, length + 1, direction) * slab_cut(
        wetness, 1, length + 2, direction
    )
    fluxes = face_wet * (
        slab_cut(field, 1, length + 2, direction) - slab_cut(field, 0, length + 1, direction)
    )
    return slab_cut(fluxes, 1, length + 1, direction) - slab_cut(fluxes, 0, length, direction)


def isopycnal_div(tracer, density, wetness, direction, length):
    grad_tracer = vertical_grad(tracer)
    grad_density = vertical_grad(density)
    face_wet = slab_cut(wetness, 0, length + 1, direction) * slab_cut(
        wetness, 1, length + 2, direction
    )
    tracer_step = slab_cut(tracer, 1, length + 2, direction) - slab_cut(
        tracer, 0, length + 1, direction
    )
    density_step = slab_cut(density, 1, length + 2, direction) - slab_cut(
        density, 0, length + 1, direction
    )
    face_rz = 0.5 * (
        slab_cut(grad_density, 0, length + 1, direction)
        + slab_cut(grad_density, 1, length + 2, direction)
    )
    face_tz = 0.5 * (
        slab_cut(grad_tracer, 0, length + 1, direction)
        + slab_cut(grad_tracer, 1, length + 2, direction)
    )
    slope = density_step * face_rz / (face_rz * face_rz + TAPER_SCALE)
    fluxes = face_wet * (tracer_step - slope * face_tz)
    return slab_cut(fluxes, 1, length + 1, direction) - slab_cut(fluxes, 0, length, direction)


def thomas(field, coupling):
    layers = field.shape[1]
    upper_terms = []
    solved = []
    for layer_index in range(layers):
        above_term = -coupling[:, layer_index]
        if layer_index == 0:
            pivot_value = 1.0 + coupling[:, 0]
            right_value = field[:, 0]
        else:
            below_term = -coupling[:, layer_index - 1]
            diagonal = 1.0 + coupling[:, layer_index] + coupling[:, layer_index - 1]
            pivot_value = diagonal - below_term * upper_terms[-1]
            right_value = field[:, layer_index] - below_term * solved[-1]
        upper_terms.append(above_term / pivot_value)
        solved.append(right_value / pivot_value)
    result = [solved[-1]]
    for layer_index in range(layers - 2, -1, -1):
        result.append(solved[layer_index] - upper_terms[layer_index] * result[-1])
    return jnp.stack(result[::-1], axis=1)


def density_of(fields):
    return EXPAND_SALT * fields[1:2] - EXPAND_HEAT * fields[0:1]


def advance(field, coupling, wetness, wet_east, wet_north, pad_fn, row_coord, total_rows):
    columns = field.shape[3]
    row_count = field.shape[2]
    east_west, north_south = pad_fn(field, 2, (1.0, 1.0, -1.0, -1.0))
    advected = advect_div(east_west[0:2], east_west[2:3], wet_east, 3, columns) + advect_div(
        north_south[0:2], north_south[3:4], wet_north, 2, row_count
    )
    tracers = (field[0:2] - ADVECT * advected) * wetness
    near_east = slab_cut(east_west, 1, columns + 3, 3)
    near_north = slab_cut(north_south, 1, row_count + 3, 2)
    wet_near_east = slab_cut(wet_east, 1, columns + 3, 3)
    wet_near_north = slab_cut(wet_north, 1, row_count + 3, 2)
    pressure_east = PRESSURE * jnp.cumsum(density_of(near_east), axis=1)
    pressure_north = PRESSURE * jnp.cumsum(density_of(near_north), axis=1)
    push_east = 0.5 * (
        slab_cut(pressure_east, 2, columns + 2, 3) - slab_cut(pressure_east, 0, columns, 3)
    )
    push_north = 0.5 * (
        slab_cut(pressure_north, 2, row_count + 2, 2) - slab_cut(pressure_north, 0, row_count, 2)
    )
    friction = laplace_div(near_east[2:4], wet_near_east, 3, columns) + laplace_div(
        near_north[2:4], wet_near_north, 2, row_count
    )
    rotation = CORIOLIS * jnp.sin(math.pi * (row_coord + 0.5) / total_rows - 0.9)
    eastward = (
        field[2:3] + rotation * field[3:4] - push_east + VISCOSITY * friction[0:1]
    ) * wetness
    northward = (
        field[3:4] - rotation * field[2:3] - push_north + VISCOSITY * friction[1:2]
    ) * wetness
    diff_east, diff_north = pad_fn(tracers, 1, (1.0, 1.0))
    lateral = isopycnal_div(
        diff_east, density_of(diff_east), wet_near_east, 3, columns
    ) + isopycnal_div(diff_north, density_of(diff_north), wet_near_north, 2, row_count)
    tracers = (tracers + DIFFUSE * lateral) * wetness
    return thomas(jnp.concatenate([tracers, eastward, northward], axis=0), coupling)


def pad_tile(field, halo_width, sign_list):
    row_count = field.shape[2]
    columns = field.shape[3]
    half_cols = columns // 2
    east_west = with_halo(field, (("lon", 3),), halo_width, True)
    north_south = with_halo(field, (("lat", 2),), halo_width, False)
    sign_array = jnp.array(sign_list, dtype=jnp.float32).reshape(-1, 1, 1, 1)
    outgoing = field[:, :, row_count - 1 - halo_width : row_count - 1, :][:, :, ::-1, :]
    gathered = lax.all_gather(outgoing, "lon", axis=3, tiled=True)
    total_cols = gathered.shape[3]
    reversed_rows = gathered[..., ::-1]
    doubled = jnp.concatenate([reversed_rows, reversed_rows[..., :columns]], axis=3)
    start = (total_cols - half_cols + lax.axis_index("lon") * columns) % total_cols
    mirrored = lax.dynamic_slice_in_dim(doubled, start, columns, 3)
    on_top = lax.axis_index("lat") == lax.axis_size("lat") - 1
    top_rows = jnp.where(
        on_top, mirrored * sign_array, north_south[:, :, row_count + halo_width :, :]
    )
    north_south = jnp.concatenate([north_south[:, :, : row_count + halo_width], top_rows], axis=2)
    return (east_west, north_south)


def local(state, mixing, wet_levels):
    layers = state.shape[1]
    row_count = state.shape[2]
    levels = jnp.arange(layers, dtype=jnp.float32).reshape(1, layers, 1, 1)
    depth = wet_levels.astype(jnp.float32)[None, None]
    wetness = (levels < depth).astype(jnp.float32)
    depth_east, depth_north = pad_tile(depth, 2, (1.0,))
    wet_east = (levels < depth_east).astype(jnp.float32)
    wet_north = (levels < depth_north).astype(jnp.float32)
    below = jnp.concatenate([wetness[:, 1:], jnp.zeros_like(wetness[:, :1])], axis=1)
    coupling = mixing[None] * wetness * below
    row_coord = (lax.axis_index("lat") * row_count + jnp.arange(row_count)).astype(jnp.float32)[
        :, None
    ]
    total_rows = row_count * lax.axis_size("lat")
    field = state * wetness
    for step_index in range(STEPS):
        field = advance(
            field, coupling, wetness, wet_east, wet_north, pad_tile, row_coord, total_rows
        )
    return field


def solution(mesh):
    return jax.shard_map(
        local,
        mesh=mesh,
        in_specs=(P(None, None, "lat", "lon"), P(None, "lat", "lon"), P("lat", "lon")),
        out_specs=P(None, None, "lat", "lon"),
        check_vma=False,
    )
```

profile of v0, /device:TPU:6, one launch (start us, length us, event | category | flops | bytes accessed | tf_op | source)
XLA Modules:
  0.0 1217.8 jit_solution(11612759500869940358)
XLA Ops:
  9.2 1.3 rev.33
  10.6 1.9 collective-permute-start.6
  12.5 10.6 collective-permute-start.7
  23.2 3.4 collective-permute-start.2
  26.6 7.2 collective-permute-start.3
  33.8 1.9 collective-permute-start.5
  35.7 76.6 %all_gather.22 = f32[1,1,2,4096]{3,2,1,0:T(2,128)S(1)} all-gather(f32[1,1,2,128]{3,2,1,0:T(2,128)S(1)} %rev.35), channel_id=1, replica_groups=mesh['lon'=32,'lat'=16] {'lon'}, dimensions={3}, use_global_device_ids=true | all-gather | bytes 33792 | tf_op jit(solution)/shard_map/all_gather | solution.py:184
  112.3 2.8 rev.36
  116.5 1.9 collective-permute-start.4
  118.5 1.9 collective-permute-start
  121.4 7.8 collective-permute-start.1
  129.4 1.4 collective-permute-done.1
  133.5 1.8 fusion.50
  136.3 69.5 %all-gather.7.cloned.1.call-done = f32[4,40,2,4096]{3,2,1,0:T(2,128)} async-done(((f32[4,40,2,128]{3,2,1,0:T(2,128)}), f32[4,40,2,4096]{3,2,1,0:T(2,128)}) %all-gather.7.cloned.1.call-update) | async-done | bytes 5242896 | tf_op jit(solution)/shard_map/all_gather | solution.py:184
  207.5 39.1 %rev.34 = f32[4,40,2,4096]{3,2,1,0:T(2,128)} reverse(f32[4,40,2,4096]{3,2,1,0:T(2,128)} %all-gather.7.cloned.1.call-done), dimensions={3} | reverse | bytes 10485760 | tf_op jit(solution)/shard_map/rev | solution.py:186
  246.6 1.4 multiply_select_fusion.2
  250.5 1.5 fusion.43
  254.8 2.0 collective-permute-start.9
  256.8 7.8 collective-permute-start.8
  264.7 2.1 fusion.217
  269.9 1.9 collective-permute-start.11
  271.8 8.6 collective-permute-start.10
  281.6 103.7 %all-gather.9.cloned.1.call-done = f32[2,40,1,4096]{3,2,1,0:T(1,128)} async-done(((f32[2,40,1,128]{3,2,1,0:T(1,128)}), f32[2,40,1,4096]{3,2,1,0:T(1,128)}) %all-gather.9.cloned.1.call-update) | async-done | bytes 1310736 | tf_op jit(solution)/shard_map/all_gather | solution.py:184
  387.0 16.0 %rev.37 = f32[2,40,1,4096]{3,2,1,0:T(1,128)S(1)} reverse(f32[2,40,1,4096]{3,2,1,0:T(1,128)} %all-gather.9.cloned.1.call-done), dimensions={3} | reverse | bytes 2621440 | tf_op jit(solution)/shard_map/rev | solution.py:186
  407.8 1.4 constant_dynamic-update-slice_fusion.39
  410.5 1.3 rev.38
  412.4 5.7 collective-permute-start.13
  418.5 1.9 collective-permute-start.12
  420.4 1.9 collective-permute-start.15
  422.3 2.4 collective-permute-start.14
  425.1 3.6 collective-permute-done.12
  431.2 1.8 fusion.36
  433.1 165.9 %all-gather.11.cloned.1.call-done = f32[4,40,2,4096]{3,2,1,0:T(2,128)} async-done(((f32[4,40,2,128]{3,2,1,0:T(2,128)}), f32[4,40,2,4096]{3,2,1,0:T(2,128)}) %all-gather.11.cloned.1.call-update) | async-done | bytes 5242896 | tf_op jit(solution)/shard_map/all_gather | solution.py:184
  600.7 39.1 %rev.39 = f32[4,40,2,4096]{3,2,1,0:T(2,128)} reverse(f32[4,40,2,4096]{3,2,1,0:T(2,128)} %all-gather.11.cloned.1.call-done), dimensions={3} | reverse | bytes 10485760 | tf_op jit(solution)/shard_map/rev | solution.py:186
  639.8 1.4 multiply_select_fusion.1
  644.4 2.3 fusion.29
  648.3 2.1 collective-permute-start.19
  650.4 8.4 collective-permute-start.18
  659.0 6.0 collective-permute-start.17
  665.0 3.9 collective-permute-start.16
  670.1 7.0 collective-permute-done.17
  677.1 3.3 collective-permute-done.16
  681.6 102.5 %all-gather.13.cloned.1.call-done = f32[2,40,1,4096]{3,2,1,0:T(1,128)} async-done(((f32[2,40,1,128]{3,2,1,0:T(1,128)}), f32[2,40,1,4096]{3,2,1,0:T(1,128)}) %all-gather.13.cloned.1.call-update) | async-done | bytes 1310736 | tf_op jit(solution)/shard_map/all_gather | solution.py:184
  785.6 16.0 %rev.40 = f32[2,40,1,4096]{3,2,1,0:T(1,128)S(1)} reverse(f32[2,40,1,4096]{3,2,1,0:T(1,128)} %all-gather.13.cloned.1.call-done), dimensions={3} | reverse | bytes 2621440 | tf_op jit(solution)/shard_map/rev | solution.py:186
  806.4 1.4 constant_dynamic-update-slice_fusion.79
  811.1 5.1 collective-permute-start.21
  816.5 1.9 collective-permute-start.20
  818.4 1.9 collective-permute-start.23
  820.3 2.4 collective-permute-start.22
  823.1 3.5 collective-permute-done.20
  829.1 1.8 fusion.22
  831.0 169.2 %all-gather.15.cloned.1.call-done = f32[4,40,2,4096]{3,2,1,0:T(2,128)} async-done(((f32[4,40,2,128]{3,2,1,0:T(2,128)}), f32[4,40,2,4096]{3,2,1,0:T(2,128)}) %all-gather.15.cloned.1.call-update) | async-done | bytes 5242896 | tf_op jit(solution)/shard_map/all_gather | solution.py:184
  1001.9 39.1 %rev.42 = f32[4,40,2,4096]{3,2,1,0:T(2,128)} reverse(f32[4,40,2,4096]{3,2,1,0:T(2,128)} %all-gather.15.cloned.1.call-done), dimensions={3} | reverse | bytes 10485760 | tf_op jit(solution)/shard_map/rev | solution.py:186
  1041.0 1.4 multiply_select_fusion
  1045.6 2.3 fusion.15
  1049.5 2.1 collective-permute-start.27
  1051.6 8.4 collective-permute-start.26
  1060.2 1.9 collective-permute-start.25
  1062.1 8.1 collective-permute-start.24
  1070.7 8.2 collective-permute-done.25
  1078.9 2.4 collective-permute-done.24
  1082.4 103.7 %all-gather.17.cloned.1.call-done = f32[2,40,1,4096]{3,2,1,0:T(1,128)} async-done(((f32[2,40,1,128]{3,2,1,0:T(1,128)}), f32[2,40,1,4096]{3,2,1,0:T(1,128)}) %all-gather.17.cloned.1.call-update) | async-done | bytes 1310736 | tf_op jit(solution)/shard_map/all_gather | solution.py:184
  1187.1 16.0 %rev.43 = f32[2,40,1,4096]{3,2,1,0:T(1,128)S(1)} reverse(f32[2,40,1,4096]{3,2,1,0:T(1,128)} %all-gather.17.cloned.1.call-done), dimensions={3} | reverse | bytes 2621440 | tf_op jit(solution)/shard_map/rev | solution.py:186
  1207.6 1.4 constant_dynamic-update-slice_fusion.119
  (592 shorter events, 66.2 us)
Async XLA Ops:
  6.5 199.2 %all-gather.7.cloned.1.call-start = ((), (), s32[]{:S(2)}) async-start(), calls=%async_computation | async-start | bytes 5406720 | tf_op jit(solution)/shard_map/all_gather | solution.py:184
  10.5 374.9 %all-gather.9.cloned.1.call-start = ((), (), s32[]{:S(2)}) async-start(), calls=%async_computation.1 | async-start | bytes 1351680 | tf_op jit(solution)/shard_map/all_gather | solution.py:184
  10.6 118.7 %collective-permute-start.6 = (f32[1,1,2,128]{3,2,1,0:T(2,128)S(1)}, f32[1,1,2,128]{3,2,1,0:T(2,128)S(1)}, u32[]{:S(2)}, u32[]{:S(2)}) collective-permute-start(f32[1,1,2,128]{3,2,1,0:T(2,128)S(1)} %get-tuple-element.305), channel_id=1, source_target_pairs={{0,1},{1,2},{2,3},{3,4},{4,5},{5,6},{6,7},{7,8},{8,9},{9,10},{10,1... | collective-permute-start | bytes 3080 | tf_op jit(solution)/shard_map/ppermute | solution.py:29
  12.5 108.9 %collective-permute-start.7 = (f32[1,1,2,128]{3,2,1,0:T(2,128)S(1)}, f32[1,1,2,128]{3,2,1,0:T(2,128)S(1)}, u32[]{:S(2)}, u32[]{:S(2)}) collective-permute-start(f32[1,1,2,128]{3,2,1,0:T(2,128)S(1)} %get-tuple-element.306), channel_id=1, source_target_pairs={{1,0},{2,1},{3,2},{4,3},{5,4},{6,5},{7,6},{8,7},{9,8},{10,9},{11,1... | collective-permute-start | bytes 3080 | tf_op jit(solution)/shard_map/ppermute | solution.py:31
  23.2 93.3 %collective-permute-start.2 = (f32[1,1,8,2]{3,2,1,0:T(8,128)S(1)}, f32[1,1,8,2]{3,2,1,0:T(8,128)S(1)}, u32[]{:S(2)}, u32[]{:S(2)}) collective-permute-start(f32[1,1,8,2]{3,2,1,0:T(8,128)S(1)} %get-tuple-element.303), channel_id=1, source_target_pairs={{0,16},{16,32},{32,48},{48,64},{64,80},{80,96},{96,112},{112,128},... | collective-permute-start | bytes 200 | tf_op jit(solution)/shard_map/ppermute | solution.py:29
  26.6 91.9 %collective-permute-start.3 = (f32[1,1,8,2]{3,2,1,0:T(8,128)S(1)}, f32[1,1,8,2]{3,2,1,0:T(8,128)S(1)}, u32[]{:S(2)}, u32[]{:S(2)}) collective-permute-start(f32[1,1,8,2]{3,2,1,0:T(8,128)S(1)} %get-tuple-element.304), channel_id=1, source_target_pairs={{16,0},{32,16},{48,32},{64,48},{80,64},{96,80},{112,96},{128,112},... | collective-permute-start | bytes 200 | tf_op jit(solution)/shard_map/ppermute | solution.py:31
  33.8 212.9 %collective-permute-start.5 = (f32[4,40,2,128]{3,2,1,0:T(2,128)}, f32[4,40,2,128]{3,2,1,0:T(2,128)}, u32[]{:S(2)}, u32[]{:S(2)}) collective-permute-start(f32[4,40,2,128]{3,2,1,0:T(2,128)} %get-tuple-element.243), channel_id=1, source_target_pairs={{1,0},{2,1},{3,2},{4,3},{5,4},{6,5},{7,6},{8,7},{9,8},{10,9},{11,1... | collective-permute-start | bytes 491528 | tf_op jit(solution)/shard_map/ppermute | solution.py:31
  116.5 148.2 %copy-start.143 = (f32[8]{0:T(128)}, f32[8]{0:T(128)S(1)}, u32[]{:S(2)}) copy-start(f32[8]{0:T(128)S(1)} %sine_multiply_fusion) | copy-start | bytes 100
  116.5 131.5 %collective-permute-start.4 = (f32[4,40,2,128]{3,2,1,0:T(2,128)}, f32[4,40,2,128]{3,2,1,0:T(2,128)}, u32[]{:S(2)}, u32[]{:S(2)}) collective-permute-start(f32[4,40,2,128]{3,2,1,0:T(2,128)} %get-tuple-element.244), channel_id=1, source_target_pairs={{0,1},{1,2},{2,3},{3,4},{4,5},{5,6},{6,7},{7,8},{8,9},{9,10},{10,1... | collective-permute-start | bytes 491528 | tf_op jit(solution)/shard_map/ppermute | solution.py:29
  118.5 12.7 %collective-permute-start = (f32[4,40,8,2]{1,2,3,0:T(8,128)S(1)}, f32[4,40,8,2]{1,2,3,0:T(8,128)S(1)}, u32[]{:S(2)}, u32[]{:S(2)}) collective-permute-start(f32[4,40,8,2]{1,2,3,0:T(8,128)S(1)} %copy.11), channel_id=1, source_target_pairs={{0,16},{16,32},{32,48},{48,64},{64,80},{80,96},{96,112},{112,128},... | collective-permute-start | bytes 30728 | tf_op jit(solution)/shard_map/ppermute | solution.py:29
  121.4 9.4 collective-permute-start.1
  207.5 39.1 %copy-start.140 = (f32[4]{0:T(128)S(1)}, f32[4]{0:T(128)}, u32[]{:S(2)}) copy-start(f32[4]{0:T(128)} %constant.120.clone) | copy-start | bytes 52
  250.5 1.5 copy-start.15
  250.5 1.5 copy-start.16
  253.1 11.6 slice-start
  254.7 344.2 %all-gather.11.cloned.1.call-start = ((), (), s32[]{:S(2)}) async-start(), calls=%async_computation.2 | async-start | bytes 5406720 | tf_op jit(solution)/shard_map/all_gather | solution.py:184
  254.8 25.6 %collective-permute-start.9 = (f32[2,40,8,1]{3,2,1,0:T(8,128)}, f32[2,40,8,1]{3,2,1,0:T(8,128)S(1)}, u32[]{:S(2)}, u32[]{:S(2)}) collective-permute-start(f32[2,40,8,1]{3,2,1,0:T(8,128)} %get-tuple-element.255), channel_id=1, source_target_pairs={{0,16},{16,32},{32,48},{48,64},{64,80},{80,96},{96,112},{112,128},... | collective-permute-start | bytes 7688 | tf_op jit(solution)/shard_map/ppermute | solution.py:29
  256.8 23.7 %collective-permute-start.8 = (f32[2,40,8,1]{3,2,1,0:T(8,128)}, f32[2,40,8,1]{3,2,1,0:T(8,128)S(1)}, u32[]{:S(2)}, u32[]{:S(2)}) collective-permute-start(f32[2,40,8,1]{3,2,1,0:T(8,128)} %get-tuple-element.256), channel_id=1, source_target_pairs={{16,0},{32,16},{48,32},{64,48},{80,64},{96,80},{112,96},{128,112},... | collective-permute-start | bytes 7688 | tf_op jit(solution)/shard_map/ppermute | solution.py:31
  269.9 134.2 %collective-permute-start.11 = (f32[2,40,1,128]{3,2,1,0:T(1,128)}, f32[2,40,1,128]{3,2,1,0:T(1,128)}, u32[]{:S(2)}, u32[]{:S(2)}) collective-permute-start(f32[2,40,1,128]{3,2,1,0:T(1,128)} %get-tuple-element.257), channel_id=1, source_target_pairs={{0,1},{1,2},{2,3},{3,4},{4,5},{5,6},{6,7},{7,8},{8,9},{9,10},{10,1... | collective-permute-start | bytes 122888 | tf_op jit(solution)/shard_map/ppermute | solution.py:29
  271.8 131.2 %collective-permute-start.10 = (f32[2,40,1,128]{3,2,1,0:T(1,128)}, f32[2,40,1,128]{3,2,1,0:T(1,128)}, u32[]{:S(2)}, u32[]{:S(2)}) collective-permute-start(f32[2,40,1,128]{3,2,1,0:T(1,128)} %get-tuple-element.258), channel_id=1, source_target_pairs={{1,0},{2,1},{3,2},{4,3},{5,4},{6,5},{7,6},{8,7},{9,8},{10,9},{11,1... | collective-permute-start | bytes 122888 | tf_op jit(solution)/shard_map/ppermute | solution.py:31
  406.4 1.0 copy-start.24
  406.4 1.0 copy-start.27
  406.4 1.0 copy-start.30
  406.4 1.0 copy-start.33
  406.4 1.0 copy-start.36
  411.8 372.2 %all-gather.13.cloned.1.call-start = ((), (), s32[]{:S(2)}) async-start(), calls=%async_computation.3 | async-start | bytes 1351680 | tf_op jit(solution)/shard_map/all_gather | solution.py:184
  412.4 12.3 %collective-permute-start.13 = (f32[4,40,8,2]{1,2,3,0:T(8,128)S(1)}, f32[4,40,8,2]{1,2,3,0:T(8,128)S(1)}, u32[]{:S(2)}, u32[]{:S(2)}) collective-permute-start(f32[4,40,8,2]{1,2,3,0:T(8,128)S(1)} %copy.19), channel_id=1, source_target_pairs={{16,0},{32,16},{48,32},{64,48},{80,64},{96,80},{112,96},{128,112},... | collective-permute-start | bytes 30728 | tf_op jit(solution)/shard_map/ppermute | solution.py:31
  418.5 10.2 collective-permute-start.12
  420.4 219.4 %collective-permute-start.15 = (f32[4,40,2,128]{3,2,1,0:T(2,128)}, f32[4,40,2,128]{3,2,1,0:T(2,128)}, u32[]{:S(2)}, u32[]{:S(2)}) collective-permute-start(f32[4,40,2,128]{3,2,1,0:T(2,128)} %get-tuple-element.238), channel_id=1, source_target_pairs={{1,0},{2,1},{3,2},{4,3},{5,4},{6,5},{7,6},{8,7},{9,8},{10,9},{11,1... | collective-permute-start | bytes 491528 | tf_op jit(solution)/shard_map/ppermute | solution.py:31
  422.3 218.9 %collective-permute-start.14 = (f32[4,40,2,128]{3,2,1,0:T(2,128)}, f32[4,40,2,128]{3,2,1,0:T(2,128)}, u32[]{:S(2)}, u32[]{:S(2)}) collective-permute-start(f32[4,40,2,128]{3,2,1,0:T(2,128)} %get-tuple-element.239), channel_id=1, source_target_pairs={{0,1},{1,2},{2,3},{3,4},{4,5},{5,6},{6,7},{7,8},{8,9},{9,10},{10,1... | collective-permute-start | bytes 491528 | tf_op jit(solution)/shard_map/ppermute | solution.py:29
  429.5 1.1 copy-start.2
  429.5 1.2 copy-start.9
  600.7 39.1 %copy-start.141 = (f32[4]{0:T(128)S(1)}, f32[4]{0:T(128)}, u32[]{:S(2)}) copy-start(f32[4]{0:T(128)} %constant.120.clone) | copy-start | bytes 52
  643.3 1.1 copy-start.4
  644.4 2.3 copy-start.18
  646.7 1.4 copy-start.3
  647.6 352.6 %all-gather.15.cloned.1.call-start = ((), (), s32[]{:S(2)}) async-start(), calls=%async_computation.4 | async-start | bytes 5406720 | tf_op jit(solution)/shard_map/all_gather | solution.py:184
  648.0 20.9 %copy-start.5 = (f32[4,40,12,128]{3,2,1,0:T(8,128)S(1)}, f32[4,40,12,128]{3,2,1,0:T(8,128)}, u32[]{:S(2)}) copy-start(f32[4,40,12,128]{3,2,1,0:T(8,128)} %copy-done.4) | copy-start | bytes 2949124
  648.3 20.8 %copy-start.11 = (f32[2,40,9,128]{3,2,1,0:T(8,128)S(1)}, f32[2,40,9,128]{3,2,1,0:T(8,128)}, u32[]{:S(2)}) copy-start(f32[2,40,9,128]{3,2,1,0:T(8,128)} %get-tuple-element.227) | copy-start | bytes 1105924
  648.3 20.8 %copy-start.13 = (f32[2,40,8,129]{3,2,1,0:T(8,128)S(1)}, f32[2,40,8,129]{3,2,1,0:T(8,128)}, u32[]{:S(2)}) copy-start(f32[2,40,8,129]{3,2,1,0:T(8,128)} %get-tuple-element.215) | copy-start | bytes 990724
  648.3 154.4 %collective-permute-start.19 = (f32[2,40,1,128]{3,2,1,0:T(1,128)}, f32[2,40,1,128]{3,2,1,0:T(1,128)}, u32[]{:S(2)}, u32[]{:S(2)}) collective-permute-start(f32[2,40,1,128]{3,2,1,0:T(1,128)} %get-tuple-element.252), channel_id=1, source_target_pairs={{0,1},{1,2},{2,3},{3,4},{4,5},{5,6},{6,7},{7,8},{8,9},{9,10},{10,1... | collective-permute-start | bytes 122888 | tf_op jit(solution)/shard_map/ppermute | solution.py:29
  650.4 151.3 %collective-permute-start.18 = (f32[2,40,1,128]{3,2,1,0:T(1,128)}, f32[2,40,1,128]{3,2,1,0:T(1,128)}, u32[]{:S(2)}, u32[]{:S(2)}) collective-permute-start(f32[2,40,1,128]{3,2,1,0:T(1,128)} %get-tuple-element.253), channel_id=1, source_target_pairs={{1,0},{2,1},{3,2},{4,3},{5,4},{6,5},{7,6},{8,7},{9,8},{10,9},{11,1... | collective-permute-start | bytes 122888 | tf_op jit(solution)/shard_map/ppermute | solution.py:31
  659.0 18.1 %collective-permute-start.17 = (f32[2,40,8,1]{3,2,1,0:T(8,128)S(1)}, f32[2,40,8,1]{3,2,1,0:T(8,128)S(1)}, u32[]{:S(2)}, u32[]{:S(2)}) collective-permute-start(f32[2,40,8,1]{3,2,1,0:T(8,128)S(1)} %get-tuple-element.250), channel_id=1, source_target_pairs={{0,16},{16,32},{32,48},{48,64},{64,80},{80,96},{96,112},{112,128},... | collective-permute-start | bytes 7688 | tf_op jit(solution)/shard_map/ppermute | solution.py:29
  665.0 4.3 copy-start.144
  665.0 15.4 %collective-permute-start.16 = (f32[2,40,8,1]{3,2,1,0:T(8,128)S(1)}, f32[2,40,8,1]{3,2,1,0:T(8,128)S(1)}, u32[]{:S(2)}, u32[]{:S(2)}) collective-permute-start(f32[2,40,8,1]{3,2,1,0:T(8,128)S(1)} %get-tuple-element.251), channel_id=1, source_target_pairs={{16,0},{32,16},{48,32},{64,48},{80,64},{96,80},{112,96},{128,112},... | collective-permute-start | bytes 7688 | tf_op jit(solution)/shard_map/ppermute | solution.py:31
  810.5 375.7 %all-gather.17.cloned.1.call-start = ((), (), s32[]{:S(2)}) async-start(), calls=%async_computation.5 | async-start | bytes 1351680 | tf_op jit(solution)/shard_map/all_gather | solution.py:184
  811.1 11.7 collective-permute-start.21
  816.5 10.1 collective-permute-start.20
  818.4 222.6 %collective-permute-start.23 = (f32[4,40,2,128]{3,2,1,0:T(2,128)}, f32[4,40,2,128]{3,2,1,0:T(2,128)}, u32[]{:S(2)}, u32[]{:S(2)}) collective-permute-start(f32[4,40,2,128]{3,2,1,0:T(2,128)} %get-tuple-element.233), channel_id=1, source_target_pairs={{1,0},{2,1},{3,2},{4,3},{5,4},{6,5},{7,6},{8,7},{9,8},{10,9},{11,1... | collective-permute-start | bytes 491528 | tf_op jit(solution)/shard_map/ppermute | solution.py:31
  820.3 222.1 %collective-permute-start.22 = (f32[4,40,2,128]{3,2,1,0:T(2,128)}, f32[4,40,2,128]{3,2,1,0:T(2,128)}, u32[]{:S(2)}, u32[]{:S(2)}) collective-permute-start(f32[4,40,2,128]{3,2,1,0:T(2,128)} %get-tuple-element.234), channel_id=1, source_target_pairs={{0,1},{1,2},{2,3},{3,4},{4,5},{5,6},{6,7},{7,8},{8,9},{9,10},{10,1... | collective-permute-start | bytes 491528 | tf_op jit(solution)/shard_map/ppermute | solution.py:29
  827.4 1.1 copy-start
  827.4 1.2 copy-start.10
  1001.9 39.1 %copy-start.142 = (f32[4]{0:T(128)S(1)}, f32[4]{0:T(128)}, u32[]{:S(2)}) copy-start(f32[4]{0:T(128)} %constant.120.clone) | copy-start | bytes 52
  1044.5 1.1 copy-start.6
  1045.6 2.3 copy-start.17
  1047.9 1.4 copy-start.1
  1049.2 21.0 %copy-start.7 = (f32[4,40,12,128]{3,2,1,0:T(8,128)S(1)}, f32[4,40,12,128]{3,2,1,0:T(8,128)}, u32[]{:S(2)}) copy-start(f32[4,40,12,128]{3,2,1,0:T(8,128)} %copy-done.6) | copy-start | bytes 2949124
  1049.5 20.9 %copy-start.12 = (f32[2,40,9,128]{3,2,1,0:T(8,128)S(1)}, f32[2,40,9,128]{3,2,1,0:T(8,128)}, u32[]{:S(2)}) copy-start(f32[2,40,9,128]{3,2,1,0:T(8,128)} %get-tuple-element.225) | copy-start | bytes 1105924
  1049.5 20.9 %copy-start.14 = (f32[2,40,8,129]{3,2,1,0:T(8,128)S(1)}, f32[2,40,8,129]{3,2,1,0:T(8,128)}, u32[]{:S(2)}) copy-start(f32[2,40,8,129]{3,2,1,0:T(8,128)} %get-tuple-element.213) | copy-start | bytes 990724
  1049.5 154.7 %collective-permute-start.27 = (f32[2,40,1,128]{3,2,1,0:T(1,128)}, f32[2,40,1,128]{3,2,1,0:T(1,128)}, u32[]{:S(2)}, u32[]{:S(2)}) collective-permute-start(f32[2,40,1,128]{3,2,1,0:T(1,128)} %get-tuple-element.247), channel_id=1, source_target_pairs={{0,1},{1,2},{2,3},{3,4},{4,5},{5,6},{6,7},{7,8},{8,9},{9,10},{10,1... | collective-permute-start | bytes 122888 | tf_op jit(solution)/shard_map/ppermute | solution.py:29
  1051.6 151.6 %collective-permute-start.26 = (f32[2,40,1,128]{3,2,1,0:T(1,128)}, f32[2,40,1,128]{3,2,1,0:T(1,128)}, u32[]{:S(2)}, u32[]{:S(2)}) collective-permute-start(f32[2,40,1,128]{3,2,1,0:T(1,128)} %get-tuple-element.248), channel_id=1, source_target_pairs={{1,0},{2,1},{3,2},{4,3},{5,4},{6,5},{7,6},{8,7},{9,8},{10,9},{11,1... | collective-permute-start | bytes 122888 | tf_op jit(solution)/shard_map/ppermute | solution.py:31
  1060.2 18.7 %collective-permute-start.25 = (f32[2,40,8,1]{3,2,1,0:T(8,128)S(1)}, f32[2,40,8,1]{3,2,1,0:T(8,128)S(1)}, u32[]{:S(2)}, u32[]{:S(2)}) collective-permute-start(f32[2,40,8,1]{3,2,1,0:T(8,128)S(1)} %get-tuple-element.245), channel_id=1, source_target_pairs={{0,16},{16,32},{32,48},{48,64},{64,80},{80,96},{96,112},{112,128},... | collective-permute-start | bytes 7688 | tf_op jit(solution)/shard_map/ppermute | solution.py:29
  1062.1 8.4 copy-start.145
  1062.1 19.1 %collective-permute-start.24 = (f32[2,40,8,1]{3,2,1,0:T(8,128)S(1)}, f32[2,40,8,1]{3,2,1,0:T(8,128)S(1)}, u32[]{:S(2)}, u32[]{:S(2)}) collective-permute-start(f32[2,40,8,1]{3,2,1,0:T(8,128)S(1)} %get-tuple-element.246), channel_id=1, source_target_pairs={{16,0},{32,16},{48,32},{64,48},{80,64},{96,80},{112,96},{128,112},... | collective-permute-start | bytes 7688 | tf_op jit(solution)/shard_map/ppermute | solution.py:31
  (118 other events, 106.6 us)
Sparse Core Ops, SparseCore 0:
  10.7 195.0 all-gather.6
  254.9 130.4 all-gather.8
  412.0 186.9 all-gather.10
  647.7 136.2 all-gather.12
  810.6 189.5 all-gather.14
  1048.9 137.1 all-gather.16
where the time goes:
time: 1230 us; the launch traced here: 1220 us
  waiting for transfers between devices  744 us (60%)
  local copies, waits for them, and re-layouts  200 us (16%)
  starting transfers between devices  121 us (10%)
  blocking collectives  76.6 us (6%)
  other arithmetic  58.8 us (5%)
  between operations  17.3 us (1%)
    all_gather x6, waiting for transfers between devices, pad_tile(): gathered = lax.all_gather(outgoing, 'lon', axis=3, tiled=True)  714 us
    rev x7, local copies, waits for them, and re-layouts, pad_tile(): reversed_rows = gathered[..., ::-1]  168 us
    ppermute x14, starting transfers between devices, with_halo(): lax.ppermute(head, axis, [((i + 1) % count, i) for i in range(ends)])  87.5 us
    all_gather x1, blocking collectives, pad_tile(): gathered = lax.all_gather(outgoing, 'lon', axis=3, tiled=True)  76.6 us
    ppermute x14, starting transfers between devices, with_halo(): lax.ppermute(tail, axis, [(i, (i + 1) % count) for i in range(ends)])  33.7 us
  transfers between devices with their start and end apart: 34, of which 13 were waited for; matrix products, arithmetic and copies ran while one was open for 17% of the time, Pallas kernels for 0%

commit v1 on v0

v1 whole, which is shorter than its diff:
```python
import functools
import math

import jax
import jax.numpy as jnp
from jax import lax
from jax.experimental import pallas as pl
from jax.experimental.pallas import tpu as pltpu
from jax.sharding import PartitionSpec as P

STEPS = 3
LEV = 40
ADVECT = 0.15
DIFFUSE = 0.12
VISCOSITY = 0.1
PRESSURE = 0.03
CORIOLIS = 0.3
EXPAND_HEAT = 0.6
EXPAND_SALT = 0.8

ITEMS = 5 * LEV + 1
TEMP, SALT, EAST, NORTH, COUP, WET = 0, LEV, 2 * LEV, 3 * LEV, 4 * LEV, 5 * LEV
HALF = (ITEMS + 1) // 2
MORE = 13
FAR = 88
STRIP = 9
PACKS = LEV // 2

FRAME_ROWS = list(range(-8, 8)) + [8, 9, 5, 6] + list(range(7, 17)) + [0, -9]

VM = pl.BlockSpec(memory_space=pltpu.VMEM)
SM = pl.BlockSpec(memory_space=pltpu.SMEM)


def call(body, outs, ins, flops, scratch=()):
    return pl.pallas_call(
        body,
        out_shape=tuple(jax.ShapeDtypeStruct(s, jnp.float32) for s in outs),
        in_specs=ins,
        out_specs=tuple(VM for _ in outs),
        scratch_shapes=list(scratch),
        compiler_params=pltpu.CompilerParams(vmem_limit_bytes=48 * 1024 * 1024),
        cost_estimate=pl.CostEstimate(flops=flops, bytes_accessed=4 * 1024 * 1024, transcendentals=0),
    )


def rows_of(shape=(8, 128)):
    return lax.broadcasted_iota(jnp.int32, shape, 0)


def lanes_of(shape=(8, 128)):
    return lax.broadcasted_iota(jnp.int32, shape, 1)


def loop(count, body, init=None, unroll=1):
    if init is None:
        lax.fori_loop(0, count, lambda i, c: (body(i), c)[1], 0, unroll=unroll)
        return None
    return lax.fori_loop(0, count, body, init, unroll=unroll)


def row_at(ref, tile, row):
    return jnp.broadcast_to(ref[tile, row : row + 1, :], (8, 128))


def turn(tile):
    turned = jnp.take_along_axis(tile, 127 - lanes_of(), axis=1)
    return jnp.take_along_axis(turned, 7 - rows_of(), axis=0)


def split_halves(full_ref, a_ref, b_ref, count):
    lanes = lanes_of()

    def one(k):
        near = pltpu.roll(full_ref[k], 64, axis=1)
        far = full_ref[k + count]
        a_ref[k] = jnp.where(lanes < 64, near, far)
        b_ref[k] = jnp.where(lanes < 64, far, near)

    loop(count, one, unroll=8)


def join_halves(full_ref, a_ref, b_ref, count):
    lanes = lanes_of()

    def one(k):
        a, b = a_ref[k], b_ref[k]
        full_ref[k] = jnp.where(lanes < 64, a, b)
        full_ref[k + count] = pltpu.roll(jnp.where(lanes < 64, b, a), 64, axis=1)

    loop(count, one, unroll=8)


def gather_body(flag_ref, state_ref, mixing_ref, wet_ref, x_ref, a_ref, b_ref, full_ref):
    wet = wet_ref[...].astype(jnp.float32)
    x_ref[WET] = wet

    def level(l):
        deep = wet > l.astype(jnp.float32)
        for k in range(4):
            x_ref[k * LEV + l] = jnp.where(deep, state_ref[k, l], 0.0)
        x_ref[COUP + l] = jnp.where(wet > (l + 1).astype(jnp.float32), mixing_ref[l], 0.0)

    loop(LEV, level, unroll=4)

    @pl.when(flag_ref[1] == 0)
    def _():
        def move(i):
            a_ref[i] = x_ref[i]

        def move_rest(i):
            b_ref[i] = x_ref[HALF + i]

        loop(HALF, move, unroll=8)
        loop(ITEMS - HALF, move_rest, unroll=8)
        b_ref[HALF - 1] = jnp.zeros((8, 128), jnp.float32)

    @pl.when(flag_ref[1] == 1)
    def _():
        def tracer(i):
            full_ref[i] = turn(x_ref[i])

        def current(i):
            full_ref[EAST + i] = -turn(x_ref[EAST + i])

        def couple(i):
            full_ref[COUP + i] = turn(x_ref[COUP + i])

        loop(2 * LEV, tracer, unroll=8)
        loop(2 * LEV, current, unroll=8)
        loop(LEV, couple, unroll=8)
        full_ref[WET] = turn(x_ref[WET])
        full_ref[2 * HALF - 1] = jnp.zeros((8, 128), jnp.float32)
        split_halves(full_ref, a_ref, b_ref, HALF)


def take_rows(ref, base, row):
    rows = rows_of()
    out = row_at(ref, base, row)
    for r in range(1, 8):
        out = jnp.where(rows == r, row_at(ref, base + r, row), out)
    return out


def outgoing_body(flag_ref, y_ref, c_ref, d_ref, full_ref):
    parity = flag_ref[0]
    fold = flag_ref[1]
    rows = rows_of()
    zero = jnp.zeros((8, 128), jnp.float32)

    def same(t):
        return t

    def mirror(t):
        return jnp.take_along_axis(t, 127 - lanes_of(), axis=1)

    def extra(out_ref, base, item, tiles, row, change):
        def eight(t):
            out_ref[base + t] = change(take_rows(y_ref, item + t * 8, row))

        loop(tiles, eight, unroll=5)

    def plain(row):
        extra(c_ref, 0, TEMP, 10, row, same)
        c_ref[10] = row_at(y_ref, WET, row)
        c_ref[11] = zero
        c_ref[12] = zero
        loop(MORE, lambda t: d_ref.__setitem__(t, zero))

    @pl.when((fold == 0) & (parity == 0))
    def _():
        plain(0)

    @pl.when((fold == 0) & (parity == 1))
    def _():
        plain(7)

    @pl.when(fold == 1)
    def _():
        extra(full_ref, 0, TEMP, 10, 6, mirror)
        extra(full_ref, 10, TEMP, 10, 7, mirror)
        extra(full_ref, 20, NORTH, 5, 7, lambda t: -mirror(t))
        wet = jnp.where(rows == 0, row_at(y_ref, WET, 6), row_at(y_ref, WET, 7))
        full_ref[25] = mirror(wet)
        split_halves(full_ref, c_ref, d_ref, MORE)


def frame_body(
    flag_ref, x_ref, y_ref, a_ref, b_ref, c_ref, d_ref, frame_ref, far_ref, east_ref, west_ref, full_ref, more_ref
):
    parity = flag_ref[0]
    fold = flag_ref[1]
    rows = rows_of()
    lanes = lanes_of()

    @pl.when(fold == 0)
    def _():
        def move(k):
            full_ref[k] = a_ref[k]
            full_ref[k + HALF] = b_ref[k]

        def move_more(k):
            more_ref[k] = c_ref[k]

        loop(HALF, move, unroll=8)
        loop(11, move_more, unroll=11)

    @pl.when(fold == 1)
    def _():
        join_halves(full_ref, a_ref, b_ref, HALF)
        join_halves(more_ref, c_ref, d_ref, MORE)

    def send_far(row):
        def eight(t):
            far_ref[pl.ds(pl.multiple_of(t * 8, 8), 8), :] = take_rows(full_ref, t * 8, row)

        loop(2 * LEV // 8, eight, unroll=5)
        far_ref[pl.ds(80, 8), :] = row_at(full_ref, WET, row)

    @pl.when(parity == 0)
    def _():
        send_far(7)

    @pl.when((parity == 1) & (fold == 0))
    def _():
        send_far(0)

    @pl.when(fold == 1)
    def _():
        send_far(1)

    def put(i, south, own, north):
        shifted = pltpu.roll(north, 5, axis=0)
        middle = jnp.where(rows < 2, north, jnp.where(rows < 5, pltpu.roll(own, 5, axis=0), shifted))
        frame_ref[i, 0:8] = south
        frame_ref[i, 8:16] = own
        frame_ref[i, 16:24] = middle
        frame_ref[i, 24:32] = jnp.where(rows < 5, shifted, 0.0)

    @pl.when(parity == 0)
    def _():
        def one(i):
            put(i, full_ref[i], x_ref[i], y_ref[i])

        loop(ITEMS, one, unroll=8)

    @pl.when((parity == 1) & (fold == 0))
    def _():
        def one(i):
            put(i, y_ref[i], x_ref[i], full_ref[i])

        loop(ITEMS, one, unroll=8)

    @pl.when(fold == 1)
    def _():
        def base(i):
            beyond = full_ref[i]
            own = x_ref[i]
            shifted = pltpu.roll(beyond, 4, axis=0)
            middle = jnp.where(
                rows < 2, pltpu.roll(beyond, 7, axis=0), jnp.where(rows < 4, pltpu.roll(own, 5, axis=0), shifted)
            )
            frame_ref[i, 0:8] = y_ref[i]
            frame_ref[i, 8:16] = own
            frame_ref[i, 16:24] = middle
            return jnp.where(rows < 4, shifted, 0.0)

        def with_near(first, tiles, more):
            def eight(t):
                for r in range(8):
                    i = first + t * 8 + r
                    frame_ref[i, 24:32] = jnp.where(rows == 4, row_at(more_ref, more + t, r), base(i))

            loop(tiles, eight)

        def eastward(i):
            frame_ref[EAST + i, 24:32] = base(EAST + i)

        def couple(i):
            frame_ref[COUP + i, 24:32] = jnp.where(rows < 3, base(COUP + i), 0.0)

        with_near(TEMP, 10, 10)
        loop(LEV, eastward, unroll=8)
        with_near(NORTH, 5, 20)
        loop(LEV, couple, unroll=8)
        frame_ref[WET, 24:32] = jnp.where(rows == 4, row_at(more_ref, 25, 1), base(WET))

    place = jnp.where(parity == 0, 7, 5)

    def far_rows(t):
        for r in range(8):
            i = t * 8 + r
            frame_ref[i, 24:32] = jnp.where(rows == place, row_at(more_ref, t, r), frame_ref[i, 24:32])

    loop(2 * LEV // 8, far_rows)
    wet_row = jnp.where(fold == 1, row_at(more_ref, 25, 0), row_at(more_ref, 10, 0))
    frame_ref[WET, 24:32] = jnp.where(rows == place, wet_row, frame_ref[WET, 24:32])

    wide = lanes_of((32, 128))

    def add_strip(out, tile, g, shift):
        here = (wide >= STRIP * g) & (wide < STRIP * (g + 1))
        return jnp.where(here, pltpu.roll(tile, (STRIP * g + shift) % 128, axis=1), out)

    def pack(k):
        to_east = to_west = jnp.zeros((32, 128), jnp.float32)
        for g in range(10):
            tile = frame_ref[(g % 5) * LEV + 2 * k + g // 5]
            to_east = add_strip(to_east, tile, g, STRIP)
            to_west = add_strip(to_west, tile, g, 0)
        east_ref[k] = to_east
        west_ref[k] = to_west

    loop(PACKS, pack)
    east_ref[0] = add_strip(east_ref[0], frame_ref[WET], 10, STRIP)
    west_ref[0] = add_strip(west_ref[0], frame_ref[WET], 10, 0)


def east_of(a):
    return pltpu.roll(a, 127, axis=1)


def west_of(a):
    return pltpu.roll(a, 1, axis=1)


def north_of(a):
    return pltpu.roll(a, a.shape[0] - 1, axis=0)


def south_of(a):
    return pltpu.roll(a, 1, axis=0)


def minmod(a, b):
    return jnp.maximum(jnp.minimum(a, b), 0.0) + jnp.minimum(jnp.maximum(a, b), 0.0)


def join_tracer(a):
    rows = rows_of()
    middle = a[16:24]
    middle = jnp.where(rows == 0, pltpu.roll(middle, 3, axis=0), middle)
    middle = jnp.where(rows == 3, pltpu.roll(a[8:16], 5, axis=0), middle)
    return jnp.concatenate([a[0:16], middle, a[24:32]], axis=0)


def join_field(a):
    rows = rows_of()
    middle = a[16:24]
    middle = jnp.where(rows < 2, pltpu.roll(middle, 3, axis=0), middle)
    middle = jnp.where((rows == 2) | (rows == 3), pltpu.roll(a[8:16], 5, axis=0), middle)
    return jnp.concatenate([a[0:16], middle, a[24:32]], axis=0)


def march(wet, turn_rate, f_ref, coup_ref, inv_ref, up_ref, adv_ref, sum_ref, dif_ref):
    wet_e = jnp.minimum(wet, east_of(wet))
    wet_n = jnp.minimum(wet, north_of(wet))
    zero = jnp.zeros((32, 128), jnp.float32)
    for k in range(4):
        sum_ref[k, 0] = zero
        sum_ref[k, LEV + 1] = zero

    def pivots(l, carry):
        above, inv_above = carry
        c = coup_ref[l]
        pivot = 1.0 + c + above * (1.0 - above * inv_above)
        inv = 1.0 / pivot
        inv_ref[l] = inv
        up_ref[l] = c * inv
        return c, inv

    loop(LEV, pivots, (zero, zero), unroll=4)

    def advect(q, face_e, face_n, speed_e, speed_n, from_w, from_s):
        de = jnp.where(face_e, east_of(q) - q, 0.0)
        dn = jnp.where(face_n, north_of(q) - q, 0.0)
        he = 0.5 * minmod(de, west_of(de))
        hn = 0.5 * minmod(dn, south_of(dn))
        fe = speed_e * jnp.where(from_w, q + he, east_of(q - he))
        fn = speed_n * jnp.where(from_s, q + hn, north_of(q - hn))
        return (fe - west_of(fe)) + (fn - south_of(fn))

    def friction(q, q_e, q_n, face_e, face_n):
        de = jnp.where(face_e, q_e - q, 0.0)
        dn = jnp.where(face_n, q_n - q, 0.0)
        return (de - west_of(de)) + (dn - south_of(dn))

    def explicit(l, pressure):
        lf = l.astype(jnp.float32)
        deep = wet > lf
        face_e = wet_e > lf
        face_n = wet_n > lf
        t, s, u, v = (f_ref[k, l] for k in range(4))
        u_e, v_n = east_of(u), north_of(v)
        speed_e = jnp.where(face_e, u + u_e, 0.0)
        speed_n = jnp.where(face_n, v + v_n, 0.0)
        from_w = speed_e > 0.0
        from_s = speed_n > 0.0
        for k, q in enumerate((t, s)):
            div = advect(q, face_e, face_n, speed_e, speed_n, from_w, from_s)
            a = join_tracer(jnp.where(deep, q - (0.5 * ADVECT) * div, 0.0))
            adv_ref[k, l] = a
            a_e, a_n = east_of(a), north_of(a)
            sum_ref[k, l + 1] = a + a_e
            dif_ref[k, l] = a_e - a
            sum_ref[2 + k, l + 1] = a + a_n
            dif_ref[2 + k, l] = a_n - a
        pressure = pressure + (EXPAND_SALT * s - EXPAND_HEAT * t)
        push_e = east_of(pressure) - west_of(pressure)
        push_n = north_of(pressure) - south_of(pressure)
        u1 = u + turn_rate * v - (0.5 * PRESSURE) * push_e + VISCOSITY * friction(u, u_e, north_of(u), face_e, face_n)
        v1 = v - turn_rate * u - (0.5 * PRESSURE) * push_n + VISCOSITY * friction(v, east_of(v), v_n, face_e, face_n)
        f_ref[2, l] = jnp.where(deep, u1, 0.0)
        f_ref[3, l] = jnp.where(deep, v1, 0.0)
        return pressure

    def lateral(l, carry):
        above, solved = carry
        lf = l.astype(jnp.float32)
        deep = wet > lf
        div = [None, None]
        for way, face, back in ((0, wet_e > lf, west_of), (2, wet_n > lf, south_of)):
            dt, ds = dif_ref[way, l], dif_ref[way + 1, l]
            gt = sum_ref[way, l + 2] - sum_ref[way, l]
            gs = sum_ref[way + 1, l + 2] - sum_ref[way + 1, l]
            gr = EXPAND_SALT * gs - EXPAND_HEAT * gt
            dr = EXPAND_SALT * ds - EXPAND_HEAT * dt
            slope = dr * gr / (gr * gr + 16.0)
            for k, (d, g) in enumerate(((dt, gt), (ds, gs))):
                flux = jnp.where(face, d - slope * g, 0.0)
                part = flux - back(flux)
                div[k] = part if div[k] is None else div[k] + part
        inv = inv_ref[l]
        done = []
        for k in range(4):
            rhs = jnp.where(deep, adv_ref[k, l] + DIFFUSE * div[k], 0.0) if k < 2 else f_ref[k, l]
            x = (rhs + above * solved[k]) * inv
            f_ref[k, l] = x
            done.append(x)
        return coup_ref[l], tuple(done)

    def back(i, solved):
        l = LEV - 1 - i
        up = up_ref[l]
        done = []
        for k in range(4):
            x = f_ref[k, l] + up * solved[k]
            f_ref[k, l] = join_field(x)
            done.append(x)
        return tuple(done)

    def step(_, carry):
        loop(LEV, explicit, zero, unroll=4)
        loop(LEV, lateral, (zero, (zero,) * 4), unroll=4)
        loop(LEV, back, (zero,) * 4, unroll=4)
        return carry

    lax.fori_loop(0, STEPS, step, 0)


WORK = [
    pltpu.VMEM((4, LEV, 32, 128), jnp.float32),
    pltpu.VMEM((LEV, 32, 128), jnp.float32),
    pltpu.VMEM((LEV, 32, 128), jnp.float32),
    pltpu.VMEM((LEV, 32, 128), jnp.float32),
    pltpu.VMEM((2, LEV, 32, 128), jnp.float32),
    pltpu.VMEM((4, LEV + 2, 32, 128), jnp.float32),
    pltpu.VMEM((4, LEV, 32, 128), jnp.float32),
]


def with_far(tile, i, far_ref, place):
    row = jnp.broadcast_to(far_ref[pl.ds(i, 1), :], (8, 128))
    return jnp.concatenate([tile[0:24], jnp.where(rows_of() == place, row, tile[24:32])], axis=0)


def main_body(flag_ref, frame_ref, far_ref, turn_ref, out_ref, f_ref, coup_ref, *work):
    place = jnp.where(flag_ref[0] == 0, 5, 7)

    def level(l):
        for k in range(2):
            f_ref[k, l] = with_far(frame_ref[k * LEV + l], k * LEV + l, far_ref, place)
        for k in range(2, 4):
            f_ref[k, l] = frame_ref[k * LEV + l]
        coup_ref[l] = frame_ref[COUP + l]

    loop(LEV, level, unroll=4)
    wet = with_far(frame_ref[WET], 80, far_ref, place)
    march(wet, turn_ref[...], f_ref, coup_ref, *work)

    def give(l):
        for k in range(4):
            out_ref[k, l] = f_ref[k, l, 8:16]

    loop(LEV, give, unroll=4)


def side_body(flag_ref, frame_ref, far_ref, turn_ref, east_ref, west_ref, main_ref, out_ref, f_ref, coup_ref, *work):
    place = jnp.where(flag_ref[0] == 0, 5, 7)
    wide = lanes_of((32, 128))

    def sides(tile, k, g):
        west = pltpu.roll(east_ref[k], (32 - STRIP - STRIP * g) % 128, axis=1)
        east = pltpu.roll(west_ref[k], (96 - STRIP * g) % 128, axis=1)
        out = jnp.where(wide < 64, pltpu.roll(tile, 32, axis=1), pltpu.roll(tile, 96, axis=1))
        out = jnp.where((wide >= 32 - STRIP) & (wide < 32), west, out)
        return jnp.where((wide >= 96) & (wide < 96 + STRIP), east, out)

    def unpack(k):
        for g in range(10):
            item, l = g % 5, 2 * k + g // 5
            tile = frame_ref[item * LEV + l]
            if item < 2:
                tile = with_far(tile, item * LEV + l, far_ref, place)
            tile = sides(tile, k, g)
            if item < 4:
                f_ref[item, l] = tile
            else:
                coup_ref[l] = tile

    loop(PACKS, unpack)
    wet = sides(with_far(frame_ref[WET], 80, far_ref, place), 0, 10)
    march(wet, turn_ref[...], f_ref, coup_ref, *work)
    lanes = lanes_of()

    def give(l):
        for k in range(4):
            side = f_ref[k, l, 8:16]
            out = main_ref[k, l]
            out = jnp.where(lanes < STRIP, pltpu.roll(side, 96, axis=1), out)
            out_ref[k, l] = jnp.where(lanes >= 128 - STRIP, pltpu.roll(side, 32, axis=1), out)

    loop(LEV, give, unroll=4)


def local(state, mixing, wet_levels):
    lons, lats = lax.axis_size("lon"), lax.axis_size("lat")
    lat = lax.axis_index("lat")
    flags = jnp.stack([lax.rem(lat, 2), (lat == lats - 1).astype(jnp.int32)]).astype(jnp.int32)
    grid_rows = lat * 8 + jnp.array(FRAME_ROWS, jnp.int32)
    grid_rows = jnp.where(grid_rows > lats * 8 - 1, 2 * (lats * 8 - 1) - grid_rows, grid_rows).astype(jnp.float32)
    rate = CORIOLIS * jnp.sin(math.pi * (grid_rows + 0.5) / (lats * 8) - 0.9)
    rate = jnp.broadcast_to(rate[:, None], (32, 128))

    def at(o, a):
        return o * lats + a

    pairs = [(at(o, a), at(o, a ^ 1)) for o in range(lons) for a in range(lats)]
    cross = [(at(o, a), at(o, a + 1 if a % 2 else a - 1)) for o in range(lons) for a in range(1, lats - 1)]
    fold_a = [(at(o, lats - 1), at((lons - o) % lons, lats - 1)) for o in range(lons)]
    fold_b = [(at(o, lats - 1), at(lons - 1 - o, lats - 1)) for o in range(lons)]
    both = ("lon", "lat")

    half = (HALF, 8, 128)
    more = (MORE, 8, 128)
    full = pltpu.VMEM((2 * HALF, 8, 128), jnp.float32)
    full_more = pltpu.VMEM((2 * MORE, 8, 128), jnp.float32)
    x, a, b = call(gather_body, [(ITEMS, 8, 128), half, half], [SM] + [VM] * 3, 10**6, [full])(
        flags, state, mixing, wet_levels
    )
    a = lax.ppermute(a, both, cross + fold_a)
    b = lax.ppermute(b, both, cross + fold_b)
    y = lax.ppermute(x, both, pairs)
    c, d = call(outgoing_body, [more, more], [SM, VM], 10**6, [full_more])(flags, y)
    c = lax.ppermute(c, both, cross + fold_a)
    d = lax.ppermute(d, both, fold_b)
    packed = (PACKS, 32, 128)
    frame, far, to_east, to_west = call(
        frame_body, [(ITEMS, 32, 128), (FAR, 128), packed, packed], [SM] + [VM] * 6, 10**6, [full, full_more]
    )(flags, x, y, a, b, c, d)
    far = lax.ppermute(far, both, pairs)
    from_west = lax.ppermute(to_east, "lon", [(i, (i + 1) % lons) for i in range(lons)])
    from_east = lax.ppermute(to_west, "lon", [((i + 1) % lons, i) for i in range(lons)])
    (middle,) = call(main_body, [state.shape], [SM] + [VM] * 3, 10**9, WORK)(flags, frame, far, rate)
    (out,) = call(side_body, [state.shape], [SM] + [VM] * 6, 10**9, WORK)(
        flags, frame, far, rate, from_west, from_east, middle
    )
    return out


def solution(mesh):
    return jax.shard_map(
        local,
        mesh=mesh,
        in_specs=(P(None, None, "lat", "lon"), P(None, "lat", "lon"), P("lat", "lon")),
        out_specs=P(None, None, "lat", "lon"),
        check_vma=False,
    )
```

time: 1230 us -> 149 us (0.12)
  waiting for transfers between devices: 744 us -> 9.55 us
  local copies, waits for them, and re-layouts: 200 us -> 4.69 us
  blocking collectives: 76.6 us -> 0 us
  Pallas kernels: 0 us -> 64.5 us
  other arithmetic: 58.8 us -> 0.12 us
  starting transfers between devices: 121 us -> 68.9 us
  between operations: 17.3 us -> 0.14 us
    all_gather x6 -> x0, waiting for transfers between devices: 714 us -> none  [pad_tile(): gathered = lax.all_gather(outgoing, 'lon', axis=3, tiled=True)]
    rev x11 -> x0, local copies, waits for them, and re-layouts: 172 us -> none  [the longest x7 168 us: pad_tile(): reversed_rows = gathered[..., ::-1]]
    all_gather x1 -> x0, blocking collectives: 76.6 us -> none  [pad_tile(): gathered = lax.all_gather(outgoing, 'lon', axis=3, tiled=True)]
    pallas_call x0 -> x5, Pallas kernels: none -> 64.5 us  [the longest x1 31.8 us: local(): call(side_body, [state.shape], [SM] + [VM] * 6, 10 ** 9, WORK)]
    ppermute x28 -> x8, starting transfers between devices: 121 us -> 68.9 us  [the longest x1 21.9 us: local(): lax.ppermute(to_east, 'lon', [(i, (i + 1) % lons) for i in range(lons)])]
    ppermute x28 -> x8, waiting for transfers between devices: 29.3 us -> 9.55 us  [the longest x1 7.49 us: local(): b = lax.ppermute(b, both, cross + fold_b)]
    slice x36 -> x0, local copies, waits for them, and re-layouts: 17.9 us -> none  [the longest x14 9.47 us: pad_tile(): reversed_rows[..., :columns]]
    mul x54 -> x1, other arithmetic: 16.9 us -> 0.05 us  [local(): rate = CORIOLIS * jnp.sin(math.pi * (grid_rows + 0.5) / (lats * 8) - 0.9)]
  transfers between devices with their start and end apart: 34 -> 8, of which waited for: 13 -> 3; matrix products, arithmetic and copies ran while one was open for 17% -> 0% of each run, Pallas kernels for 0% -> 18%
where the time goes in v1:
time: 149 us; the launch traced here: 148 us
  starting transfers between devices  68.9 us (46%)
  Pallas kernels  64.5 us (43%)
  waiting for transfers between devices  9.55 us (6%)
  local copies, waits for them, and re-layouts  4.69 us (3%)
    pallas_call x1, Pallas kernels, local(): call(side_body, [state.shape], [SM] + [VM] * 6, 10 ** 9, WORK)  31.8 us
    pallas_call x1, Pallas kernels, local(): call(main_body, [state.shape], [SM] + [VM] * 3, 10 ** 9, WORK)  25.5 us
    ppermute x1, starting transfers between devices, local(): lax.ppermute(to_east, 'lon', [(i, (i + 1) % lons) for i in range(lons)])  21.9 us
    ppermute x1, starting transfers between devices, local(): far = lax.ppermute(far, both, pairs)  20.8 us
    ppermute x1, starting transfers between devices, local(): a = lax.ppermute(a, both, cross + fold_a)  11.3 us
    ppermute x1, starting transfers between devices, local(): c = lax.ppermute(c, both, cross + fold_a)  8.45 us
    ppermute x1, waiting for transfers between devices, local(): b = lax.ppermute(b, both, cross + fold_b)  7.49 us
    pallas_call x1, Pallas kernels, local(): call(frame_body, [(ITEMS, 32, 128), (FAR, 128), packed, packed], [SM] + [...  5.6 us
  transfers between devices with their start and end apart: 8, of which 3 were waited for; matrix products, arithmetic and copies ran while one was open for 0% of the time, Pallas kernels for 18%

profile of v1, /device:TPU:6, one launch (start us, length us, event | category | flops | bytes accessed | tf_op | source)
XLA Modules:
  0.0 147.8 jit_solution(6163535317764529657)
XLA Ops:
  0.0 0.0 copy-start.4
  0.0 0.1 pad_add_fusion.flag_ref
  0.1 0.0 copy-start.1
  0.1 1.1 copy-done.1
  1.2 0.0 copy-start.2
  1.2 0.9 copy-done.2
  2.1 0.0 copy-start.3
  2.1 0.7 copy-done.3
  2.8 0.8 shard_map.46
  3.6 1.9 %collective-permute-start = (f32[201,8,128]{2,1,0:T(8,128)S(1)}, f32[201,8,128]{2,1,0:T(8,128)S(1)}, u32[]{:S(2)}, u32[]{:S(2)}) collective-permute-start(f32[201,8,128]{2,1,0:T(8,128)S(1)} %get-tuple-element.14.x_ref), channel_id=1, source_target_pairs={{0,1},{1,0},{2,3},{3,2},{4,5},{5,4},{6,7},{7,6},{8,9},{9,8},{10,11... | collective-permute-start | bytes 2469896 | tf_op jit(solution)/shard_map/ppermute | solution.py:563
  5.6 11.3 %collective-permute-start.1 = (f32[101,8,128]{2,1,0:T(8,128)S(1)}, f32[101,8,128]{2,1,0:T(8,128)S(1)}, u32[]{:S(2)}, u32[]{:S(2)}) collective-permute-start(f32[101,8,128]{2,1,0:T(8,128)S(1)} %get-tuple-element.15), channel_id=1, source_target_pairs={{1,2},{2,1},{3,4},{4,3},{5,6},{6,5},{7,8},{8,7},{9,10},{10,9},{11,... | collective-permute-start | bytes 1241096 | tf_op jit(solution)/shard_map/ppermute | solution.py:561
  16.8 1.9 %collective-permute-start.2 = (f32[101,8,128]{2,1,0:T(8,128)S(1)}, f32[101,8,128]{2,1,0:T(8,128)S(1)}, u32[]{:S(2)}, u32[]{:S(2)}) collective-permute-start(f32[101,8,128]{2,1,0:T(8,128)S(1)} %get-tuple-element.16), channel_id=1, source_target_pairs={{1,2},{2,1},{3,4},{4,3},{5,6},{6,5},{7,8},{8,7},{9,10},{10,9},{11,... | collective-permute-start | bytes 1241096 | tf_op jit(solution)/shard_map/ppermute | solution.py:562
  18.8 0.0 collective-permute-done.y_ref
  18.8 0.7 shard_map.47
  19.4 8.4 %collective-permute-start.3 = (f32[13,8,128]{2,1,0:T(8,128)S(1)}, f32[13,8,128]{2,1,0:T(8,128)S(1)}, u32[]{:S(2)}, u32[]{:S(2)}) collective-permute-start(f32[13,8,128]{2,1,0:T(8,128)S(1)} %get-tuple-element.17), channel_id=1, source_target_pairs={{1,2},{2,1},{3,4},{4,3},{5,6},{6,5},{7,8},{8,7},{9,10},{10,9},{11,... | collective-permute-start | bytes 159752 | tf_op jit(solution)/shard_map/ppermute | solution.py:565
  27.9 0.7 collective-permute-start.4
  28.6 0.0 collective-permute-done.1.a_ref
  28.6 7.5 %collective-permute-done.2.b_ref = f32[101,8,128]{2,1,0:T(8,128)S(1)} collective-permute-done((f32[101,8,128]{2,1,0:T(8,128)S(1)}, f32[101,8,128]{2,1,0:T(8,128)S(1)}, u32[]{:S(2)}, u32[]{:S(2)}) %collective-permute-start.2) | collective-permute-done | bytes 413728 | tf_op jit(solution)/shard_map/ppermute | solution.py:562
  36.1 1.3 collective-permute-done.3.c_ref
  37.3 0.0 collective-permute-done.4.d_ref
  37.3 5.6 %shard_map.48 = (f32[201,32,128]{2,1,0:T(8,128)}, f32[88,128]{1,0:T(8,128)S(1)}, f32[20,32,128]{2,1,0:T(8,128)S(1)}, f32[20,32,128]{2,1,0:T(8,128)S(1)}) custom-call(s32[2]{0:T(128)S(1)} %pad_add_fusion.flag_ref, f32[201,8,128]{2,1,0:T(8,128)S(1)} %get-tuple-element.14.x_ref, f32[201,8,128]{2,1,0:T(8,128)S(1)} %collective-permute-done.y_ref, ...), custom_call_target="tpu_custom_call" | custom-call | flops 1000000 | bytes 4194304 | tf_op jit(solution)/shard_map/pallas_call | solution.py:568
  42.9 21.9 %collective-permute-start.6 = (f32[20,32,128]{2,1,0:T(8,128)S(1)}, f32[20,32,128]{2,1,0:T(8,128)S(1)}, u32[]{:S(2)}, u32[]{:S(2)}) collective-permute-start(f32[20,32,128]{2,1,0:T(8,128)S(1)} %get-tuple-element.21), channel_id=1, source_target_pairs={{0,16},{16,32},{32,48},{48,64},{64,80},{80,96},{96,112},{112,128},... | collective-permute-start | bytes 983048 | tf_op jit(solution)/shard_map/ppermute | solution.py:572
  64.8 1.9 %collective-permute-start.7 = (f32[20,32,128]{2,1,0:T(8,128)S(1)}, f32[20,32,128]{2,1,0:T(8,128)S(1)}, u32[]{:S(2)}, u32[]{:S(2)}) collective-permute-start(f32[20,32,128]{2,1,0:T(8,128)S(1)} %get-tuple-element.22), channel_id=1, source_target_pairs={{16,0},{32,16},{48,32},{64,48},{80,64},{96,80},{112,96},{128,112},... | collective-permute-start | bytes 983048 | tf_op jit(solution)/shard_map/ppermute | solution.py:573
  66.7 20.8 %collective-permute-start.5 = (f32[88,128]{1,0:T(8,128)S(1)}, f32[88,128]{1,0:T(8,128)S(1)}, u32[]{:S(2)}, u32[]{:S(2)}) collective-permute-start(f32[88,128]{1,0:T(8,128)S(1)} %get-tuple-element.20), channel_id=1, source_target_pairs={{0,1},{1,0},{2,3},{3,2},{4,5},{5,4},{6,7},{7,6},{8,9},{9,8},{10,11... | collective-permute-start | bytes 135176 | tf_op jit(solution)/shard_map/ppermute | solution.py:571
  87.6 0.0 copy-done.4
  87.6 0.8 collective-permute-done.5.far_ref
  88.4 0.1 broadcast_in_dim.2.turn_ref
  88.5 0.0 copy-start
  88.5 1.9 %copy-done = f32[201,32,128]{2,1,0:T(8,128)S(1)} copy-done((f32[201,32,128]{2,1,0:T(8,128)S(1)}, f32[201,32,128]{2,1,0:T(8,128)}, u32[]{:S(2)}) %copy-start) | copy-done | bytes 3293208
  90.4 25.5 %shard_map.49.main_ref = f32[4,40,8,128]{3,2,1,0:T(8,128)S(1)} custom-call(s32[2]{0:T(128)S(1)} %pad_add_fusion.flag_ref, f32[201,32,128]{2,1,0:T(8,128)S(1)} %copy-done, f32[88,128]{1,0:T(8,128)S(1)} %collective-permute-done.5.far_ref, f32[32,128]{1,0:T(8,128)S(1)} %broadcast_in_dim.2.turn_ref), custom_call_target="tpu_custom_call" | custom-call | flops 1000000000 | bytes 4194304 | tf_op jit(solution)/shard_map/pallas_call | solution.py:574
  116.0 0.0 collective-permute-done.6.east_ref
  116.0 0.0 collective-permute-done.7.west_ref
  116.0 31.8 %shard_map.50 = f32[4,40,8,128]{3,2,1,0:T(8,128)} custom-call(s32[2]{0:T(128)S(1)} %pad_add_fusion.flag_ref, f32[201,32,128]{2,1,0:T(8,128)S(1)} %copy-done, f32[88,128]{1,0:T(8,128)S(1)} %collective-permute-done.5.far_ref, f32[32,128]{1,0:T(8,128)S(1)} %broadcast_in_dim.2.turn_ref, f32[20,32,128]{2,1,0:T(8,128)S(1)} %collective-permute-done.6.east_ref, ...), custom_call_target="tpu_custom_call" | custom-call | flops 1000000000 | bytes 4194304 | tf_op jit(solution)/shard_map/pallas_call | solution.py:575
  (1 shorter events, 0.0 us)
Async XLA Ops:
  0.0 87.6 %copy-start.4 = (s32[32]{0:T(128)S(1)}, s32[32]{0:T(128)}, u32[]{:S(2)}) copy-start(s32[32]{0:T(128)} %constant.31.clone) | copy-start | bytes 388
  0.1 1.1 copy-start.1
  1.2 0.9 copy-start.2
  2.1 0.7 copy-start.3
  3.6 15.2 %collective-permute-start = (f32[201,8,128]{2,1,0:T(8,128)S(1)}, f32[201,8,128]{2,1,0:T(8,128)S(1)}, u32[]{:S(2)}, u32[]{:S(2)}) collective-permute-start(f32[201,8,128]{2,1,0:T(8,128)S(1)} %get-tuple-element.14.x_ref), channel_id=1, source_target_pairs={{0,1},{1,0},{2,3},{3,2},{4,5},{5,4},{6,7},{7,6},{8,9},{9,8},{10,11... | collective-permute-start | bytes 2469896 | tf_op jit(solution)/shard_map/ppermute | solution.py:563
  5.6 23.0 %collective-permute-start.1 = (f32[101,8,128]{2,1,0:T(8,128)S(1)}, f32[101,8,128]{2,1,0:T(8,128)S(1)}, u32[]{:S(2)}, u32[]{:S(2)}) collective-permute-start(f32[101,8,128]{2,1,0:T(8,128)S(1)} %get-tuple-element.15), channel_id=1, source_target_pairs={{1,2},{2,1},{3,4},{4,3},{5,6},{6,5},{7,8},{8,7},{9,10},{10,9},{11,... | collective-permute-start | bytes 1241096 | tf_op jit(solution)/shard_map/ppermute | solution.py:561
  16.8 19.2 %collective-permute-start.2 = (f32[101,8,128]{2,1,0:T(8,128)S(1)}, f32[101,8,128]{2,1,0:T(8,128)S(1)}, u32[]{:S(2)}, u32[]{:S(2)}) collective-permute-start(f32[101,8,128]{2,1,0:T(8,128)S(1)} %get-tuple-element.16), channel_id=1, source_target_pairs={{1,2},{2,1},{3,4},{4,3},{5,6},{6,5},{7,8},{8,7},{9,10},{10,9},{11,... | collective-permute-start | bytes 1241096 | tf_op jit(solution)/shard_map/ppermute | solution.py:562
  19.4 17.9 %collective-permute-start.3 = (f32[13,8,128]{2,1,0:T(8,128)S(1)}, f32[13,8,128]{2,1,0:T(8,128)S(1)}, u32[]{:S(2)}, u32[]{:S(2)}) collective-permute-start(f32[13,8,128]{2,1,0:T(8,128)S(1)} %get-tuple-element.17), channel_id=1, source_target_pairs={{1,2},{2,1},{3,4},{4,3},{5,6},{6,5},{7,8},{8,7},{9,10},{10,9},{11,... | collective-permute-start | bytes 159752 | tf_op jit(solution)/shard_map/ppermute | solution.py:565
  27.9 9.4 %collective-permute-start.4 = (f32[13,8,128]{2,1,0:T(8,128)S(1)}, f32[13,8,128]{2,1,0:T(8,128)S(1)}, u32[]{:S(2)}, u32[]{:S(2)}) collective-permute-start(f32[13,8,128]{2,1,0:T(8,128)S(1)} %get-tuple-element.18), channel_id=1, source_target_pairs={{15,511},{31,495},{47,479},{63,463},{79,447},{95,431},{111,415},{1... | collective-permute-start | bytes 159752 | tf_op jit(solution)/shard_map/ppermute | solution.py:566
  42.9 73.1 %collective-permute-start.6 = (f32[20,32,128]{2,1,0:T(8,128)S(1)}, f32[20,32,128]{2,1,0:T(8,128)S(1)}, u32[]{:S(2)}, u32[]{:S(2)}) collective-permute-start(f32[20,32,128]{2,1,0:T(8,128)S(1)} %get-tuple-element.21), channel_id=1, source_target_pairs={{0,16},{16,32},{32,48},{48,64},{64,80},{80,96},{96,112},{112,128},... | collective-permute-start | bytes 983048 | tf_op jit(solution)/shard_map/ppermute | solution.py:572
  64.8 51.2 %collective-permute-start.7 = (f32[20,32,128]{2,1,0:T(8,128)S(1)}, f32[20,32,128]{2,1,0:T(8,128)S(1)}, u32[]{:S(2)}, u32[]{:S(2)}) collective-permute-start(f32[20,32,128]{2,1,0:T(8,128)S(1)} %get-tuple-element.22), channel_id=1, source_target_pairs={{16,0},{32,16},{48,32},{64,48},{80,64},{96,80},{112,96},{128,112},... | collective-permute-start | bytes 983048 | tf_op jit(solution)/shard_map/ppermute | solution.py:573
  66.7 21.7 %collective-permute-start.5 = (f32[88,128]{1,0:T(8,128)S(1)}, f32[88,128]{1,0:T(8,128)S(1)}, u32[]{:S(2)}, u32[]{:S(2)}) collective-permute-start(f32[88,128]{1,0:T(8,128)S(1)} %get-tuple-element.20), channel_id=1, source_target_pairs={{0,1},{1,0},{2,3},{3,2},{4,5},{5,4},{6,7},{7,6},{8,9},{9,8},{10,11... | collective-permute-start | bytes 135176 | tf_op jit(solution)/shard_map/ppermute | solution.py:571
  88.5 1.9 %copy-start = (f32[201,32,128]{2,1,0:T(8,128)S(1)}, f32[201,32,128]{2,1,0:T(8,128)}, u32[]{:S(2)}) copy-start(f32[201,32,128]{2,1,0:T(8,128)} %get-tuple-element.19.frame_ref) | copy-start | bytes 9879556

commit v2 on v0

v2 whole, which is shorter than its diff:
```python
import math

import jax
import jax.numpy as jnp
from jax import lax
from jax.experimental import pallas as pl
from jax.experimental.pallas import tpu as pltpu
from jax.sharding import PartitionSpec as P

STEPS = 3
LEV = 40
GROUPS = LEV // 8
ADVECT = 0.15
DIFFUSE = 0.12
VISCOSITY = 0.1
PRESSURE = 0.03
CORIOLIS = 0.3
EXPAND_HEAT = 0.6
EXPAND_SALT = 0.8

TEMP, SALT, EAST, NORTH, COUP = range(5)

ROWS = 27
FRAME_ROWS = list(range(-9, 8)) + list(range(7, 17))
WET_AT = 5 * ROWS * LEV
FRAME = WET_AT + 32

OWN_WET = 40 * LEV
OWN = OWN_WET + 8
SLOT = {TEMP: 0, SALT: 8, NORTH: 16, EAST: 24, COUP: 31}
COUNT = {TEMP: 8, SALT: 8, NORTH: 8, EAST: 7, COUP: 6}
BULK_WET = 37 * LEV
HALF = (BULK_WET + 8) // 2
MORE = 144
MORE_WET = 7 * LEV
FAR = 2 * LEV + 8
STRIP = 9
WIDE = 14

STRIPS = (
    [(k, i) for k in (TEMP, SALT, NORTH) for i in range(1, 26)]
    + [(EAST, i) for i in range(2, 25)]
    + [(COUP, i) for i in range(3, 24)]
)
PACKS = -(-len(STRIPS) // WIDE)
STRIP_WET = PACKS * LEV

SPANS = (
    ((-7, 7), (7, 14), (-6, 7), (7, 13)),
    ((-4, 7), (7, 11), (-3, 7), (7, 10)),
    ((-1, 7), (8, 8), (0, 7), None),
)
PRESSURE_TILES = ((2, 10, 18), (5, 13, 14), (8, 11))
COLUMN_TILES = ((3, 11, 19), (6, 14), (9,))

VM = pl.BlockSpec(memory_space=pltpu.VMEM)
SM = pl.BlockSpec(memory_space=pltpu.SMEM)
LIMIT = 32 * 1024 * 1024
UNROLL = {"column": 4}


def call(body, outs, ins, flops, scratch=()):
    return pl.pallas_call(
        body,
        out_shape=tuple(jax.ShapeDtypeStruct(s, jnp.float32) for s in outs),
        in_specs=ins,
        out_specs=tuple(VM for _ in outs),
        scratch_shapes=[pltpu.VMEM(s, jnp.float32) for s in scratch],
        compiler_params=pltpu.CompilerParams(vmem_limit_bytes=LIMIT),
        cost_estimate=pl.CostEstimate(flops=flops, bytes_accessed=4 * 1024 * 1024, transcendentals=0),
    )


def rows_of(shape=(8, 128)):
    return lax.broadcasted_iota(jnp.int32, shape, 0)


def lanes_of(shape=(8, 128)):
    return lax.broadcasted_iota(jnp.int32, shape, 1)


def mirror(tile):
    return jnp.take_along_axis(tile, 127 - lanes_of(), axis=1)


def spread(ref, row):
    return jnp.broadcast_to(ref[row : row + 1, :], (8, 128))


def copy_block(out, to, source, at, change=lambda t: t):
    for g in range(GROUPS):
        out[to + 8 * g : to + 8 * g + 8, :] = change(source[at + 8 * g : at + 8 * g + 8, :])


def copy_blocks(out, to, source, at, count):
    if count:
        out[to : to + count * LEV, :] = source[at : at + count * LEV, :]


def split_halves(full_ref, a_ref, b_ref, rows):
    lanes = lanes_of()

    def one(k, c):
        at = pl.ds(pl.multiple_of(k * 8, 8), 8)
        near = pltpu.roll(full_ref[at, :], 64, axis=1)
        far = full_ref[pl.ds(pl.multiple_of(k * 8 + rows, 8), 8), :]
        a_ref[at, :] = jnp.where(lanes < 64, near, far)
        b_ref[at, :] = jnp.where(lanes < 64, far, near)
        return c

    lax.fori_loop(0, rows // 8, one, 0, unroll=8)


def join_halves(full_ref, a_ref, b_ref, rows):
    lanes = lanes_of()

    def one(k, c):
        at = pl.ds(pl.multiple_of(k * 8, 8), 8)
        a, b = a_ref[at, :], b_ref[at, :]
        full_ref[at, :] = jnp.where(lanes < 64, a, b)
        joined = pltpu.roll(jnp.where(lanes < 64, b, a), 64, axis=1)
        full_ref[pl.ds(pl.multiple_of(k * 8 + rows, 8), 8), :] = joined
        return c

    lax.fori_loop(0, rows // 8, one, 0, unroll=8)


def own_body(flag_ref, state_ref, mixing_ref, wet_ref, x_ref, a_ref, b_ref, full_ref):
    levels = rows_of().astype(jnp.float32)
    wet_ref_f = wet_ref[...].astype(jnp.float32)
    x_ref[OWN_WET:OWN, :] = wet_ref_f
    for r in range(8):
        wet = spread(x_ref, OWN_WET + r)
        for g in range(GROUPS):
            deep = wet > levels + float(8 * g)
            for k in range(4):
                tile = state_ref[pl.ds(k * 8 * LEV + g * 64 + r, 8, stride=8), :]
                at = (k * 8 + r) * LEV + 8 * g
                x_ref[at : at + 8, :] = jnp.where(deep, tile, 0.0)
            at = (COUP * 8 + r) * LEV + 8 * g
            tile = mixing_ref[pl.ds(g * 64 + r, 8, stride=8), :]
            x_ref[at : at + 8, :] = jnp.where(wet > levels + float(8 * g + 1), tile, 0.0)

    def ship(first_u, first_c):
        for k in SLOT:
            first = {EAST: first_u, COUP: first_c}.get(k, 0)
            copy_blocks(full_ref, SLOT[k] * LEV, x_ref, (k * 8 + first) * LEV, COUNT[k])
        full_ref[BULK_WET : BULK_WET + 8, :] = x_ref[OWN_WET:OWN, :]
        a_ref[...] = full_ref[0:HALF, :]
        b_ref[...] = full_ref[HALF : 2 * HALF, :]

    even = flag_ref[0] == 0
    fold = flag_ref[1] == 1

    @pl.when(even)
    def _():
        ship(0, 0)

    @pl.when(jnp.logical_not(even | fold))
    def _():
        ship(1, 2)

    @pl.when(fold)
    def _():
        for k in SLOT:
            sign = (lambda t: -mirror(t)) if k in (EAST, NORTH) else mirror
            for j in range(COUNT[k]):
                copy_block(full_ref, (SLOT[k] + j) * LEV, x_ref, (k * 8 + 7 - j) * LEV, sign)
        wet = jnp.zeros((8, 128), jnp.float32)
        for j in range(8):
            wet = jnp.where(rows_of() == j, spread(x_ref, OWN_WET + 7 - j), wet)
        full_ref[BULK_WET : BULK_WET + 8, :] = mirror(wet)
        split_halves(full_ref, a_ref, b_ref, HALF)


def outgoing_body(flag_ref, x_ref, y_ref, c_ref, d_ref, full_ref):
    even = flag_ref[0] == 0
    fold = flag_ref[1] == 1

    def plain(row):
        for k in (TEMP, SALT):
            copy_blocks(c_ref, k * LEV, y_ref, (k * 8 + row) * LEV, 1)
        c_ref[2 * LEV : 2 * LEV + 8, :] = spread(y_ref, OWN_WET + row)
        c_ref[2 * LEV + 8 : MORE, :] = jnp.zeros((MORE - 2 * LEV - 8, 128), jnp.float32)
        d_ref[...] = jnp.zeros((MORE, 128), jnp.float32)

    @pl.when(even)
    def _():
        plain(0)

    @pl.when(jnp.logical_not(even | fold))
    def _():
        plain(7)

    @pl.when(fold)
    def _():
        minus = lambda t: -mirror(t)
        for n, (source, k, row, change) in enumerate(
            (
                (y_ref, TEMP, 7, mirror),
                (y_ref, SALT, 7, mirror),
                (y_ref, NORTH, 7, minus),
                (y_ref, TEMP, 6, mirror),
                (y_ref, SALT, 6, mirror),
                (x_ref, EAST, 0, minus),
                (x_ref, COUP, 1, mirror),
            )
        ):
            copy_block(full_ref, n * LEV, source, (k * 8 + row) * LEV, change)
        wet = jnp.where(rows_of() == 0, spread(y_ref, OWN_WET + 7), spread(y_ref, OWN_WET + 6))
        full_ref[MORE_WET : MORE_WET + 8, :] = mirror(wet)
        split_halves(full_ref, c_ref, d_ref, MORE)


def frame_body(flag_ref, x_ref, y_ref, a_ref, b_ref, c_ref, d_ref, frame_ref, far_ref, east_ref, west_ref, full_ref, more_ref):
    even = flag_ref[0] == 0
    fold = flag_ref[1] == 1
    plain_odd = jnp.logical_not(even | fold)

    def at(k, place):
        return (k * ROWS + place) * LEV

    def bulk(k, place, slot, count):
        copy_blocks(frame_ref, at(k, place), full_ref, (SLOT[k] + slot) * LEV, count)

    def wet_rows(place, source, first, count):
        frame_ref[WET_AT + place : WET_AT + place + count, :] = source[first : first + count, :]

    def send_far(slot, wet_row):
        for k in (TEMP, SALT):
            copy_blocks(far_ref, k * LEV, full_ref, (SLOT[k] + slot) * LEV, 1)
        far_ref[2 * LEV : FAR, :] = spread(full_ref, BULK_WET + wet_row)

    frame_ref[WET_AT : WET_AT + 32, :] = jnp.zeros((32, 128), jnp.float32)

    @pl.when(jnp.logical_not(fold))
    def _():
        full_ref[0:HALF, :] = a_ref[...]
        full_ref[HALF : 2 * HALF, :] = b_ref[...]
        for k in range(5):
            copy_blocks(frame_ref, at(k, 17), x_ref, (k * 8 + 7) * LEV, 1)
        wet_rows(17, x_ref, OWN_WET + 7, 1)

    for k in range(5):
        copy_blocks(frame_ref, at(k, 9), x_ref, k * 8 * LEV, 8)
    wet_rows(9, x_ref, OWN_WET, 8)

    @pl.when(even)
    def _():
        for k in range(5):
            bulk(k, 9 - COUNT[k], 0, COUNT[k])
            copy_blocks(frame_ref, at(k, 18), y_ref, k * 8 * LEV, 8)
        wet_rows(1, full_ref, BULK_WET, 8)
        wet_rows(18, y_ref, OWN_WET, 8)
        for k in (TEMP, SALT):
            copy_blocks(frame_ref, at(k, 0), c_ref, k * LEV, 1)
            copy_blocks(frame_ref, at(k, 26), c_ref, k * LEV, 1)
        wet_rows(0, c_ref, 2 * LEV, 1)
        send_far(7, 7)

    @pl.when(jnp.logical_not(even))
    def _():
        for k in range(5):
            copy_blocks(frame_ref, at(k, 1), y_ref, k * 8 * LEV, 8)
        wet_rows(1, y_ref, OWN_WET, 8)

    @pl.when(plain_odd)
    def _():
        for k in range(5):
            bulk(k, 18, 0, COUNT[k])
        wet_rows(18, full_ref, BULK_WET, 8)
        for k in (TEMP, SALT):
            copy_blocks(frame_ref, at(k, 0), c_ref, k * LEV, 1)
            copy_blocks(frame_ref, at(k, 26), c_ref, k * LEV, 1)
        wet_rows(26, c_ref, 2 * LEV, 1)
        send_far(0, 0)

    @pl.when(fold)
    def _():
        join_halves(full_ref, a_ref, b_ref, HALF)
        join_halves(more_ref, c_ref, d_ref, MORE)
        for k in range(5):
            bulk(k, 17, 0, COUNT[k])
        wet_rows(17, full_ref, BULK_WET, 8)
        for n, (k, place) in enumerate(
            ((TEMP, 25), (SALT, 25), (NORTH, 25), (TEMP, 26), (SALT, 26), (EAST, 24), (COUP, 23))
        ):
            copy_blocks(frame_ref, at(k, place), more_ref, n * LEV, 1)
        wet_rows(25, more_ref, MORE_WET, 2)
        for k in (TEMP, SALT):
            copy_blocks(frame_ref, at(k, 0), more_ref, 3 * LEV + k * LEV, 1)
        send_far(1, 1)

    lanes = lanes_of()

    def add_strip(out, tile, n, shift):
        here = (lanes >= STRIP * n) & (lanes < STRIP * (n + 1))
        return jnp.where(here, pltpu.roll(tile, (STRIP * n + shift) % 128, axis=1), out)

    zero = jnp.zeros((8, 128), jnp.float32)

    def pack(g, c):
        first = pl.multiple_of(g * 8, 8)
        for p in range(PACKS):
            to_east = to_west = zero
            for n, (k, place) in enumerate(STRIPS[p * WIDE : (p + 1) * WIDE]):
                tile = frame_ref[pl.ds(first + at(k, place), 8), :]
                to_east = add_strip(to_east, tile, n, STRIP)
                to_west = add_strip(to_west, tile, n, 0)
            east_ref[pl.ds(first + p * LEV, 8), :] = to_east
            west_ref[pl.ds(first + p * LEV, 8), :] = to_west
        return c

    lax.fori_loop(0, GROUPS, pack, 0)
    for t in range(0, 32, 8):
        tile = frame_ref[WET_AT + t : WET_AT + t + 8, :]
        east_ref[STRIP_WET + t : STRIP_WET + t + 8, :] = add_strip(zero, tile, 0, STRIP)
        west_ref[STRIP_WET + t : STRIP_WET + t + 8, :] = add_strip(zero, tile, 0, 0)


def east_of(a):
    return pltpu.roll(a, 127, axis=1)


def west_of(a):
    return pltpu.roll(a, 1, axis=1)


def minmod(a, b):
    return jnp.maximum(jnp.minimum(a, b), 0.0) + jnp.minimum(jnp.maximum(a, b), 0.0)


def place_of(row, north):
    if north:
        return row + 10 if row >= 7 else row + 9
    return row + 9 if row <= 7 else row + 10


WINDOW = 5


def in_turn(jobs):
    waiting, active = list(jobs), []
    while waiting or active:
        if waiting and len(active) < WINDOW:
            active.append(waiting.pop(0))
        for job in list(active):
            if next(job, "end") == "end":
                active.remove(job)


ADV = LEV + 16


def march(first_step, coup, wet_ref, rate_ref, emit, f_ref, rhs_ref, adv_ref, p_ref, coef_ref, wet_e_ref):
    levels = rows_of().astype(jnp.float32)
    zero = jnp.zeros((8, 128), jnp.float32)
    wet_e_ref[...] = jnp.minimum(wet_ref[...], pltpu.roll(wet_ref[...], 127, axis=1))
    for k in range(2):
        for place in range(ROWS):
            at = (k * ROWS + place) * ADV
            adv_ref[at : at + 8, :] = zero
            adv_ref[at + 8 + LEV : at + ADV, :] = zero

    def eight(ref, k, place, level):
        return ref[pl.ds((k * ROWS + place) * LEV + level, 8, stride=LEV), :]

    def put_eight(ref, k, place, level, value):
        ref[pl.ds((k * ROWS + place) * LEV + level, 8, stride=LEV), :] = value

    def pivots(l, carry):
        done = []
        for tile, (above, up_above) in zip(COLUMN_TILES[0], carry):
            c = coup(tile, l)
            inv = 1.0 / (1.0 + c + above * (1.0 - up_above))
            up = c * inv
            put_eight(coef_ref, 0, tile, l, inv)
            put_eight(coef_ref, 1, tile, l, above * inv)
            put_eight(coef_ref, 2, tile, l, up)
            done.append((c, up))
        return tuple(done)

    lax.fori_loop(0, LEV, pivots, ((zero, zero),) * 3, unroll=4)

    def explicit(step, g):
        south_a, north_a, south_f, north_f = SPANS[step]
        first = g * 8 if isinstance(g, int) else pl.multiple_of(g * 8, 8)
        depth = levels + (float(8 * g) if isinstance(g, int) else (g * 8).astype(jnp.float32))
        cache = {}

        def once(key, make):
            if key not in cache:
                cache[key] = make()
            return cache[key]

        def field(k, place):
            def load():
                if step == 0:
                    return first_step(k, place, first)
                return f_ref[pl.ds(first + (k * ROWS + place) * LEV, 8), :]

            return once((k, place), load)

        def pressure(place):
            return once(("p", place), lambda: p_ref[pl.ds(first + place * LEV, 8), :])

        def deep(place):
            return once(("m", place), lambda: spread(wet_ref, place) > depth)

        def face_e(place):
            return once(("e", place), lambda: spread(wet_e_ref, place) > depth)

        def to_east(k, place):
            return once(("r", k, place), lambda: east_of(field(k, place)))

        jobs = []

        def piece(north, span_a, span_f):

            def here(row):
                return place_of(row, north)

            def face_n(row):
                return once(("n", north, row), lambda: deep(here(row)) & deep(here(row + 1)))

            def diff_n(k, row):
                def make():
                    return jnp.where(face_n(row), field(k, here(row + 1)) - field(k, here(row)), 0.0)

                return once(("d", north, k, row), make)

            def half_n(k, row):
                return once(("h", north, k, row), lambda: 0.5 * minmod(diff_n(k, row - 1), diff_n(k, row)))

            def speed_n(row):
                def make():
                    u = jnp.where(face_n(row), field(NORTH, here(row)) + field(NORTH, here(row + 1)), 0.0)
                    return u, u > 0.0

                return once(("s", north, row), make)

            def flux_n(k, row):
                def make():
                    speed, upward = speed_n(row)
                    below = field(k, here(row)) + half_n(k, row)
                    above = field(k, here(row + 1)) - half_n(k, row + 1)
                    return speed * jnp.where(upward, below, above)

                return once(("f", north, k, row), make)

            def work(row):
                place = here(row)
                mask_e = face_e(place)
                tracers = (TEMP, SALT)
                new_fields = span_f is not None and span_f[0] <= row <= span_f[1]
                for k in (TEMP, SALT, EAST):
                    to_east(k, place)
                if new_fields:
                    to_east(NORTH, place)
                    p_e, p_w = east_of(pressure(place)), west_of(pressure(place))
                yield
                diffs = [jnp.where(mask_e, to_east(k, place) - field(k, place), 0.0) for k in range(4 if new_fields else 2)]
                diffs_w = [west_of(d) for d in diffs]
                yield
                halves = [0.5 * minmod(diffs_w[k], diffs[k]) for k in tracers]
                beyond = [east_of(field(k, place) - halves[k]) for k in tracers]
                yield
                speed_e = jnp.where(mask_e, field(EAST, place) + to_east(EAST, place), 0.0)
                fluxes = [
                    speed_e * jnp.where(speed_e > 0.0, field(k, place) + halves[k], beyond[k]) for k in tracers
                ]
                fluxes_w = [west_of(f) for f in fluxes]
                yield
                for k in tracers:
                    div = (fluxes[k] - fluxes_w[k]) + (flux_n(k, row) - flux_n(k, row - 1))
                    out = jnp.where(deep(place), field(k, place) - (0.5 * ADVECT) * div, 0.0)
                    adv_ref[pl.ds(first + (k * ROWS + place) * ADV + 8, 8), :] = out
                if new_fields:
                    u, v = field(EAST, place), field(NORTH, place)
                    rate = spread(rate_ref, place)
                    push_n = pressure(here(row + 1)) - pressure(here(row - 1))
                    for k, other, push in ((EAST, rate * v, p_e - p_w), (NORTH, -(rate * u), push_n)):
                        lap = (diffs[k] - diffs_w[k]) + (diff_n(k, row) - diff_n(k, row - 1))
                        out = field(k, place) + other - (0.5 * PRESSURE) * push + VISCOSITY * lap
                        rhs_ref[pl.ds(first + (k * ROWS + place) * LEV, 8), :] = jnp.where(deep(place), out, 0.0)

            return [work(row) for row in range(span_a[0], span_a[1] + 1)]

        jobs += piece(False, south_a, south_f)
        jobs += piece(True, north_a, north_f)

        in_turn(jobs)

    def lateral(step, g):
        _, _, south_f, north_f = SPANS[step]
        first = g * 8 if isinstance(g, int) else pl.multiple_of(g * 8, 8)
        depth = levels + (float(8 * g) if isinstance(g, int) else (g * 8).astype(jnp.float32))
        cache = {}

        def once(key, make):
            if key not in cache:
                cache[key] = make()
            return cache[key]

        def tracer(k, place, shift=0):
            at = first + (k * ROWS + place) * ADV + 8 + shift
            return once((k, place, shift), lambda: adv_ref[pl.ds(at, 8), :])

        def grad(k, place):
            return once(("g", k, place), lambda: tracer(k, place, 1) - tracer(k, place, -1))

        def deep(place):
            return once(("m", place), lambda: spread(wet_ref, place) > depth)

        def fluxes(mask, dt, ds, gt, gs):
            gr = EXPAND_SALT * gs - EXPAND_HEAT * gt
            dr = EXPAND_SALT * ds - EXPAND_HEAT * dt
            slope = dr * gr / (gr * gr + 16.0)
            return jnp.where(mask, dt - slope * gt, 0.0), jnp.where(mask, ds - slope * gs, 0.0)

        def piece(north, span_f):
            def here(row):
                return place_of(row, north)

            def flux_n(row):
                def make():
                    a, b = here(row), here(row + 1)
                    return fluxes(
                        deep(a) & deep(b),
                        tracer(TEMP, b) - tracer(TEMP, a),
                        tracer(SALT, b) - tracer(SALT, a),
                        grad(TEMP, a) + grad(TEMP, b),
                        grad(SALT, a) + grad(SALT, b),
                    )

                return once(("f", north, row), make)

            def work(row):
                place = here(row)
                cells = [(tracer(k, place), grad(k, place)) for k in (TEMP, SALT)]
                beyond = [(east_of(q), east_of(g)) for q, g in cells]
                yield
                flux_n(row)
                yield
                (t, gt), (s, gs) = cells
                (t_e, gt_e), (s_e, gs_e) = beyond
                east = fluxes(spread(wet_e_ref, place) > depth, t_e - t, s_e - s, gt + gt_e, gs + gs_e)
                west = [west_of(f) for f in east]
                yield
                for k in (TEMP, SALT):
                    div = (east[k] - west[k]) + (flux_n(row)[k] - flux_n(row - 1)[k])
                    out = jnp.where(deep(place), cells[k][0] + DIFFUSE * div, 0.0)
                    rhs_ref[pl.ds(first + (k * ROWS + place) * LEV, 8), :] = out

            return [work(row) for row in range(span_f[0], span_f[1] + 1)]

        in_turn(piece(False, south_f) + (piece(True, north_f) if north_f else []))

    for step in range(STEPS):

        def weigh(l, carry):
            done = []
            for tile, p in zip(PRESSURE_TILES[step], carry):
                if step == 0:
                    t, s = (first_step(k, tile, l, LEV) for k in (TEMP, SALT))
                else:
                    t, s = eight(f_ref, TEMP, tile, l), eight(f_ref, SALT, tile, l)
                p = p + (EXPAND_SALT * s - EXPAND_HEAT * t)
                put_eight(p_ref, 0, tile, l, p)
                done.append(p)
            return tuple(done)

        lax.fori_loop(0, LEV, weigh, (zero,) * len(PRESSURE_TILES[step]), unroll=UNROLL["column"])

        def explicit_group(g, c):
            explicit(step, g)
            return c

        def lateral_group(g, c):
            lateral(step, g)
            return c

        lax.fori_loop(0, GROUPS, explicit_group, 0)
        lax.fori_loop(0, GROUPS, lateral_group, 0)
        tiles = COLUMN_TILES[step]

        def down(l, carry):
            done = []
            for tile, above in zip(tiles, carry):
                inv, low = eight(coef_ref, 0, tile, l), eight(coef_ref, 1, tile, l)
                solved = []
                for k in range(4):
                    x = eight(rhs_ref, k, tile, l) * inv + low * above[k]
                    put_eight(rhs_ref, k, tile, l, x)
                    solved.append(x)
                done.append(tuple(solved))
            return tuple(done)

        def up(i, carry):
            l = LEV - 1 - i
            done = []
            for tile, below in zip(tiles, carry):
                factor = eight(coef_ref, 2, tile, l)
                solved = []
                for k in range(4):
                    x = eight(rhs_ref, k, tile, l) + factor * below[k]
                    if step < STEPS - 1:
                        put_eight(f_ref, k, tile, l, x)
                    else:
                        emit(k, l, x)
                    solved.append(x)
                done.append(tuple(solved))
            return tuple(done)

        start = ((zero,) * 4,) * len(tiles)
        lax.fori_loop(0, LEV, down, start, unroll=UNROLL["column"])
        lax.fori_loop(0, LEV, up, start, unroll=UNROLL["column"])


WORK = [
    (4 * ROWS * LEV, 128),
    (4 * ROWS * LEV, 128),
    (2 * ROWS * ADV, 128),
    (ROWS * LEV, 128),
    (3 * ROWS * LEV, 128),
    (32, 128),
]


def far_place(even, place):
    return even if place == 26 else jnp.logical_not(even)


def load_wet(even, frame_ref, far_ref, wet_ref):
    wet_ref[...] = frame_ref[WET_AT : WET_AT + 32, :]
    for place in (0, 26):
        old = frame_ref[WET_AT + place : WET_AT + place + 1, :]
        wet_ref[place : place + 1, :] = jnp.where(far_place(even, place), far_ref[2 * LEV : 2 * LEV + 1, :], old)


def main_body(flag_ref, frame_ref, far_ref, rate_ref, out_ref, wet_ref, *work):
    even = flag_ref[0] == 0
    load_wet(even, frame_ref, far_ref, wet_ref)

    def first_step(k, place, row, stride=None):
        at = (k * ROWS + place) * LEV + row
        if stride is not None:
            return frame_ref[pl.ds(at, 8, stride=stride), :]
        tile = frame_ref[pl.ds(at, 8), :]
        if place in (0, 26):
            tile = jnp.where(far_place(even, place), far_ref[pl.ds(row + k * LEV, 8), :], tile)
        return tile

    def coup(place, l):
        return frame_ref[pl.ds((COUP * ROWS + place) * LEV + l, 8, stride=LEV), :]

    def emit(k, l, x):
        out_ref[k, l] = x

    march(first_step, coup, wet_ref, rate_ref, emit, *work)


def side_body(flag_ref, frame_ref, far_ref, rate_ref, east_ref, west_ref, main_ref, out_ref, wet_ref, side_ref, *work):
    even = flag_ref[0] == 0
    load_wet(even, frame_ref, far_ref, wet_ref)
    lanes = lanes_of()

    def edges(tile):
        return jnp.where(lanes < 64, pltpu.roll(tile, 32, axis=1), pltpu.roll(tile, 96, axis=1))

    def with_strips(tile, west, east, n):
        out = edges(tile)
        west = pltpu.roll(west, (32 - STRIP - STRIP * n) % 128, axis=1)
        east = pltpu.roll(east, (96 - STRIP * n) % 128, axis=1)
        out = jnp.where((lanes >= 32 - STRIP) & (lanes < 32), west, out)
        return jnp.where((lanes >= 96) & (lanes < 96 + STRIP), east, out)

    for t in range(0, 32, 8):
        at = STRIP_WET + t
        wet_ref[t : t + 8, :] = with_strips(wet_ref[t : t + 8, :], east_ref[at : at + 8, :], west_ref[at : at + 8, :], 0)

    def unpack(g, c):
        first = pl.multiple_of(g * 8, 8)
        for n, (k, place) in enumerate(STRIPS):
            at = pl.ds(first + (k * ROWS + place) * LEV, 8)
            p = pl.ds(first + n // WIDE * LEV, 8)
            side_ref[at, :] = with_strips(frame_ref[at, :], east_ref[p, :], west_ref[p, :], n % WIDE)
        for k in (TEMP, SALT):
            for place in (0, 26):
                at = pl.ds(first + (k * ROWS + place) * LEV, 8)
                far = far_ref[pl.ds(first + k * LEV, 8), :]
                side_ref[at, :] = edges(jnp.where(far_place(even, place), far, frame_ref[at, :]))
        return c

    lax.fori_loop(0, GROUPS, unpack, 0)

    def first_step(k, place, row, stride=None):
        at = (k * ROWS + place) * LEV + row
        if stride is not None:
            return side_ref[pl.ds(at, 8, stride=stride), :]
        return side_ref[pl.ds(at, 8), :]

    def coup(place, l):
        return side_ref[pl.ds((COUP * ROWS + place) * LEV + l, 8, stride=LEV), :]

    def emit(k, l, x):
        out = jnp.where(lanes < STRIP, pltpu.roll(x, 96, axis=1), main_ref[k, l])
        out_ref[k, l] = jnp.where(lanes >= 128 - STRIP, pltpu.roll(x, 32, axis=1), out)

    march(first_step, coup, wet_ref, rate_ref, emit, *work)


def local(state, mixing, wet_levels):
    lons, lats = lax.axis_size("lon"), lax.axis_size("lat")
    lat = lax.axis_index("lat")
    flags = jnp.stack([lax.rem(lat, 2), (lat == lats - 1).astype(jnp.int32)]).astype(jnp.int32)
    grid_rows = lat * 8 + jnp.array(FRAME_ROWS + [0] * (32 - ROWS), jnp.int32)
    grid_rows = jnp.where(grid_rows > lats * 8 - 1, 2 * (lats * 8 - 1) - grid_rows, grid_rows).astype(jnp.float32)
    rate = CORIOLIS * jnp.sin(math.pi * (grid_rows + 0.5) / (lats * 8) - 0.9)
    rate = jnp.broadcast_to(rate[:, None], (32, 128))

    def at(o, a):
        return o * lats + a

    pairs = [(at(o, a), at(o, a ^ 1)) for o in range(lons) for a in range(lats)]
    cross = [(at(o, a), at(o, a + 1 if a % 2 else a - 1)) for o in range(lons) for a in range(1, lats - 1)]
    fold_a = [(at(o, lats - 1), at((lons - o) % lons, lats - 1)) for o in range(lons)]
    fold_b = [(at(o, lats - 1), at(lons - 1 - o, lats - 1)) for o in range(lons)]
    both = ("lon", "lat")

    half = (HALF, 128)
    more = (MORE, 128)
    x, a, b = call(own_body, [(OWN, 128), half, half], [SM] + [VM] * 3, 10**6, [(2 * HALF, 128)])(
        flags, state.reshape(4 * LEV * 8, 128), mixing.reshape(LEV * 8, 128), wet_levels
    )
    a = lax.ppermute(a, both, cross + fold_a)
    b = lax.ppermute(b, both, cross + fold_b)
    y = lax.ppermute(x, both, pairs)
    c, d = call(outgoing_body, [more, more], [SM, VM, VM], 10**6, [(2 * MORE, 128)])(flags, x, y)
    c = lax.ppermute(c, both, cross + fold_a)
    d = lax.ppermute(d, both, fold_b)
    packed = (STRIP_WET + 32, 128)
    frame, far, to_east, to_west = call(
        frame_body,
        [(FRAME, 128), (FAR, 128), packed, packed],
        [SM] + [VM] * 6,
        10**6,
        [(2 * HALF, 128), (2 * MORE, 128)],
    )(flags, x, y, a, b, c, d)
    far = lax.ppermute(far, both, pairs)
    from_west = lax.ppermute(to_east, "lon", [(i, (i + 1) % lons) for i in range(lons)])
    from_east = lax.ppermute(to_west, "lon", [((i + 1) % lons, i) for i in range(lons)])
    wet = (32, 128)
    (middle,) = call(main_body, [state.shape], [SM] + [VM] * 3, 10**9, [wet] + WORK)(flags, frame, far, rate)
    (out,) = call(side_body, [state.shape], [SM] + [VM] * 6, 10**9, [wet, (WET_AT, 128)] + WORK)(
        flags, frame, far, rate, from_west, from_east, middle
    )
    return out


def solution(mesh):
    return jax.shard_map(
        local,
        mesh=mesh,
        in_specs=(P(None, None, "lat", "lon"), P(None, "lat", "lon"), P("lat", "lon")),
        out_specs=P(None, None, "lat", "lon"),
        check_vma=False,
    )
```

time: 1230 us -> 119 us (0.10)
  waiting for transfers between devices: 744 us -> 15.9 us
  local copies, waits for them, and re-layouts: 200 us -> 2.76 us
  blocking collectives: 76.6 us -> 0 us
  starting transfers between devices: 121 us -> 56.6 us
  other arithmetic: 58.8 us -> 0.13 us
  Pallas kernels: 0 us -> 42.9 us
  between operations: 17.3 us -> 0.14 us
    all_gather x6 -> x0, waiting for transfers between devices: 714 us -> none  [pad_tile(): gathered = lax.all_gather(outgoing, 'lon', axis=3, tiled=True)]
    rev x11 -> x0, local copies, waits for them, and re-layouts: 172 us -> none  [the longest x7 168 us: pad_tile(): reversed_rows = gathered[..., ::-1]]
    all_gather x1 -> x0, blocking collectives: 76.6 us -> none  [pad_tile(): gathered = lax.all_gather(outgoing, 'lon', axis=3, tiled=True)]
    ppermute x28 -> x8, starting transfers between devices: 121 us -> 56.6 us  [the longest x1 16.2 us: local(): lax.ppermute(to_west, 'lon', [((i + 1) % lons, i) for i in range(lons)])]
    pallas_call x0 -> x5, Pallas kernels: none -> 42.9 us  [the longest x1 21.9 us: local(): call(side_body, [state.shape], [SM] + [VM] * 6, 10 ** 9, [wet, (WET_AT, 1...]
    slice x36 -> x0, local copies, waits for them, and re-layouts: 17.9 us -> none  [the longest x14 9.47 us: pad_tile(): reversed_rows[..., :columns]]
    mul x54 -> x1, other arithmetic: 16.9 us -> 0.05 us  [local(): rate = CORIOLIS * jnp.sin(math.pi * (grid_rows + 0.5) / (lats * 8) - 0.9)]
    ppermute x28 -> x8, waiting for transfers between devices: 29.3 us -> 15.9 us  [the longest x1 11.5 us: local(): b = lax.ppermute(b, both, cross + fold_b)]
  transfers between devices with their start and end apart: 34 -> 8, of which waited for: 13 -> 2; matrix products, arithmetic and copies ran while one was open for 17% -> 0% of each run, Pallas kernels for 0% -> 15%
where the time goes in v2:
time: 119 us; the launch traced here: 118 us
  starting transfers between devices  56.6 us (48%)
  Pallas kernels  42.9 us (36%)
  waiting for transfers between devices  15.9 us (13%)
  local copies, waits for them, and re-layouts  2.76 us (2%)
    pallas_call x1, Pallas kernels, local(): call(side_body, [state.shape], [SM] + [VM] * 6, 10 ** 9, [wet, (WET_AT, 1...  21.9 us
    pallas_call x1, Pallas kernels, local(): call(main_body, [state.shape], [SM] + [VM] * 3, 10 ** 9, [wet] + WORK)  17.3 us
    ppermute x1, starting transfers between devices, local(): lax.ppermute(to_west, 'lon', [((i + 1) % lons, i) for i in range(lons)])  16.2 us
    ppermute x1, waiting for transfers between devices, local(): b = lax.ppermute(b, both, cross + fold_b)  11.5 us
    ppermute x1, starting transfers between devices, local(): a = lax.ppermute(a, both, cross + fold_a)  11.3 us
    ppermute x1, starting transfers between devices, local(): lax.ppermute(to_east, 'lon', [(i, (i + 1) % lons) for i in range(lons)])  9.24 us
    ppermute x1, starting transfers between devices, local(): c = lax.ppermute(c, both, cross + fold_a)  8.45 us
    ppermute x1, starting transfers between devices, local(): far = lax.ppermute(far, both, pairs)  6.9 us
  transfers between devices with their start and end apart: 8, of which 2 were waited for; matrix products, arithmetic and copies ran while one was open for 0% of the time, Pallas kernels for 15%

profile of v2, /device:TPU:6, one launch (start us, length us, event | category | flops | bytes accessed | tf_op | source)
XLA Modules:
  0.0 118.5 jit_solution(6582540916899322859)
XLA Ops:
  0.0 0.0 copy-start.3
  0.0 0.1 pad_add_fusion.flag_ref
  0.1 0.0 copy-start
  0.1 1.1 copy-done
  1.2 0.0 copy-start.1
  1.2 0.9 copy-done.1
  2.1 0.0 copy-start.2
  2.1 0.7 copy-done.2
  2.8 0.9 shard_map.46
  3.6 1.9 %collective-permute-start = (f32[1608,128]{1,0:T(8,128)S(1)}, f32[1608,128]{1,0:T(8,128)S(1)}, u32[]{:S(2)}, u32[]{:S(2)}) collective-permute-start(f32[1608,128]{1,0:T(8,128)S(1)} %get-tuple-element.14.x_ref), channel_id=1, source_target_pairs={{0,1},{1,0},{2,3},{3,2},{4,5},{5,4},{6,7},{7,6},{8,9},{9,8},{10,11... | collective-permute-start | bytes 2469896 | tf_op jit(solution)/shard_map/ppermute | solution.py:738
  5.6 11.3 %collective-permute-start.1 = (f32[744,128]{1,0:T(8,128)S(1)}, f32[744,128]{1,0:T(8,128)S(1)}, u32[]{:S(2)}, u32[]{:S(2)}) collective-permute-start(f32[744,128]{1,0:T(8,128)S(1)} %get-tuple-element.15), channel_id=1, source_target_pairs={{1,2},{2,1},{3,4},{4,3},{5,6},{6,5},{7,8},{8,7},{9,10},{10,9},{11,... | collective-permute-start | bytes 1142792 | tf_op jit(solution)/shard_map/ppermute | solution.py:736
  16.9 1.9 %collective-permute-start.2 = (f32[744,128]{1,0:T(8,128)S(1)}, f32[744,128]{1,0:T(8,128)S(1)}, u32[]{:S(2)}, u32[]{:S(2)}) collective-permute-start(f32[744,128]{1,0:T(8,128)S(1)} %get-tuple-element.16), channel_id=1, source_target_pairs={{1,2},{2,1},{3,4},{4,3},{5,6},{6,5},{7,8},{8,7},{9,10},{10,9},{11,... | collective-permute-start | bytes 1142792 | tf_op jit(solution)/shard_map/ppermute | solution.py:737
  18.8 0.0 collective-permute-done.y_ref
  18.8 0.6 shard_map.47
  19.4 8.4 %collective-permute-start.3 = (f32[144,128]{1,0:T(8,128)S(1)}, f32[144,128]{1,0:T(8,128)S(1)}, u32[]{:S(2)}, u32[]{:S(2)}) collective-permute-start(f32[144,128]{1,0:T(8,128)S(1)} %get-tuple-element.17), channel_id=1, source_target_pairs={{1,2},{2,1},{3,4},{4,3},{5,6},{6,5},{7,8},{8,7},{9,10},{10,9},{11,... | collective-permute-start | bytes 221192 | tf_op jit(solution)/shard_map/ppermute | solution.py:740
  27.8 0.7 collective-permute-start.4
  28.5 0.0 collective-permute-done.1.a_ref
  28.5 11.5 %collective-permute-done.2.b_ref = f32[744,128]{1,0:T(8,128)S(1)} collective-permute-done((f32[744,128]{1,0:T(8,128)S(1)}, f32[744,128]{1,0:T(8,128)S(1)}, u32[]{:S(2)}, u32[]{:S(2)}) %collective-permute-start.2) | collective-permute-done | bytes 380960 | tf_op jit(solution)/shard_map/ppermute | solution.py:737
  40.0 4.4 %collective-permute-done.3.c_ref = f32[144,128]{1,0:T(8,128)S(1)} collective-permute-done((f32[144,128]{1,0:T(8,128)S(1)}, f32[144,128]{1,0:T(8,128)S(1)}, u32[]{:S(2)}, u32[]{:S(2)}) %collective-permute-start.3) | collective-permute-done | bytes 73760 | tf_op jit(solution)/shard_map/ppermute | solution.py:740
  44.4 0.0 collective-permute-done.4.d_ref
  44.4 2.4 %shard_map.48 = (f32[5432,128]{1,0:T(8,128)S(1)}, f32[88,128]{1,0:T(8,128)S(1)}, f32[392,128]{1,0:T(8,128)S(1)}, f32[392,128]{1,0:T(8,128)S(1)}) custom-call(s32[2]{0:T(128)S(1)} %pad_add_fusion.flag_ref, f32[1608,128]{1,0:T(8,128)S(1)} %get-tuple-element.14.x_ref, f32[1608,128]{1,0:T(8,128)S(1)} %collective-permute-done.y_ref, ...), custom_call_target="tpu_custom_call" | custom-call | flops 1000000 | bytes 4194304 | tf_op jit(solution)/shard_map/pallas_call | solution.py:743
  46.8 6.9 %collective-permute-start.5 = (f32[88,128]{1,0:T(8,128)S(1)}, f32[88,128]{1,0:T(8,128)S(1)}, u32[]{:S(2)}, u32[]{:S(2)}) collective-permute-start(f32[88,128]{1,0:T(8,128)S(1)} %get-tuple-element.20), channel_id=1, source_target_pairs={{0,1},{1,0},{2,3},{3,2},{4,5},{5,4},{6,7},{7,6},{8,9},{9,8},{10,11... | collective-permute-start | bytes 135176 | tf_op jit(solution)/shard_map/ppermute | solution.py:750
  53.7 9.2 %collective-permute-start.6 = (f32[392,128]{1,0:T(8,128)S(1)}, f32[392,128]{1,0:T(8,128)S(1)}, u32[]{:S(2)}, u32[]{:S(2)}) collective-permute-start(f32[392,128]{1,0:T(8,128)S(1)} %get-tuple-element.21), channel_id=1, source_target_pairs={{0,16},{16,32},{32,48},{48,64},{64,80},{80,96},{96,112},{112,128},... | collective-permute-start | bytes 602120 | tf_op jit(solution)/shard_map/ppermute | solution.py:751
  63.0 16.2 %collective-permute-start.7 = (f32[392,128]{1,0:T(8,128)S(1)}, f32[392,128]{1,0:T(8,128)S(1)}, u32[]{:S(2)}, u32[]{:S(2)}) collective-permute-start(f32[392,128]{1,0:T(8,128)S(1)} %get-tuple-element.22), channel_id=1, source_target_pairs={{16,0},{32,16},{48,32},{64,48},{80,64},{96,80},{112,96},{128,112},... | collective-permute-start | bytes 602120 | tf_op jit(solution)/shard_map/ppermute | solution.py:752
  79.1 0.0 copy-done.3
  79.1 0.1 fusion.5
  79.2 0.0 collective-permute-done.5.far_ref
  79.2 0.1 broadcast_in_dim.2.rate_ref
  79.3 17.3 %shard_map.49.main_ref = f32[4,40,8,128]{3,2,1,0:T(8,128)S(1)} custom-call(s32[2]{0:T(128)S(1)} %pad_add_fusion.flag_ref, f32[5432,128]{1,0:T(8,128)S(1)} %get-tuple-element.19.frame_ref, f32[88,128]{1,0:T(8,128)S(1)} %collective-permute-done.5.far_ref, f32[32,128]{1,0:T(8,128)S(1)} %broadcast_in_dim.2.rate_ref), custom_call_target="tpu_custom_call" | custom-call | flops 1000000000 | bytes 4194304 | tf_op jit(solution)/shard_map/pallas_call | solution.py:754
  96.6 0.0 collective-permute-done.6.east_ref
  96.6 0.0 collective-permute-done.7.west_ref
  96.6 21.9 %shard_map.50 = f32[4,40,8,128]{3,2,1,0:T(8,128)} custom-call(s32[2]{0:T(128)S(1)} %pad_add_fusion.flag_ref, f32[5432,128]{1,0:T(8,128)S(1)} %get-tuple-element.19.frame_ref, f32[88,128]{1,0:T(8,128)S(1)} %collective-permute-done.5.far_ref, f32[32,128]{1,0:T(8,128)S(1)} %broadcast_in_dim.2.rate_ref, f32[392,128]{1,0:T(8,128)S(1)} %collective-permute-done.6.east_ref, ...), custom_call_target="tpu_custom_call" | custom-call | flops 1000000000 | bytes 4194304 | tf_op jit(solution)/shard_map/pallas_call | solution.py:755
Async XLA Ops:
  0.0 79.1 %copy-start.3 = (s32[32]{0:T(128)S(1)}, s32[32]{0:T(128)}, u32[]{:S(2)}) copy-start(s32[32]{0:T(128)} %constant.31.clone) | copy-start | bytes 388
  0.1 1.1 copy-start
  1.2 0.9 copy-start.1
  2.1 0.7 copy-start.2
  3.6 15.2 %collective-permute-start = (f32[1608,128]{1,0:T(8,128)S(1)}, f32[1608,128]{1,0:T(8,128)S(1)}, u32[]{:S(2)}, u32[]{:S(2)}) collective-permute-start(f32[1608,128]{1,0:T(8,128)S(1)} %get-tuple-element.14.x_ref), channel_id=1, source_target_pairs={{0,1},{1,0},{2,3},{3,2},{4,5},{5,4},{6,7},{7,6},{8,9},{9,8},{10,11... | collective-permute-start | bytes 2469896 | tf_op jit(solution)/shard_map/ppermute | solution.py:738
  5.6 22.9 %collective-permute-start.1 = (f32[744,128]{1,0:T(8,128)S(1)}, f32[744,128]{1,0:T(8,128)S(1)}, u32[]{:S(2)}, u32[]{:S(2)}) collective-permute-start(f32[744,128]{1,0:T(8,128)S(1)} %get-tuple-element.15), channel_id=1, source_target_pairs={{1,2},{2,1},{3,4},{4,3},{5,6},{6,5},{7,8},{8,7},{9,10},{10,9},{11,... | collective-permute-start | bytes 1142792 | tf_op jit(solution)/shard_map/ppermute | solution.py:736
  16.9 23.1 %collective-permute-start.2 = (f32[744,128]{1,0:T(8,128)S(1)}, f32[744,128]{1,0:T(8,128)S(1)}, u32[]{:S(2)}, u32[]{:S(2)}) collective-permute-start(f32[744,128]{1,0:T(8,128)S(1)} %get-tuple-element.16), channel_id=1, source_target_pairs={{1,2},{2,1},{3,4},{4,3},{5,6},{6,5},{7,8},{8,7},{9,10},{10,9},{11,... | collective-permute-start | bytes 1142792 | tf_op jit(solution)/shard_map/ppermute | solution.py:737
  19.4 25.1 %collective-permute-start.3 = (f32[144,128]{1,0:T(8,128)S(1)}, f32[144,128]{1,0:T(8,128)S(1)}, u32[]{:S(2)}, u32[]{:S(2)}) collective-permute-start(f32[144,128]{1,0:T(8,128)S(1)} %get-tuple-element.17), channel_id=1, source_target_pairs={{1,2},{2,1},{3,4},{4,3},{5,6},{6,5},{7,8},{8,7},{9,10},{10,9},{11,... | collective-permute-start | bytes 221192 | tf_op jit(solution)/shard_map/ppermute | solution.py:740
  27.8 16.6 %collective-permute-start.4 = (f32[144,128]{1,0:T(8,128)S(1)}, f32[144,128]{1,0:T(8,128)S(1)}, u32[]{:S(2)}, u32[]{:S(2)}) collective-permute-start(f32[144,128]{1,0:T(8,128)S(1)} %get-tuple-element.18), channel_id=1, source_target_pairs={{15,511},{31,495},{47,479},{63,463},{79,447},{95,431},{111,415},{1... | collective-permute-start | bytes 221192 | tf_op jit(solution)/shard_map/ppermute | solution.py:741
  46.8 32.4 %collective-permute-start.5 = (f32[88,128]{1,0:T(8,128)S(1)}, f32[88,128]{1,0:T(8,128)S(1)}, u32[]{:S(2)}, u32[]{:S(2)}) collective-permute-start(f32[88,128]{1,0:T(8,128)S(1)} %get-tuple-element.20), channel_id=1, source_target_pairs={{0,1},{1,0},{2,3},{3,2},{4,5},{5,4},{6,7},{7,6},{8,9},{9,8},{10,11... | collective-permute-start | bytes 135176 | tf_op jit(solution)/shard_map/ppermute | solution.py:750
  53.7 42.9 %collective-permute-start.6 = (f32[392,128]{1,0:T(8,128)S(1)}, f32[392,128]{1,0:T(8,128)S(1)}, u32[]{:S(2)}, u32[]{:S(2)}) collective-permute-start(f32[392,128]{1,0:T(8,128)S(1)} %get-tuple-element.21), channel_id=1, source_target_pairs={{0,16},{16,32},{32,48},{48,64},{64,80},{80,96},{96,112},{112,128},... | collective-permute-start | bytes 602120 | tf_op jit(solution)/shard_map/ppermute | solution.py:751
  63.0 33.6 %collective-permute-start.7 = (f32[392,128]{1,0:T(8,128)S(1)}, f32[392,128]{1,0:T(8,128)S(1)}, u32[]{:S(2)}, u32[]{:S(2)}) collective-permute-start(f32[392,128]{1,0:T(8,128)S(1)} %get-tuple-element.22), channel_id=1, source_target_pairs={{16,0},{32,16},{48,32},{64,48},{80,64},{96,80},{112,96},{128,112},... | collective-permute-start | bytes 602120 | tf_op jit(solution)/shard_map/ppermute | solution.py:752

commit v3 on v2

v3 whole, which is shorter than its diff:
```python
import math

import jax
import jax.numpy as jnp
from jax import lax
from jax.experimental import pallas as pl
from jax.experimental.pallas import tpu as pltpu
from jax.sharding import PartitionSpec as P

STEPS = 3
LEV = 40
GROUPS = LEV // 8
ADVECT = 0.15
DIFFUSE = 0.12
VISCOSITY = 0.1
PRESSURE = 0.03
CORIOLIS = 0.3
EXPAND_HEAT = 0.6
EXPAND_SALT = 0.8

TEMP, SALT, EAST, NORTH, COUP = range(5)

ROWS = 27
PLACE_NEAR = {16: 0, 15: 1, 14: 2, 13: 6} | {r: 14 + r for r in range(13)}
PLACE_FAR = {-9: 3, -8: 4, -7: 5} | {-r: 13 - r for r in range(7)}
PLACE_ROW = {p: r for r, p in (PLACE_NEAR | PLACE_FAR).items()} | {14: 0, 13: 0}
WET_AT = 5 * ROWS * LEV
FRAME = WET_AT + 32

OWN_WET = 40 * LEV
OWN = OWN_WET + 8
SLOT = {TEMP: 0, SALT: 8, NORTH: 16, EAST: 24, COUP: 31}
COUNT = {TEMP: 8, SALT: 8, NORTH: 8, EAST: 7, COUP: 6}
BULK_WET = 37 * LEV
HALF = (BULK_WET + 8) // 2
MORE = 144
MORE_WET = 7 * LEV
FAR = 2 * LEV + 8
STRIP = 9
WIDE = 14


class Strips:
    def __init__(self, items):
        self.items = items
        self.packs = -(-len(items) // WIDE)
        self.wet = self.packs * LEV
        self.shape = (self.wet + 32, 128)


EARLY = Strips([(k, PLACE_NEAR[r]) for k in range(4) for r in range(16)] + [(COUP, PLACE_NEAR[r]) for r in range(14)])
LATE = Strips(
    [(k, PLACE_FAR[-r]) for k in (TEMP, SALT, NORTH) for r in range(9)]
    + [(EAST, PLACE_FAR[-r]) for r in range(8)]
    + [(COUP, PLACE_FAR[-r]) for r in range(7)]
)

PARTS = {
    "early": (
        (range(2, 14), (), range(3, 13), (), (6, 16, 19), (17, 19)),
        (range(5, 11), (), range(6, 10), (), (19,), (19,)),
    ),
    "late": (
        ((0, 1, 14), range(0, -8, -1), (0, 1, 2, 13), range(0, -7, -1), (2, 10, 19), (6, 14)),
        ((0, 1, 2, 3, 4, 11), range(0, -5, -1), (0, 1, 2, 3, 4, 5, 10), range(0, -4, -1), (9, 17, 19), (10, 18)),
        (range(0, 9), (-1,), range(0, 8), (), (12, 15), (14,)),
    ),
}
PIVOT_TILES = {"early": (17, 19), "late": (6, 14, 19)}
HANDED = ((range(3, 13), (2, 3, 12, 13)), (range(6, 10), (5, 6, 9, 10)))

VM = pl.BlockSpec(memory_space=pltpu.VMEM)
SM = pl.BlockSpec(memory_space=pltpu.SMEM)
LIMIT = 32 * 1024 * 1024
UNROLL = {"column": 4}


def call(body, outs, ins, flops, scratch=()):
    return pl.pallas_call(
        body,
        out_shape=tuple(jax.ShapeDtypeStruct(s, jnp.float32) for s in outs),
        in_specs=ins,
        out_specs=tuple(VM for _ in outs),
        scratch_shapes=[pltpu.VMEM(s, jnp.float32) for s in scratch],
        compiler_params=pltpu.CompilerParams(vmem_limit_bytes=LIMIT),
        cost_estimate=pl.CostEstimate(flops=flops, bytes_accessed=4 * 1024 * 1024, transcendentals=0),
    )


def rows_of(shape=(8, 128)):
    return lax.broadcasted_iota(jnp.int32, shape, 0)


def lanes_of(shape=(8, 128)):
    return lax.broadcasted_iota(jnp.int32, shape, 1)


def mirror(tile):
    return jnp.take_along_axis(tile, 127 - lanes_of(), axis=1)


def spread(ref, row):
    return jnp.broadcast_to(ref[row : row + 1, :], (8, 128))


def copy_block(out, to, source, at, change=lambda t: t):
    for g in range(GROUPS):
        out[to + 8 * g : to + 8 * g + 8, :] = change(source[at + 8 * g : at + 8 * g + 8, :])


def copy_blocks(out, to, source, at, count):
    if count:
        out[to : to + count * LEV, :] = source[at : at + count * LEV, :]


def split_halves(full_ref, a_ref, b_ref, rows):
    lanes = lanes_of()

    def one(k, c):
        at = pl.ds(pl.multiple_of(k * 8, 8), 8)
        near = pltpu.roll(full_ref[at, :], 64, axis=1)
        far = full_ref[pl.ds(pl.multiple_of(k * 8 + rows, 8), 8), :]
        a_ref[at, :] = jnp.where(lanes < 64, near, far)
        b_ref[at, :] = jnp.where(lanes < 64, far, near)
        return c

    lax.fori_loop(0, rows // 8, one, 0, unroll=8)


def join_halves(full_ref, a_ref, b_ref, rows):
    lanes = lanes_of()

    def one(k, c):
        at = pl.ds(pl.multiple_of(k * 8, 8), 8)
        a, b = a_ref[at, :], b_ref[at, :]
        full_ref[at, :] = jnp.where(lanes < 64, a, b)
        joined = pltpu.roll(jnp.where(lanes < 64, b, a), 64, axis=1)
        full_ref[pl.ds(pl.multiple_of(k * 8 + rows, 8), 8), :] = joined
        return c

    lax.fori_loop(0, rows // 8, one, 0, unroll=8)


def own_body(flag_ref, state_ref, mixing_ref, wet_ref, x_ref, a_ref, b_ref, full_ref):
    levels = rows_of().astype(jnp.float32)
    odd = flag_ref[0] == 1
    fold = flag_ref[1] == 1
    order = jnp.where(odd, 7 - rows_of(), rows_of())
    x_ref[OWN_WET:OWN, :] = jnp.take_along_axis(wet_ref[...].astype(jnp.float32), order, axis=0)

    def load(turned):
        for r in range(8):
            wet = spread(x_ref, OWN_WET + r)
            source = 7 - r if turned else r
            for g in range(GROUPS):
                deep = wet > levels + float(8 * g)
                for k in range(4):
                    tile = state_ref[pl.ds(k * 8 * LEV + g * 64 + source, 8, stride=8), :]
                    at = (k * 8 + r) * LEV + 8 * g
                    x_ref[at : at + 8, :] = jnp.where(deep, -tile if turned and k == NORTH else tile, 0.0)
                at = (COUP * 8 + r) * LEV + 8 * g
                tile = mixing_ref[pl.ds(g * 64 + source, 8, stride=8), :]
                x_ref[at : at + 8, :] = jnp.where(wet > levels + float(8 * g + 1), tile, 0.0)

    pl.when(odd)(lambda: load(True))
    pl.when(jnp.logical_not(odd))(lambda: load(False))

    @pl.when(jnp.logical_not(fold))
    def _():
        for k in SLOT:
            if k == NORTH:
                for j in range(COUNT[k]):
                    copy_block(full_ref, (SLOT[k] + j) * LEV, x_ref, (k * 8 + j) * LEV, lambda t: -t)
            else:
                copy_blocks(full_ref, SLOT[k] * LEV, x_ref, k * 8 * LEV, COUNT[k])
        full_ref[BULK_WET : BULK_WET + 8, :] = x_ref[OWN_WET:OWN, :]
        a_ref[...] = full_ref[0:HALF, :]
        b_ref[...] = full_ref[HALF : 2 * HALF, :]

    @pl.when(fold)
    def _():
        for k in SLOT:
            sign = (lambda t: -mirror(t)) if k in (EAST, NORTH) else mirror
            for j in range(COUNT[k]):
                copy_block(full_ref, (SLOT[k] + j) * LEV, x_ref, (k * 8 + j) * LEV, sign)
        full_ref[BULK_WET : BULK_WET + 8, :] = mirror(x_ref[OWN_WET:OWN, :])
        split_halves(full_ref, a_ref, b_ref, HALF)


def block_at(k, place):
    return (k * ROWS + place) * LEV


def wet_row(ref, place, source, row):
    ref[WET_AT + place : WET_AT + place + 1, :] = source[row : row + 1, :]


def pack_strips(strips, frame_ref, east_ref, west_ref):
    lanes = lanes_of()
    zero = jnp.zeros((8, 128), jnp.float32)

    def add_strip(out, tile, n, shift):
        here = (lanes >= STRIP * n) & (lanes < STRIP * (n + 1))
        return jnp.where(here, pltpu.roll(tile, (STRIP * n + shift) % 128, axis=1), out)

    def pack(g, c):
        first = pl.multiple_of(g * 8, 8)
        for p in range(strips.packs):
            to_east = to_west = zero
            for n, (k, place) in enumerate(strips.items[p * WIDE : (p + 1) * WIDE]):
                tile = frame_ref[pl.ds(first + block_at(k, place), 8), :]
                to_east = add_strip(to_east, tile, n, STRIP)
                to_west = add_strip(to_west, tile, n, 0)
            east_ref[pl.ds(first + p * LEV, 8), :] = to_east
            west_ref[pl.ds(first + p * LEV, 8), :] = to_west
        return c

    lax.fori_loop(0, GROUPS, pack, 0)
    for t in range(0, 32, 8):
        tile = frame_ref[WET_AT + t : WET_AT + t + 8, :]
        east_ref[strips.wet + t : strips.wet + t + 8, :] = add_strip(zero, tile, 0, STRIP)
        west_ref[strips.wet + t : strips.wet + t + 8, :] = add_strip(zero, tile, 0, 0)


def early_frame_body(flag_ref, x_ref, y_ref, b_in, b_ref, c_ref, frame_ref, east_ref, west_ref, full_ref):
    fold = flag_ref[1] == 1
    b_ref[0:HALF, :] = b_in[...]

    @pl.when(jnp.logical_not(fold))
    def _():
        for k in (TEMP, SALT):
            copy_blocks(b_ref, HALF + k * LEV, y_ref, (k * 8 + 7) * LEV, 1)
        b_ref[HALF + 2 * LEV : HALF + 2 * LEV + 8, :] = spread(y_ref, OWN_WET + 7)
        b_ref[HALF + 2 * LEV + 8 : HALF + MORE, :] = jnp.zeros((MORE - 2 * LEV - 8, 128), jnp.float32)
        c_ref[...] = jnp.zeros((MORE, 128), jnp.float32)

    @pl.when(fold)
    def _():
        for n, (source, k, row, change) in enumerate(
            (
                (y_ref, TEMP, 7, mirror),
                (y_ref, SALT, 7, mirror),
                (y_ref, NORTH, 7, mirror),
                (y_ref, TEMP, 6, mirror),
                (y_ref, SALT, 6, mirror),
                (x_ref, EAST, 7, lambda t: -mirror(t)),
                (x_ref, COUP, 6, mirror),
            )
        ):
            copy_block(full_ref, n * LEV, source, (k * 8 + row) * LEV, change)
        wet = jnp.where(rows_of() == 0, spread(y_ref, OWN_WET + 7), spread(y_ref, OWN_WET + 6))
        full_ref[MORE_WET : MORE_WET + 8, :] = mirror(wet)
        split_halves(full_ref, c_ref, b_ref.at[HALF : HALF + MORE], MORE)

    frame_ref[...] = jnp.zeros((FRAME, 128), jnp.float32)
    for k in range(5):
        copy_blocks(frame_ref, block_at(k, PLACE_NEAR[0]), x_ref, k * 8 * LEV, 8)
        for r in range(8, 16):
            change = (lambda t: -t) if k == NORTH else (lambda t: t)
            copy_block(frame_ref, block_at(k, PLACE_NEAR[r]), y_ref, (k * 8 + 15 - r) * LEV, change)
    for r in range(8):
        wet_row(frame_ref, PLACE_NEAR[r], x_ref, OWN_WET + r)
        wet_row(frame_ref, PLACE_NEAR[r + 8], y_ref, OWN_WET + 7 - r)
    pack_strips(EARLY, frame_ref, east_ref, west_ref)


def frame_body(
    flag_ref, early_ref, a_ref, b_ref, c_ref, main_early, side_early, frame_ref, far_ref, east_ref, west_ref, full_ref, more_ref
):
    fold = flag_ref[1] == 1

    def bulk(k, row, slot, count):
        for j in range(count):
            copy_blocks(frame_ref, block_at(k, PLACE_FAR[row - j]), full_ref, (SLOT[k] + slot + j) * LEV, 1)

    def send_far(slot):
        for k in (TEMP, SALT):
            copy_blocks(far_ref, k * LEV, full_ref, (SLOT[k] + slot) * LEV, 1)
        far_ref[2 * LEV : FAR, :] = spread(full_ref, BULK_WET + slot)

    frame_ref[...] = early_ref[...]

    @pl.when(jnp.logical_not(fold))
    def _():
        full_ref[0:HALF, :] = a_ref[...]
        full_ref[HALF : 2 * HALF, :] = b_ref[0:HALF, :]
        for k in range(5):
            copy_blocks(frame_ref, block_at(k, PLACE_FAR[0]), early_ref, block_at(k, PLACE_NEAR[0]), 1)
            bulk(k, -1, 0, COUNT[k])
        wet_row(frame_ref, PLACE_FAR[0], early_ref, WET_AT + PLACE_NEAR[0])
        for r in range(8):
            wet_row(frame_ref, PLACE_FAR[-1 - r], full_ref, BULK_WET + r)
        for k in (TEMP, SALT):
            copy_blocks(frame_ref, block_at(k, PLACE_FAR[-9]), b_ref, HALF + k * LEV, 1)
        wet_row(frame_ref, PLACE_FAR[-9], b_ref, HALF + 2 * LEV)
        send_far(0)

    @pl.when(fold)
    def _():
        join_halves(full_ref, a_ref, b_ref, HALF)
        join_halves(more_ref, c_ref, b_ref.at[HALF : HALF + MORE], MORE)
        for k in range(5):
            bulk(k, 0, 0, COUNT[k])
        for r in range(8):
            wet_row(frame_ref, PLACE_FAR[-r], full_ref, BULK_WET + r)
        for n, (k, row) in enumerate(
            ((TEMP, -8), (SALT, -8), (NORTH, -8), (TEMP, -9), (SALT, -9), (EAST, -7), (COUP, -6))
        ):
            copy_blocks(frame_ref, block_at(k, PLACE_FAR[row]), more_ref, n * LEV, 1)
        wet_row(frame_ref, PLACE_FAR[-8], more_ref, MORE_WET)
        wet_row(frame_ref, PLACE_FAR[-9], more_ref, MORE_WET + 1)
        send_far(1)

    pack_strips(LATE, frame_ref, east_ref, west_ref)


def east_of(a):
    return pltpu.roll(a, 127, axis=1)


def west_of(a):
    return pltpu.roll(a, 1, axis=1)


def minmod(a, b):
    return jnp.maximum(jnp.minimum(a, b), 0.0) + jnp.minimum(jnp.maximum(a, b), 0.0)


def place_of(row, far):
    if far:
        return PLACE_FAR[row] if row <= 0 else PLACE_NEAR[row]
    return PLACE_NEAR[row] if row >= 0 else PLACE_FAR[row]


WINDOW = 5


def in_turn(jobs):
    waiting, active = list(jobs), []
    while waiting or active:
        if waiting and len(active) < WINDOW:
            active.append(waiting.pop(0))
        for job in list(active):
            if next(job, "end") == "end":
                active.remove(job)


ADV = LEV + 16


def march(
    part, frame_ref, wet_ref, rate_ref, after, emit, f_ref, rhs_ref, adv_ref, adv_e_ref, p_ref, coef_ref, wet_e_ref
):
    levels = rows_of().astype(jnp.float32)
    zero = jnp.zeros((8, 128), jnp.float32)
    spans = PARTS[part]
    last = len(spans) - 1
    wet_e_ref[...] = jnp.minimum(wet_ref[...], pltpu.roll(wet_ref[...], 127, axis=1))
    for k in range(2):
        for place in range(ROWS):
            at = (k * ROWS + place) * ADV
            for ref in (adv_ref, adv_e_ref):
                ref[at : at + 8, :] = zero
                ref[at + 8 + LEV : at + ADV, :] = zero

    def eight(ref, k, place, level):
        return ref[pl.ds((k * ROWS + place) * LEV + level, 8, stride=LEV), :]

    def put_eight(ref, k, place, level, value):
        ref[pl.ds((k * ROWS + place) * LEV + level, 8, stride=LEV), :] = value

    def pivots(l, carry):
        done = []
        for tile, (above, up_above) in zip(PIVOT_TILES[part], carry):
            c = eight(frame_ref, COUP, tile, l)
            inv = 1.0 / (1.0 + c + above * (1.0 - up_above))
            up = c * inv
            put_eight(coef_ref, 0, tile, l, inv)
            put_eight(coef_ref, 1, tile, l, above * inv)
            put_eight(coef_ref, 2, tile, l, up)
            done.append((c, up))
        return tuple(done)

    lax.fori_loop(0, LEV, pivots, ((zero, zero),) * len(PIVOT_TILES[part]), unroll=4)

    def explicit(step, g):
        near_a, far_a, near_f, far_f = spans[step][:4]
        first = g * 8 if isinstance(g, int) else pl.multiple_of(g * 8, 8)
        depth = levels + (float(8 * g) if isinstance(g, int) else (g * 8).astype(jnp.float32))
        cache = {}

        def once(key, make):
            if key not in cache:
                cache[key] = make()
            return cache[key]

        def field(k, place):
            ref = frame_ref if step == 0 else f_ref
            return once((k, place), lambda: ref[pl.ds(first + block_at(k, place), 8), :])

        def pressure(place):
            return once(("p", place), lambda: p_ref[pl.ds(first + place * LEV, 8), :])

        def deep(place):
            return once(("m", place), lambda: spread(wet_ref, place) > depth)

        def face_e(place):
            return once(("e", place), lambda: spread(wet_e_ref, place) > depth)

        def to_east(k, place):
            return once(("r", k, place), lambda: east_of(field(k, place)))

        def piece(far, span_a, span_f):

            def here(row):
                return place_of(row, far)

            def face_n(row):
                return once(("n", far, row), lambda: deep(here(row)) & deep(here(row + 1)))

            def diff_n(k, row):
                def make():
                    return jnp.where(face_n(row), field(k, here(row + 1)) - field(k, here(row)), 0.0)

                return once(("d", far, k, row), make)

            def half_n(k, row):
                return once(("h", far, k, row), lambda: 0.5 * minmod(diff_n(k, row - 1), diff_n(k, row)))

            def speed_n(row):
                def make():
                    u = jnp.where(face_n(row), field(NORTH, here(row)) + field(NORTH, here(row + 1)), 0.0)
                    return u, u > 0.0

                return once(("s", far, row), make)

            def flux_n(k, row):
                def make():
                    speed, upward = speed_n(row)
                    below = field(k, here(row)) + half_n(k, row)
                    above = field(k, here(row + 1)) - half_n(k, row + 1)
                    return speed * jnp.where(upward, below, above)

                return once(("f", far, k, row), make)

            def work(row):
                place = here(row)
                mask_e = face_e(place)
                tracers = (TEMP, SALT)
                new_fields = row in span_f
                for k in (TEMP, SALT, EAST):
                    to_east(k, place)
                if new_fields:
                    to_east(NORTH, place)
                    p_e = east_of(pressure(place))
                yield
                diffs = [jnp.where(mask_e, to_east(k, place) - field(k, place), 0.0) for k in range(4 if new_fields else 2)]
                terms = list(diffs)
                if new_fields:
                    terms[EAST] = VISCOSITY * diffs[EAST] - (0.5 * PRESSURE) * pressure(place)
                diffs_w = [west_of(d) for d in terms]
                yield
                halves = [0.5 * minmod(diffs_w[k], diffs[k]) for k in tracers]
                beyond = [east_of(field(k, place) - halves[k]) for k in tracers]
                yield
                speed_e = jnp.where(mask_e, field(EAST, place) + to_east(EAST, place), 0.0)
                fluxes = [
                    speed_e * jnp.where(speed_e > 0.0, field(k, place) + halves[k], beyond[k]) for k in tracers
                ]
                fluxes_w = [west_of(f) for f in fluxes]
                yield
                for k in tracers if row in span_a else ():
                    div = (fluxes[k] - fluxes_w[k]) + (flux_n(k, row) - flux_n(k, row - 1))
                    out = jnp.where(deep(place), field(k, place) - (0.5 * ADVECT) * div, 0.0)
                    adv_ref[pl.ds(first + (k * ROWS + place) * ADV + 8, 8), :] = out
                    if new_fields:
                        adv_e_ref[pl.ds(first + (k * ROWS + place) * ADV + 8, 8), :] = east_of(out)
                if new_fields:
                    u, v = field(EAST, place), field(NORTH, place)
                    rate = spread(rate_ref, place)
                    push_n = pressure(here(row + 1)) - pressure(here(row - 1))
                    lap_n = [diff_n(k, row) - diff_n(k, row - 1) for k in (EAST, NORTH)]
                    u1 = u + rate * v - (0.5 * PRESSURE) * p_e + VISCOSITY * (diffs[EAST] + lap_n[0]) - diffs_w[EAST]
                    lap = (diffs[NORTH] - diffs_w[NORTH]) + lap_n[1]
                    v1 = v - rate * u - (0.5 * PRESSURE) * push_n + VISCOSITY * lap
                    for k, out in ((EAST, u1), (NORTH, v1)):
                        rhs_ref[pl.ds(first + (k * ROWS + place) * LEV, 8), :] = jnp.where(deep(place), out, 0.0)

            return [work(row) for row in sorted({*span_a, *span_f})]

        in_turn(piece(False, near_a, near_f) + piece(True, far_a, far_f))

    def lateral(step, g):
        near_f, far_f = spans[step][2:4]
        first = g * 8 if isinstance(g, int) else pl.multiple_of(g * 8, 8)
        depth = levels + (float(8 * g) if isinstance(g, int) else (g * 8).astype(jnp.float32))
        cache = {}

        def once(key, make):
            if key not in cache:
                cache[key] = make()
            return cache[key]

        def tracer(k, place, shift=0):
            at = first + (k * ROWS + place) * ADV + 8 + shift
            return once((k, place, shift), lambda: adv_ref[pl.ds(at, 8), :])

        def grad(k, place):
            return once(("g", k, place), lambda: tracer(k, place, 1) - tracer(k, place, -1))

        def deep(place):
            return once(("m", place), lambda: spread(wet_ref, place) > depth)

        def fluxes(mask, dt, ds, gt, gs):
            gr = EXPAND_SALT * gs - EXPAND_HEAT * gt
            dr = EXPAND_SALT * ds - EXPAND_HEAT * dt
            slope = dr * gr / (gr * gr + 16.0)
            return jnp.where(mask, dt - slope * gt, 0.0), jnp.where(mask, ds - slope * gs, 0.0)

        def piece(far, span_f):
            def here(row):
                return place_of(row, far)

            def flux_n(row):
                def make():
                    a, b = here(row), here(row + 1)
                    return fluxes(
                        deep(a) & deep(b),
                        tracer(TEMP, b) - tracer(TEMP, a),
                        tracer(SALT, b) - tracer(SALT, a),
                        grad(TEMP, a) + grad(TEMP, b),
                        grad(SALT, a) + grad(SALT, b),
                    )

                return once(("f", far, row), make)

            def work(row):
                place = here(row)
                cells = [(tracer(k, place), grad(k, place)) for k in (TEMP, SALT)]
                beyond = []
                for k in (TEMP, SALT):
                    at = first + (k * ROWS + place) * ADV + 8
                    q, below, above = (adv_e_ref[pl.ds(at + shift, 8), :] for shift in (0, 1, -1))
                    beyond.append((q, below - above))
                yield
                flux_n(row)
                yield
                (t, gt), (s, gs) = cells
                (t_e, gt_e), (s_e, gs_e) = beyond
                east = fluxes(spread(wet_e_ref, place) > depth, t_e - t, s_e - s, gt + gt_e, gs + gs_e)
                west = [west_of(f) for f in east]
                yield
                for k in (TEMP, SALT):
                    div = (east[k] - west[k]) + (flux_n(row)[k] - flux_n(row - 1)[k])
                    out = jnp.where(deep(place), cells[k][0] + DIFFUSE * div, 0.0)
                    rhs_ref[pl.ds(first + (k * ROWS + place) * LEV, 8), :] = out

            return [work(row) for row in sorted(span_f)]

        in_turn(piece(False, near_f) + piece(True, far_f))

    for step in range(len(spans)):
        source = frame_ref if step == 0 else f_ref
        weights, tiles = spans[step][4:]

        def weigh(l, carry):
            done = []
            for tile, p in zip(weights, carry):
                p = p + (EXPAND_SALT * eight(source, SALT, tile, l) - EXPAND_HEAT * eight(source, TEMP, tile, l))
                put_eight(p_ref, 0, tile, l, p)
                done.append(p)
            return tuple(done)

        lax.fori_loop(0, LEV, weigh, (zero,) * len(weights), unroll=UNROLL["column"])

        def explicit_group(g, c):
            explicit(step, g)
            return c

        def lateral_group(g, c):
            lateral(step, g)
            return c

        lax.fori_loop(0, GROUPS, explicit_group, 0)
        after(step, "adv")
        lax.fori_loop(0, GROUPS, lateral_group, 0)

        def down(l, carry):
            loads = [(eight(coef_ref, 0, t, l), eight(coef_ref, 1, t, l), [eight(rhs_ref, k, t, l) for k in range(4)]) for t in tiles]
            done = []
            for (inv, low, rhs), above in zip(loads, carry):
                done.append(tuple(rhs[k] * inv + low * above[k] for k in range(4)))
            for tile, solved in zip(tiles, done):
                for k in range(4):
                    put_eight(rhs_ref, k, tile, l, solved[k])
            return tuple(done)

        def up(i, carry):
            l = LEV - 1 - i
            done = []
            for tile, below in zip(tiles, carry):
                factor = eight(coef_ref, 2, tile, l)
                solved = []
                for k in range(4):
                    x = eight(rhs_ref, k, tile, l) + factor * below[k]
                    if emit is None or step < last:
                        put_eight(f_ref, k, tile, l, x)
                    else:
                        emit(k, l, x)
                    solved.append(x)
                done.append(tuple(solved))
            return tuple(done)

        start = ((zero,) * 4,) * len(tiles)
        lax.fori_loop(0, LEV, down, start, unroll=UNROLL["column"])
        lax.fori_loop(0, LEV, up, start, unroll=UNROLL["column"])
        after(step, "new")


WORK = [
    (4 * ROWS * LEV, 128),
    (4 * ROWS * LEV, 128),
    (2 * ROWS * ADV, 128),
    (2 * ROWS * ADV, 128),
    (ROWS * LEV, 128),
    (3 * ROWS * LEV, 128),
    (32, 128),
]
HANDED_SHAPES = [
    shape for rows, adv_rows in HANDED for shape in ((2 * len(adv_rows) * ADV, 128), (4 * len(rows) * LEV, 128))
]


def early(frame_ref, wet_ref, rate_ref, outs, work):
    f_ref, _, adv_ref = work[:3]

    def after(step, what):
        rows, adv_rows = HANDED[step]
        adv_out, new_out = outs[2 * step : 2 * step + 2]
        if what == "adv":
            for k in range(2):
                for n, r in enumerate(adv_rows):
                    at, to = (k * ROWS + PLACE_NEAR[r]) * ADV, (k * len(adv_rows) + n) * ADV
                    adv_out[to : to + ADV, :] = adv_ref[at : at + ADV, :]
        else:
            for k in range(4):
                copy_blocks(new_out, k * len(rows) * LEV, f_ref, block_at(k, PLACE_NEAR[rows[0]]), len(rows))

    march("early", frame_ref, wet_ref, rate_ref, after, None, *work)


def late(frame_ref, wet_ref, rate_ref, emit, ins, work):
    f_ref, _, adv_ref, adv_e_ref = work[:4]

    def after(step, what):
        if step >= len(HANDED):
            return
        rows, adv_rows = HANDED[step]
        adv_in, new_in = ins[2 * step : 2 * step + 2]
        if what == "adv":
            for k in range(2):
                for n, r in enumerate(adv_rows):
                    at, source = (k * ROWS + PLACE_NEAR[r]) * ADV, (k * len(adv_rows) + n) * ADV
                    adv_ref[at : at + ADV, :] = adv_in[source : source + ADV, :]
                    if r in PARTS["late"][step][2]:
                        for g in range(GROUPS):
                            to, part = at + 8 + 8 * g, source + 8 + 8 * g
                            adv_e_ref[to : to + 8, :] = east_of(adv_in[part : part + 8, :])
        else:
            for k in range(4):
                copy_blocks(f_ref, block_at(k, PLACE_NEAR[rows[0]]), new_in, k * len(rows) * LEV, len(rows))

    march("late", frame_ref, wet_ref, rate_ref, after, emit, *work)


def early_main_body(flag_ref, frame_ref, rate_ref, *rest):
    outs, (wet_ref, *work) = rest[:4], rest[4:]
    wet_ref[...] = frame_ref[WET_AT : WET_AT + 32, :]
    early(frame_ref, wet_ref, rate_ref, outs, work)


def edges(tile):
    return jnp.where(lanes_of() < 64, pltpu.roll(tile, 32, axis=1), pltpu.roll(tile, 96, axis=1))


def with_strips(tile, west, east, n):
    lanes = lanes_of()
    out = edges(tile)
    west = pltpu.roll(west, (32 - STRIP - STRIP * n) % 128, axis=1)
    east = pltpu.roll(east, (96 - STRIP * n) % 128, axis=1)
    out = jnp.where((lanes >= 32 - STRIP) & (lanes < 32), west, out)
    return jnp.where((lanes >= 96) & (lanes < 96 + STRIP), east, out)


def unpack_strips(strips, frame_ref, east_ref, west_ref, side_ref):
    def unpack(g, c):
        first = pl.multiple_of(g * 8, 8)
        for n, (k, place) in enumerate(strips.items):
            at = pl.ds(first + block_at(k, place), 8)
            p = pl.ds(first + n // WIDE * LEV, 8)
            side_ref[at, :] = with_strips(frame_ref[at, :], east_ref[p, :], west_ref[p, :], n % WIDE)
        return c

    lax.fori_loop(0, GROUPS, unpack, 0)


def unpack_wet(strips, tile_ref, east_ref, west_ref, out_ref, base, places):
    rows = rows_of()
    for t in range(0, 32, 8):
        at = strips.wet + t
        here = [p - t for p in places if t <= p < t + 8]
        if here:
            tile = with_strips(tile_ref[WET_AT + t : WET_AT + t + 8, :], east_ref[at : at + 8, :], west_ref[at : at + 8, :], 0)
            mask = rows == here[0]
            for p in here[1:]:
                mask = mask | (rows == p)
            out_ref[base + t : base + t + 8, :] = jnp.where(mask, tile, out_ref[base + t : base + t + 8, :])


def early_side_body(flag_ref, frame_ref, rate_ref, east_ref, west_ref, side_ref, *rest):
    outs, work = rest[:4], rest[4:]
    wet_ref, *work = work
    side_ref[...] = jnp.zeros((FRAME, 128), jnp.float32)
    unpack_strips(EARLY, frame_ref, east_ref, west_ref, side_ref)
    unpack_wet(EARLY, frame_ref, east_ref, west_ref, side_ref, WET_AT, [PLACE_NEAR[r] for r in range(16)])
    wet_ref[...] = side_ref[WET_AT : WET_AT + 32, :]
    early(side_ref, wet_ref, rate_ref, outs, work)


def late_main_body(flag_ref, frame_in, far_ref, rate_ref, *rest):
    ins, (out_ref, frame_ref, wet_ref, *work) = rest[:4], rest[4:]
    frame_ref[...] = frame_in[...]
    for k in (TEMP, SALT):
        copy_blocks(frame_ref, block_at(k, PLACE_NEAR[16]), far_ref, k * LEV, 1)
    wet_row(frame_ref, PLACE_NEAR[16], far_ref, 2 * LEV)
    wet_ref[...] = frame_ref[WET_AT : WET_AT + 32, :]

    def emit(k, l, x):
        out_ref[k, l] = x

    late(frame_ref, wet_ref, rate_ref, emit, ins, work)


def late_side_body(flag_ref, frame_in, far_ref, rate_ref, side_in, east_ref, west_ref, main_ref, *rest):
    ins, (out_ref, frame_ref, wet_ref, *work) = rest[:4], rest[4:]
    frame_ref[...] = side_in[...]
    unpack_strips(LATE, frame_in, east_ref, west_ref, frame_ref)
    unpack_wet(LATE, frame_in, east_ref, west_ref, frame_ref, WET_AT, [PLACE_FAR[-r] for r in range(9)])
    for k in (TEMP, SALT):
        copy_block(frame_ref, block_at(k, PLACE_NEAR[16]), far_ref, k * LEV, edges)
        copy_block(frame_ref, block_at(k, PLACE_FAR[-9]), frame_in, block_at(k, PLACE_FAR[-9]), edges)
    wet_ref[...] = frame_ref[WET_AT : WET_AT + 32, :]
    for place, row in (
        (PLACE_NEAR[16], spread(far_ref, 2 * LEV)),
        (PLACE_FAR[-9], spread(frame_in, WET_AT + PLACE_FAR[-9])),
    ):
        wet_ref[place : place + 1, :] = edges(row)[0:1, :]
    lanes = lanes_of()
    odd = flag_ref[0] == 1
    order = jnp.where(odd, 7 - rows_of(), rows_of())
    sign = jnp.where(odd, -1.0, 1.0)

    def emit(k, l, x):
        out = jnp.where(lanes < STRIP, pltpu.roll(x, 96, axis=1), main_ref[k, l])
        out = jnp.where(lanes >= 128 - STRIP, pltpu.roll(x, 32, axis=1), out)
        out = jnp.take_along_axis(out, order, axis=0)
        out_ref[k, l] = out * sign if k == NORTH else out

    late(frame_ref, wet_ref, rate_ref, emit, ins, work)


def local(state, mixing, wet_levels):
    lons, lats = lax.axis_size("lon"), lax.axis_size("lat")
    lat = lax.axis_index("lat")
    odd = lax.rem(lat, 2)
    flags = jnp.stack([odd, (lat == lats - 1).astype(jnp.int32)]).astype(jnp.int32)
    rows = jnp.array([PLACE_ROW.get(p, 0) for p in range(32)], jnp.int32)
    grid_rows = lat * 8 + jnp.where(odd == 1, 7 - rows, rows)
    grid_rows = jnp.where(grid_rows > lats * 8 - 1, 2 * (lats * 8 - 1) - grid_rows, grid_rows).astype(jnp.float32)
    rate = CORIOLIS * jnp.sin(math.pi * (grid_rows + 0.5) / (lats * 8) - 0.9)
    rate = jnp.broadcast_to(jnp.where(odd == 1, -rate, rate)[:, None], (32, 128))

    def at(o, a):
        return o * lats + a

    pairs = [(at(o, a), at(o, a ^ 1)) for o in range(lons) for a in range(lats)]
    cross = [(at(o, a), at(o, a + 1 if a % 2 else a - 1)) for o in range(lons) for a in range(1, lats - 1)]
    fold_a = [(at(o, lats - 1), at((lons - o) % lons, lats - 1)) for o in range(lons)]
    fold_b = [(at(o, lats - 1), at(lons - 1 - o, lats - 1)) for o in range(lons)]
    both = ("lon", "lat")

    half = (HALF, 128)
    x, a, b = call(own_body, [(OWN, 128), half, half], [SM] + [VM] * 3, 10**6, [(2 * HALF, 128)])(
        flags, state.reshape(4 * LEV * 8, 128), mixing.reshape(LEV * 8, 128), wet_levels
    )
    a = lax.ppermute(a, both, cross + fold_a)
    y = lax.ppermute(x, both, pairs)
    to_east_pairs = [(i, (i + 1) % lons) for i in range(lons)]
    to_west_pairs = [((i + 1) % lons, i) for i in range(lons)]
    b, c, early_frame, to_east, to_west = call(
        early_frame_body,
        [(HALF + MORE, 128), (MORE, 128), (FRAME, 128), EARLY.shape, EARLY.shape],
        [SM, VM, VM, VM],
        10**6,
        [(2 * MORE, 128)],
    )(flags, x, y, b)
    from_west = lax.ppermute(to_east, "lon", to_east_pairs)
    from_east = lax.ppermute(to_west, "lon", to_west_pairs)
    b = lax.ppermute(b, both, cross + fold_b)
    c = lax.ppermute(c, both, fold_a)
    wet = (32, 128)
    main_early = call(early_main_body, HANDED_SHAPES, [SM, VM, VM], 10**9, [wet] + WORK)(flags, early_frame, rate)
    side_frame, *side_early = call(
        early_side_body, [(FRAME, 128)] + HANDED_SHAPES, [SM] + [VM] * 4, 10**11, [wet] + WORK
    )(flags, early_frame, rate, from_west, from_east)
    frame, far, to_east, to_west = call(
        frame_body,
        [(FRAME, 128), (FAR, 128), LATE.shape, LATE.shape],
        [SM] + [VM] * 4 + [pl.BlockSpec(memory_space=pl.ANY)] * 2,
        10**6,
        [(2 * HALF, 128), (2 * MORE, 128)],
    )(flags, early_frame, a, b, c, main_early[0], side_early[0])
    far = lax.ppermute(far, both, pairs)
    from_west = lax.ppermute(to_east, "lon", to_east_pairs)
    from_east = lax.ppermute(to_west, "lon", to_west_pairs)
    work = [(FRAME, 128), wet] + WORK
    (middle,) = call(late_main_body, [state.shape], [SM] + [VM] * 7, 10**9, work)(flags, frame, far, rate, *main_early)
    (out,) = call(late_side_body, [state.shape], [SM] + [VM] * 11, 10**9, work)(
        flags, frame, far, rate, side_frame, from_west, from_east, middle, *side_early
    )
    return out


def solution(mesh):
    return jax.shard_map(
        local,
        mesh=mesh,
        in_specs=(P(None, None, "lat", "lon"), P(None, "lat", "lon"), P("lat", "lon")),
        out_specs=P(None, None, "lat", "lon"),
        check_vma=False,
    )
```

time: 119 us -> 110 us (0.924)
  waiting for transfers between devices: 15.9 us -> 5.2 us
  Pallas kernels: 42.9 us -> 51.5 us
  starting transfers between devices: 56.6 us -> 49 us
    ppermute x4 -> x5, starting transfers between devices: 34.5 us -> 20.4 us  [the longest x2 14.5 us: local(): from_east = lax.ppermute(to_west, 'lon', to_west_pairs)]
    ppermute x1, waiting for transfers between devices: 11.5 us -> 2.41 us  [local(): b = lax.ppermute(b, both, cross + fold_b)]
    pallas_call x4 -> x6, Pallas kernels: 42.1 us -> 50.7 us  [the longest x1 15.7 us: local(): call(late_side_body, [state.shape], [SM] + [VM] * 11, 10 ** 9, work)]
    ppermute x1, starting transfers between devices: 6.9 us -> 13.4 us  [local(): far = lax.ppermute(far, both, pairs)]
    ppermute x4 -> x5, waiting for transfers between devices: 4.45 us -> 2.78 us  [the longest x2 2.77 us: local(): from_east = lax.ppermute(to_west, 'lon', to_west_pairs)]
    unnamed x8 -> x10, local copies, waits for them, and re-layouts: 2.69 us -> 2.7 us
  transfers between devices with their start and end apart: 8 -> 9, of which waited for: 2 -> 2; matrix products, arithmetic and copies ran while one was open for 0% -> 0% of each run, Pallas kernels for 15% -> 31%
where the time goes in v3:
time: 110 us; the launch traced here: 109 us
  Pallas kernels  51.5 us (47%)
  starting transfers between devices  49 us (45%)
  waiting for transfers between devices  5.2 us (5%)
  local copies, waits for them, and re-layouts  2.77 us (3%)
    pallas_call x1, Pallas kernels, local(): call(late_side_body, [state.shape], [SM] + [VM] * 11, 10 ** 9, work)  15.7 us
    ppermute x2, starting transfers between devices, local(): from_east = lax.ppermute(to_west, 'lon', to_west_pairs)  14.5 us
    ppermute x1, starting transfers between devices, local(): far = lax.ppermute(far, both, pairs)  13.4 us
    pallas_call x1, Pallas kernels, local(): call(late_main_body, [state.shape], [SM] + [VM] * 7, 10 ** 9, work)  12.7 us
    ppermute x1, starting transfers between devices, local(): a = lax.ppermute(a, both, cross + fold_a)  11.3 us
    pallas_call x1, Pallas kernels, local(): call(early_side_body, [(FRAME, 128)] + HANDED_SHAPES, [SM] + [VM] * 4, 10...  10.4 us
    pallas_call x1, Pallas kernels, local(): call(early_main_body, HANDED_SHAPES, [SM, VM, VM], 10 ** 9, [wet] + WORK)  8.18 us
    ppermute x2, starting transfers between devices, local(): from_west = lax.ppermute(to_east, 'lon', to_east_pairs)  5.3 us
  transfers between devices with their start and end apart: 9, of which 2 were waited for; matrix products, arithmetic and copies ran while one was open for 0% of the time, Pallas kernels for 31%

profile of v3, /device:TPU:6, one launch (start us, length us, event | category | flops | bytes accessed | tf_op | source)
XLA Modules:
  0.0 108.8 jit_solution(774003934828856647)
XLA Ops:
  0.0 0.0 copy-start.3
  0.0 0.0 copy-start.4
  0.0 0.1 pad_add_fusion.flag_ref
  0.1 0.0 copy-start
  0.1 1.1 copy-done
  1.2 0.0 copy-start.1
  1.2 0.9 copy-done.1
  2.1 0.0 copy-start.2
  2.1 0.7 copy-done.2
  2.8 0.9 shard_map.46
  3.6 1.9 %collective-permute-start = (f32[1608,128]{1,0:T(8,128)S(1)}, f32[1608,128]{1,0:T(8,128)S(1)}, u32[]{:S(2)}, u32[]{:S(2)}) collective-permute-start(f32[1608,128]{1,0:T(8,128)S(1)} %get-tuple-element.26.x_ref), channel_id=1, source_target_pairs={{0,1},{1,0},{2,3},{3,2},{4,5},{5,4},{6,7},{7,6},{8,9},{9,8},{10,11... | collective-permute-start | bytes 2469896 | tf_op jit(solution)/shard_map/ppermute | solution.py:797
  5.6 11.3 %collective-permute-start.1 = (f32[744,128]{1,0:T(8,128)S(1)}, f32[744,128]{1,0:T(8,128)S(1)}, u32[]{:S(2)}, u32[]{:S(2)}) collective-permute-start(f32[744,128]{1,0:T(8,128)S(1)} %get-tuple-element.29), channel_id=1, source_target_pairs={{1,2},{2,1},{3,4},{4,3},{5,6},{6,5},{7,8},{8,7},{9,10},{10,9},{11,... | collective-permute-start | bytes 1142792 | tf_op jit(solution)/shard_map/ppermute | solution.py:796
  16.9 0.0 collective-permute-done.y_ref
  16.9 2.0 %shard_map.47 = (f32[888,128]{1,0:T(8,128)S(1)}, f32[144,128]{1,0:T(8,128)S(1)}, f32[5432,128]{1,0:T(8,128)S(1)}, f32[272,128]{1,0:T(8,128)S(1)}, f32[272,128]{1,0:T(8,128)S(1)}) custom-call(s32[2]{0:T(128)S(1)} %pad_add_fusion.flag_ref, f32[1608,128]{1,0:T(8,128)S(1)} %get-tuple-element.26.x_ref, f32[1608,128]{1,0:T(8,128)S(1)} %collective-permute-done.y_ref, ...), custom_call_target="tpu_custom_call" | custom-call | flops 1000000 | bytes 4194304 | tf_op jit(solution)/shard_map/pallas_call | solution.py:800
  18.8 3.4 %collective-permute-start.4 = (f32[272,128]{1,0:T(8,128)S(1)}, f32[272,128]{1,0:T(8,128)S(1)}, u32[]{:S(2)}, u32[]{:S(2)}) collective-permute-start(f32[272,128]{1,0:T(8,128)S(1)} %get-tuple-element.33), channel_id=1, source_target_pairs={{0,16},{16,32},{32,48},{48,64},{64,80},{80,96},{96,112},{112,128},... | collective-permute-start | bytes 417800 | tf_op jit(solution)/shard_map/ppermute | solution.py:807
  22.2 6.6 %collective-permute-start.5 = (f32[272,128]{1,0:T(8,128)S(1)}, f32[272,128]{1,0:T(8,128)S(1)}, u32[]{:S(2)}, u32[]{:S(2)}) collective-permute-start(f32[272,128]{1,0:T(8,128)S(1)} %get-tuple-element.34), channel_id=1, source_target_pairs={{16,0},{32,16},{48,32},{64,48},{80,64},{96,80},{112,96},{128,112},... | collective-permute-start | bytes 417800 | tf_op jit(solution)/shard_map/ppermute | solution.py:808
  28.9 0.0 copy-done.3
  28.9 0.0 copy-done.4
  28.9 0.1 broadcast_select_fusion
  28.9 0.7 collective-permute-start.3
  29.6 1.9 %collective-permute-start.2 = (f32[888,128]{1,0:T(8,128)S(1)}, f32[888,128]{1,0:T(8,128)S(1)}, u32[]{:S(2)}, u32[]{:S(2)}) collective-permute-start(f32[888,128]{1,0:T(8,128)S(1)} %get-tuple-element.30), channel_id=1, source_target_pairs={{1,2},{2,1},{3,4},{4,3},{5,6},{6,5},{7,8},{8,7},{9,10},{10,9},{11,... | collective-permute-start | bytes 1363976 | tf_op jit(solution)/shard_map/ppermute | solution.py:809
  31.5 0.1 broadcast_in_dim.2.rate_ref
  31.6 8.2 %shard_map.48 = (f32[448,128]{1,0:T(8,128)S(1)}, f32[1600,128]{1,0:T(8,128)S(1)}, f32[448,128]{1,0:T(8,128)S(1)}, f32[640,128]{1,0:T(8,128)S(1)}) custom-call(s32[2]{0:T(128)S(1)} %pad_add_fusion.flag_ref, f32[5432,128]{1,0:T(8,128)S(1)} %get-tuple-element.28.frame_ref.early_ref, f32[32,128]{1,0:T(8,128)S(1)} %broadcast_in_dim.2.rate_ref), custom_call_target="tpu_custom_call" | custom-call | flops 1000000000 | bytes 4194304 | tf_op jit(solution)/shard_map/pallas_call | solution.py:812
  39.8 0.0 collective-permute-done.4.east_ref
  39.8 2.8 %collective-permute-done.5.west_ref = f32[272,128]{1,0:T(8,128)S(1)} collective-permute-done((f32[272,128]{1,0:T(8,128)S(1)}, f32[272,128]{1,0:T(8,128)S(1)}, u32[]{:S(2)}, u32[]{:S(2)}) %collective-permute-start.5) | collective-permute-done | bytes 139296 | tf_op jit(solution)/shard_map/ppermute | solution.py:808
  42.6 10.4 %shard_map.49 = (f32[5432,128]{1,0:T(8,128)S(1)}, f32[448,128]{1,0:T(8,128)S(1)}, f32[1600,128]{1,0:T(8,128)S(1)}, f32[448,128]{1,0:T(8,128)S(1)}, f32[640,128]{1,0:T(8,128)S(1)}) custom-call(s32[2]{0:T(128)S(1)} %pad_add_fusion.flag_ref, f32[5432,128]{1,0:T(8,128)S(1)} %get-tuple-element.28.frame_ref.early_ref, f32[32,128]{1,0:T(8,128)S(1)} %broadcast_in_dim.2.rate_ref, ...), custom_call_target="tpu_custom_call" | custom-call | flops 99999997952 | bytes 4194304 | tf_op jit(solution)/shard_map/pallas_call | solution.py:813
  53.0 0.0 collective-permute-done.1.a_ref
  53.0 0.0 collective-permute-done.3.c_ref
  53.1 2.4 %collective-permute-done.2.b_ref = f32[888,128]{1,0:T(8,128)S(1)} collective-permute-done((f32[888,128]{1,0:T(8,128)S(1)}, f32[888,128]{1,0:T(8,128)S(1)}, u32[]{:S(2)}, u32[]{:S(2)}) %collective-permute-start.2) | collective-permute-done | bytes 454688 | tf_op jit(solution)/shard_map/ppermute | solution.py:809
  55.5 1.7 %shard_map.50 = (f32[5432,128]{1,0:T(8,128)S(1)}, f32[88,128]{1,0:T(8,128)S(1)}, f32[152,128]{1,0:T(8,128)S(1)}, f32[152,128]{1,0:T(8,128)S(1)}) custom-call(s32[2]{0:T(128)S(1)} %pad_add_fusion.flag_ref, f32[5432,128]{1,0:T(8,128)S(1)} %get-tuple-element.28.frame_ref.early_ref, f32[744,128]{1,0:T(8,128)S(1)} %collective-permute-done.1.a_ref, ...), custom_call_target="tpu_custom_call" | custom-call | flops 1000000 | bytes 4194304 | tf_op jit(solution)/shard_map/pallas_call | solution.py:816
  57.1 13.4 %collective-permute-start.6 = (f32[88,128]{1,0:T(8,128)S(1)}, f32[88,128]{1,0:T(8,128)S(1)}, u32[]{:S(2)}, u32[]{:S(2)}) collective-permute-start(f32[88,128]{1,0:T(8,128)S(1)} %get-tuple-element.37), channel_id=1, source_target_pairs={{0,1},{1,0},{2,3},{3,2},{4,5},{5,4},{6,7},{7,6},{8,9},{9,8},{10,11... | collective-permute-start | bytes 135176 | tf_op jit(solution)/shard_map/ppermute | solution.py:823
  70.6 1.9 %collective-permute-start.7 = (f32[152,128]{1,0:T(8,128)S(1)}, f32[152,128]{1,0:T(8,128)S(1)}, u32[]{:S(2)}, u32[]{:S(2)}) collective-permute-start(f32[152,128]{1,0:T(8,128)S(1)} %get-tuple-element.39), channel_id=1, source_target_pairs={{0,16},{16,32},{32,48},{48,64},{64,80},{80,96},{96,112},{112,128},... | collective-permute-start | bytes 233480 | tf_op jit(solution)/shard_map/ppermute | solution.py:824
  72.5 7.8 %collective-permute-start.8 = (f32[152,128]{1,0:T(8,128)S(1)}, f32[152,128]{1,0:T(8,128)S(1)}, u32[]{:S(2)}, u32[]{:S(2)}) collective-permute-start(f32[152,128]{1,0:T(8,128)S(1)} %get-tuple-element.40), channel_id=1, source_target_pairs={{16,0},{32,16},{48,32},{64,48},{80,64},{96,80},{112,96},{128,112},... | collective-permute-start | bytes 233480 | tf_op jit(solution)/shard_map/ppermute | solution.py:825
  80.3 0.0 collective-permute-done.6.far_ref
  80.3 12.7 %shard_map.51.main_ref = f32[4,40,8,128]{3,2,1,0:T(8,128)S(1)} custom-call(s32[2]{0:T(128)S(1)} %pad_add_fusion.flag_ref, f32[5432,128]{1,0:T(8,128)S(1)} %get-tuple-element.36.frame_in, f32[88,128]{1,0:T(8,128)S(1)} %collective-permute-done.6.far_ref, f32[32,128]{1,0:T(8,128)S(1)} %broadcast_in_dim.2.rate_ref, ...), custom_call_target="tpu_custom_call" | custom-call | flops 1000000000 | bytes 4194304 | tf_op jit(solution)/shard_map/pallas_call | solution.py:827
  93.1 0.0 collective-permute-done.7.east_ref
  93.1 0.0 collective-permute-done.8.west_ref
  93.1 15.7 %shard_map.52 = f32[4,40,8,128]{3,2,1,0:T(8,128)} custom-call(s32[2]{0:T(128)S(1)} %pad_add_fusion.flag_ref, f32[5432,128]{1,0:T(8,128)S(1)} %get-tuple-element.36.frame_in, f32[88,128]{1,0:T(8,128)S(1)} %collective-permute-done.6.far_ref, f32[32,128]{1,0:T(8,128)S(1)} %broadcast_in_dim.2.rate_ref, f32[5432,128]{1,0:T(8,128)S(1)} %get-tuple-element.38.side_in, ...), custom_call_target="tpu_custom_call" | custom-call | flops 1000000000 | bytes 4194304 | tf_op jit(solution)/shard_map/pallas_call | solution.py:828
Async XLA Ops:
  0.0 28.9 %copy-start.3 = (s32[32]{0:T(128)S(1)}, s32[32]{0:T(128)}, u32[]{:S(2)}) copy-start(s32[32]{0:T(128)} %constant.39) | copy-start | bytes 388
  0.0 28.9 %copy-start.4 = (s32[32]{0:T(128)S(1)}, s32[32]{0:T(128)}, u32[]{:S(2)}) copy-start(s32[32]{0:T(128)} %constant.34.clone) | copy-start | bytes 388
  0.1 1.1 copy-start
  1.2 0.9 copy-start.1
  2.1 0.7 copy-start.2
  3.6 13.2 %collective-permute-start = (f32[1608,128]{1,0:T(8,128)S(1)}, f32[1608,128]{1,0:T(8,128)S(1)}, u32[]{:S(2)}, u32[]{:S(2)}) collective-permute-start(f32[1608,128]{1,0:T(8,128)S(1)} %get-tuple-element.26.x_ref), channel_id=1, source_target_pairs={{0,1},{1,0},{2,3},{3,2},{4,5},{5,4},{6,7},{7,6},{8,9},{9,8},{10,11... | collective-permute-start | bytes 2469896 | tf_op jit(solution)/shard_map/ppermute | solution.py:797
  5.6 47.5 %collective-permute-start.1 = (f32[744,128]{1,0:T(8,128)S(1)}, f32[744,128]{1,0:T(8,128)S(1)}, u32[]{:S(2)}, u32[]{:S(2)}) collective-permute-start(f32[744,128]{1,0:T(8,128)S(1)} %get-tuple-element.29), channel_id=1, source_target_pairs={{1,2},{2,1},{3,4},{4,3},{5,6},{6,5},{7,8},{8,7},{9,10},{10,9},{11,... | collective-permute-start | bytes 1142792 | tf_op jit(solution)/shard_map/ppermute | solution.py:796
  18.8 21.0 %collective-permute-start.4 = (f32[272,128]{1,0:T(8,128)S(1)}, f32[272,128]{1,0:T(8,128)S(1)}, u32[]{:S(2)}, u32[]{:S(2)}) collective-permute-start(f32[272,128]{1,0:T(8,128)S(1)} %get-tuple-element.33), channel_id=1, source_target_pairs={{0,16},{16,32},{32,48},{48,64},{64,80},{80,96},{96,112},{112,128},... | collective-permute-start | bytes 417800 | tf_op jit(solution)/shard_map/ppermute | solution.py:807
  22.2 20.4 %collective-permute-start.5 = (f32[272,128]{1,0:T(8,128)S(1)}, f32[272,128]{1,0:T(8,128)S(1)}, u32[]{:S(2)}, u32[]{:S(2)}) collective-permute-start(f32[272,128]{1,0:T(8,128)S(1)} %get-tuple-element.34), channel_id=1, source_target_pairs={{16,0},{32,16},{48,32},{64,48},{80,64},{96,80},{112,96},{128,112},... | collective-permute-start | bytes 417800 | tf_op jit(solution)/shard_map/ppermute | solution.py:808
  28.9 24.1 %collective-permute-start.3 = (f32[144,128]{1,0:T(8,128)S(1)}, f32[144,128]{1,0:T(8,128)S(1)}, u32[]{:S(2)}, u32[]{:S(2)}) collective-permute-start(f32[144,128]{1,0:T(8,128)S(1)} %get-tuple-element.31), channel_id=1, source_target_pairs={{15,15},{31,511},{47,495},{63,479},{79,463},{95,447},{111,431},{12... | collective-permute-start | bytes 221192 | tf_op jit(solution)/shard_map/ppermute | solution.py:810
  29.6 25.8 %collective-permute-start.2 = (f32[888,128]{1,0:T(8,128)S(1)}, f32[888,128]{1,0:T(8,128)S(1)}, u32[]{:S(2)}, u32[]{:S(2)}) collective-permute-start(f32[888,128]{1,0:T(8,128)S(1)} %get-tuple-element.30), channel_id=1, source_target_pairs={{1,2},{2,1},{3,4},{4,3},{5,6},{6,5},{7,8},{8,7},{9,10},{10,9},{11,... | collective-permute-start | bytes 1363976 | tf_op jit(solution)/shard_map/ppermute | solution.py:809
  57.1 23.2 %collective-permute-start.6 = (f32[88,128]{1,0:T(8,128)S(1)}, f32[88,128]{1,0:T(8,128)S(1)}, u32[]{:S(2)}, u32[]{:S(2)}) collective-permute-start(f32[88,128]{1,0:T(8,128)S(1)} %get-tuple-element.37), channel_id=1, source_target_pairs={{0,1},{1,0},{2,3},{3,2},{4,5},{5,4},{6,7},{7,6},{8,9},{9,8},{10,11... | collective-permute-start | bytes 135176 | tf_op jit(solution)/shard_map/ppermute | solution.py:823
  70.6 22.5 %collective-permute-start.7 = (f32[152,128]{1,0:T(8,128)S(1)}, f32[152,128]{1,0:T(8,128)S(1)}, u32[]{:S(2)}, u32[]{:S(2)}) collective-permute-start(f32[152,128]{1,0:T(8,128)S(1)} %get-tuple-element.39), channel_id=1, source_target_pairs={{0,16},{16,32},{32,48},{48,64},{64,80},{80,96},{96,112},{112,128},... | collective-permute-start | bytes 233480 | tf_op jit(solution)/shard_map/ppermute | solution.py:824
  72.5 20.6 %collective-permute-start.8 = (f32[152,128]{1,0:T(8,128)S(1)}, f32[152,128]{1,0:T(8,128)S(1)}, u32[]{:S(2)}, u32[]{:S(2)}) collective-permute-start(f32[152,128]{1,0:T(8,128)S(1)} %get-tuple-element.40), channel_id=1, source_target_pairs={{16,0},{32,16},{48,32},{64,48},{80,64},{96,80},{112,96},{128,112},... | collective-permute-start | bytes 233480 | tf_op jit(solution)/shard_map/ppermute | solution.py:825

commit v4 on v3

--- a/solution.py
+++ b/solution.py
@@ -72,7 +72,7 @@
 VM = pl.BlockSpec(memory_space=pltpu.VMEM)
 SM = pl.BlockSpec(memory_space=pltpu.SMEM)
 LIMIT = 32 * 1024 * 1024
-UNROLL = {"column": 4}
+UNROLL = {"column": 8}
 
 
 def call(body, outs, ins, flops, scratch=()):
@@ -81,7 +81,7 @@
         out_shape=tuple(jax.ShapeDtypeStruct(s, jnp.float32) for s in outs),
         in_specs=ins,
         out_specs=tuple(VM for _ in outs),
-        scratch_shapes=[pltpu.VMEM(s, jnp.float32) for s in scratch],
+        scratch_shapes=[pltpu.VMEM(s, jnp.float32) if isinstance(s, tuple) else s for s in scratch],
         compiler_params=pltpu.CompilerParams(vmem_limit_bytes=LIMIT),
         cost_estimate=pl.CostEstimate(flops=flops, bytes_accessed=4 * 1024 * 1024, transcendentals=0),
     )
@@ -141,7 +141,15 @@
     lax.fori_loop(0, rows // 8, one, 0, unroll=8)
 
 
-def own_body(flag_ref, state_ref, mixing_ref, wet_ref, x_ref, a_ref, b_ref, full_ref):
+def own_body(
+    flag_ref, state_in, mixing_in, wet_in, x_ref, a_ref, b_ref, full_ref, state_ref, mixing_ref, wet_ref, arrived
+):
+    pairs = ((wet_in, wet_ref), (mixing_in, mixing_ref), (state_in, state_ref))
+    copies = [pltpu.make_async_copy(source, out, arrived.at[n]) for n, (source, out) in enumerate(pairs)]
+    for copy in copies:
+        copy.start()
+    for copy in copies:
+        copy.wait()
     levels = rows_of().astype(jnp.float32)
     odd = flag_ref[0] == 1
     fold = flag_ref[1] == 1
@@ -252,7 +260,6 @@
         full_ref[MORE_WET : MORE_WET + 8, :] = mirror(wet)
         split_halves(full_ref, c_ref, b_ref.at[HALF : HALF + MORE], MORE)
 
-    frame_ref[...] = jnp.zeros((FRAME, 128), jnp.float32)
     for k in range(5):
         copy_blocks(frame_ref, block_at(k, PLACE_NEAR[0]), x_ref, k * 8 * LEV, 8)
         for r in range(8, 16):
@@ -349,7 +356,7 @@
 
 
 def march(
-    part, frame_ref, wet_ref, rate_ref, after, emit, f_ref, rhs_ref, adv_ref, adv_e_ref, p_ref, coef_ref, wet_e_ref
+    part, frame_ref, wet_ref, rate_ref, after, emit, f_ref, rhs_ref, adv_ref, adv_e_ref, p_ref, coef_ref, wet_e_ref, far_ref=None
 ):
     levels = rows_of().astype(jnp.float32)
     zero = jnp.zeros((8, 128), jnp.float32)
@@ -395,6 +402,8 @@
             return cache[key]
 
         def field(k, place):
+            if step == 0 and far_ref is not None and place == PLACE_NEAR[16] and k in (TEMP, SALT):
+                return once((k, place), lambda: far_ref[pl.ds(first + k * LEV, 8), :])
             ref = frame_ref if step == 0 else f_ref
             return once((k, place), lambda: ref[pl.ds(first + block_at(k, place), 8), :])
 
@@ -649,7 +658,7 @@
     march("early", frame_ref, wet_ref, rate_ref, after, None, *work)
 
 
-def late(frame_ref, wet_ref, rate_ref, emit, ins, work):
+def late(frame_ref, wet_ref, rate_ref, emit, ins, work, far_ref=None):
     f_ref, _, adv_ref, adv_e_ref = work[:4]
 
     def after(step, what):
@@ -670,7 +679,7 @@
             for k in range(4):
                 copy_blocks(f_ref, block_at(k, PLACE_NEAR[rows[0]]), new_in, k * len(rows) * LEV, len(rows))
 
-    march("late", frame_ref, wet_ref, rate_ref, after, emit, *work)
+    march("late", frame_ref, wet_ref, rate_ref, after, emit, *work, far_ref=far_ref)
 
 
 def early_main_body(flag_ref, frame_ref, rate_ref, *rest):
@@ -727,18 +736,15 @@
     early(side_ref, wet_ref, rate_ref, outs, work)
 
 
-def late_main_body(flag_ref, frame_in, far_ref, rate_ref, *rest):
-    ins, (out_ref, frame_ref, wet_ref, *work) = rest[:4], rest[4:]
-    frame_ref[...] = frame_in[...]
-    for k in (TEMP, SALT):
-        copy_blocks(frame_ref, block_at(k, PLACE_NEAR[16]), far_ref, k * LEV, 1)
-    wet_row(frame_ref, PLACE_NEAR[16], far_ref, 2 * LEV)
+def late_main_body(flag_ref, frame_ref, far_ref, rate_ref, *rest):
+    ins, (out_ref, wet_ref, *work) = rest[:4], rest[4:]
     wet_ref[...] = frame_ref[WET_AT : WET_AT + 32, :]
+    wet_ref[PLACE_NEAR[16] : PLACE_NEAR[16] + 1, :] = far_ref[2 * LEV : 2 * LEV + 1, :]
 
     def emit(k, l, x):
         out_ref[k, l] = x
 
-    late(frame_ref, wet_ref, rate_ref, emit, ins, work)
+    late(frame_ref, wet_ref, rate_ref, emit, ins, work, far_ref)
 
 
 def late_side_body(flag_ref, frame_in, far_ref, rate_ref, side_in, east_ref, west_ref, main_ref, *rest):
@@ -790,7 +796,19 @@
     both = ("lon", "lat")
 
     half = (HALF, 128)
-    x, a, b = call(own_body, [(OWN, 128), half, half], [SM] + [VM] * 3, 10**6, [(2 * HALF, 128)])(
+    x, a, b = call(
+        own_body,
+        [(OWN, 128), half, half],
+        [SM] + [pl.BlockSpec(memory_space=pltpu.HBM)] * 3,
+        10**6,
+        [
+            (2 * HALF, 128),
+            (4 * LEV * 8, 128),
+            (LEV * 8, 128),
+            pltpu.VMEM(wet_levels.shape, wet_levels.dtype),
+            pltpu.SemaphoreType.DMA((3,)),
+        ],
+    )(
         flags, state.reshape(4 * LEV * 8, 128), mixing.reshape(LEV * 8, 128), wet_levels
     )
     a = lax.ppermute(a, both, cross + fold_a)
@@ -824,7 +842,7 @@
     from_west = lax.ppermute(to_east, "lon", to_east_pairs)
     from_east = lax.ppermute(to_west, "lon", to_west_pairs)
     work = [(FRAME, 128), wet] + WORK
-    (middle,) = call(late_main_body, [state.shape], [SM] + [VM] * 7, 10**9, work)(flags, frame, far, rate, *main_early)
+    (middle,) = call(late_main_body, [state.shape], [SM] + [VM] * 7, 10**9, [wet] + WORK)(flags, frame, far, rate, *main_early)
     (out,) = call(late_side_body, [state.shape], [SM] + [VM] * 11, 10**9, work)(
         flags, frame, far, rate, side_frame, from_west, from_east, middle, *side_early
     )

time: 110 us -> 109 us (level)
  transfers between devices with their start and end apart: 9 -> 9, of which waited for: 2 -> 2; matrix products, arithmetic and copies ran while one was open for 0% -> 0% of each run, Pallas kernels for 31% -> 30%
where the time goes in v4:
time: 109 us; the launch traced here: 108 us
  Pallas kernels  50.5 us (46%)
  starting transfers between devices  49 us (45%)
  waiting for transfers between devices  5.58 us (5%)
  local copies, waits for them, and re-layouts  2.77 us (3%)
    pallas_call x1, Pallas kernels, local(): call(late_side_body, [state.shape], [SM] + [VM] * 11, 10 ** 9, work)  15.1 us
    ppermute x2, starting transfers between devices, local(): from_east = lax.ppermute(to_west, 'lon', to_west_pairs)  14.5 us
    ppermute x1, starting transfers between devices, local(): far = lax.ppermute(far, both, pairs)  13.4 us
    pallas_call x1, Pallas kernels, local(): call(late_main_body, [state.shape], [SM] + [VM] * 7, 10 ** 9, [wet] + WORK)  12.3 us
    ppermute x1, starting transfers between devices, local(): a = lax.ppermute(a, both, cross + fold_a)  11.3 us
    pallas_call x1, Pallas kernels, local(): call(early_side_body, [(FRAME, 128)] + HANDED_SHAPES, [SM] + [VM] * 4, 10...  10.3 us
    pallas_call x1, Pallas kernels, local(): call(early_main_body, HANDED_SHAPES, [SM, VM, VM], 10 ** 9, [wet] + WORK)  8.03 us
    ppermute x2, starting transfers between devices, local(): from_west = lax.ppermute(to_east, 'lon', to_east_pairs)  5.3 us
  transfers between devices with their start and end apart: 9, of which 2 were waited for; matrix products, arithmetic and copies ran while one was open for 0% of the time, Pallas kernels for 30%

profile of v4, /device:TPU:6, one launch (start us, length us, event | category | flops | bytes accessed | tf_op | source)
XLA Modules:
  0.0 108.2 jit_solution(17532777156036464848)
XLA Ops:
  0.0 0.0 copy-start.3
  0.0 0.0 copy-start.4
  0.0 0.1 pad_add_fusion.flag_ref
  0.1 0.0 copy-start
  0.1 1.1 %copy-done = f32[4,40,8,128]{3,2,1,0:T(8,128)S(1)} copy-done((f32[4,40,8,128]{3,2,1,0:T(8,128)S(1)}, f32[4,40,8,128]{3,2,1,0:T(8,128)}, u32[]{:S(2)}) %copy-start) | copy-done | bytes 655384
  1.2 0.0 copy-start.1
  1.2 0.9 copy-done.1
  2.1 0.0 copy-start.2
  2.1 0.7 copy-done.2
  2.8 1.3 %shard_map.46 = (f32[1608,128]{1,0:T(8,128)S(1)}, f32[744,128]{1,0:T(8,128)S(1)}, f32[744,128]{1,0:T(8,128)S(1)}) custom-call(s32[2]{0:T(128)S(1)} %pad_add_fusion.flag_ref, f32[1280,128]{1,0:T(8,128)S(1)} %bitcast.4, f32[320,128]{1,0:T(8,128)S(1)} %bitcast.5, s32[8,128]{1,0:T(8,128)S(1)} %copy-done.2), custom_call_target="tpu_custom_call" | custom-call | flops 1000000 | bytes 4194304 | tf_op jit(solution)/shard_map/pallas_call | solution.py:799
  4.1 1.9 %collective-permute-start = (f32[1608,128]{1,0:T(8,128)S(1)}, f32[1608,128]{1,0:T(8,128)S(1)}, u32[]{:S(2)}, u32[]{:S(2)}) collective-permute-start(f32[1608,128]{1,0:T(8,128)S(1)} %get-tuple-element.26.x_ref), channel_id=1, source_target_pairs={{0,1},{1,0},{2,3},{3,2},{4,5},{5,4},{6,7},{7,6},{8,9},{9,8},{10,11... | collective-permute-start | bytes 2469896 | tf_op jit(solution)/shard_map/ppermute | solution.py:815
  6.0 11.3 %collective-permute-start.1 = (f32[744,128]{1,0:T(8,128)S(1)}, f32[744,128]{1,0:T(8,128)S(1)}, u32[]{:S(2)}, u32[]{:S(2)}) collective-permute-start(f32[744,128]{1,0:T(8,128)S(1)} %get-tuple-element.29), channel_id=1, source_target_pairs={{1,2},{2,1},{3,4},{4,3},{5,6},{6,5},{7,8},{8,7},{9,10},{10,9},{11,... | collective-permute-start | bytes 1142792 | tf_op jit(solution)/shard_map/ppermute | solution.py:814
  17.3 0.0 collective-permute-done.y_ref
  17.3 1.9 %shard_map.47 = (f32[888,128]{1,0:T(8,128)S(1)}, f32[144,128]{1,0:T(8,128)S(1)}, f32[5432,128]{1,0:T(8,128)S(1)}, f32[272,128]{1,0:T(8,128)S(1)}, f32[272,128]{1,0:T(8,128)S(1)}) custom-call(s32[2]{0:T(128)S(1)} %pad_add_fusion.flag_ref, f32[1608,128]{1,0:T(8,128)S(1)} %get-tuple-element.26.x_ref, f32[1608,128]{1,0:T(8,128)S(1)} %collective-permute-done.y_ref, ...), custom_call_target="tpu_custom_call" | custom-call | flops 1000000 | bytes 4194304 | tf_op jit(solution)/shard_map/pallas_call | solution.py:818
  19.2 3.4 %collective-permute-start.4 = (f32[272,128]{1,0:T(8,128)S(1)}, f32[272,128]{1,0:T(8,128)S(1)}, u32[]{:S(2)}, u32[]{:S(2)}) collective-permute-start(f32[272,128]{1,0:T(8,128)S(1)} %get-tuple-element.33), channel_id=1, source_target_pairs={{0,16},{16,32},{32,48},{48,64},{64,80},{80,96},{96,112},{112,128},... | collective-permute-start | bytes 417800 | tf_op jit(solution)/shard_map/ppermute | solution.py:825
  22.6 6.6 %collective-permute-start.5 = (f32[272,128]{1,0:T(8,128)S(1)}, f32[272,128]{1,0:T(8,128)S(1)}, u32[]{:S(2)}, u32[]{:S(2)}) collective-permute-start(f32[272,128]{1,0:T(8,128)S(1)} %get-tuple-element.34), channel_id=1, source_target_pairs={{16,0},{32,16},{48,32},{64,48},{80,64},{96,80},{112,96},{128,112},... | collective-permute-start | bytes 417800 | tf_op jit(solution)/shard_map/ppermute | solution.py:826
  29.2 0.0 copy-done.3
  29.3 0.0 copy-done.4
  29.3 0.1 broadcast_select_fusion
  29.3 0.7 collective-permute-start.3
  30.0 1.9 %collective-permute-start.2 = (f32[888,128]{1,0:T(8,128)S(1)}, f32[888,128]{1,0:T(8,128)S(1)}, u32[]{:S(2)}, u32[]{:S(2)}) collective-permute-start(f32[888,128]{1,0:T(8,128)S(1)} %get-tuple-element.30), channel_id=1, source_target_pairs={{1,2},{2,1},{3,4},{4,3},{5,6},{6,5},{7,8},{8,7},{9,10},{10,9},{11,... | collective-permute-start | bytes 1363976 | tf_op jit(solution)/shard_map/ppermute | solution.py:827
  31.9 0.1 broadcast_in_dim.2.rate_ref
  32.0 8.0 %shard_map.48 = (f32[448,128]{1,0:T(8,128)S(1)}, f32[1600,128]{1,0:T(8,128)S(1)}, f32[448,128]{1,0:T(8,128)S(1)}, f32[640,128]{1,0:T(8,128)S(1)}) custom-call(s32[2]{0:T(128)S(1)} %pad_add_fusion.flag_ref, f32[5432,128]{1,0:T(8,128)S(1)} %get-tuple-element.28.frame_ref.early_ref, f32[32,128]{1,0:T(8,128)S(1)} %broadcast_in_dim.2.rate_ref), custom_call_target="tpu_custom_call" | custom-call | flops 1000000000 | bytes 4194304 | tf_op jit(solution)/shard_map/pallas_call | solution.py:830
  40.0 0.0 collective-permute-done.4.east_ref
  40.0 3.0 %collective-permute-done.5.west_ref = f32[272,128]{1,0:T(8,128)S(1)} collective-permute-done((f32[272,128]{1,0:T(8,128)S(1)}, f32[272,128]{1,0:T(8,128)S(1)}, u32[]{:S(2)}, u32[]{:S(2)}) %collective-permute-start.5) | collective-permute-done | bytes 139296 | tf_op jit(solution)/shard_map/ppermute | solution.py:826
  43.0 10.3 %shard_map.49 = (f32[5432,128]{1,0:T(8,128)S(1)}, f32[448,128]{1,0:T(8,128)S(1)}, f32[1600,128]{1,0:T(8,128)S(1)}, f32[448,128]{1,0:T(8,128)S(1)}, f32[640,128]{1,0:T(8,128)S(1)}) custom-call(s32[2]{0:T(128)S(1)} %pad_add_fusion.flag_ref, f32[5432,128]{1,0:T(8,128)S(1)} %get-tuple-element.28.frame_ref.early_ref, f32[32,128]{1,0:T(8,128)S(1)} %broadcast_in_dim.2.rate_ref, ...), custom_call_target="tpu_custom_call" | custom-call | flops 99999997952 | bytes 4194304 | tf_op jit(solution)/shard_map/pallas_call | solution.py:831
  53.3 0.0 collective-permute-done.1.a_ref
  53.3 0.0 collective-permute-done.3.c_ref
  53.3 2.6 %collective-permute-done.2.b_ref = f32[888,128]{1,0:T(8,128)S(1)} collective-permute-done((f32[888,128]{1,0:T(8,128)S(1)}, f32[888,128]{1,0:T(8,128)S(1)}, u32[]{:S(2)}, u32[]{:S(2)}) %collective-permute-start.2) | collective-permute-done | bytes 454688 | tf_op jit(solution)/shard_map/ppermute | solution.py:827
  55.9 1.7 %shard_map.50 = (f32[5432,128]{1,0:T(8,128)S(1)}, f32[88,128]{1,0:T(8,128)S(1)}, f32[152,128]{1,0:T(8,128)S(1)}, f32[152,128]{1,0:T(8,128)S(1)}) custom-call(s32[2]{0:T(128)S(1)} %pad_add_fusion.flag_ref, f32[5432,128]{1,0:T(8,128)S(1)} %get-tuple-element.28.frame_ref.early_ref, f32[744,128]{1,0:T(8,128)S(1)} %collective-permute-done.1.a_ref, ...), custom_call_target="tpu_custom_call" | custom-call | flops 1000000 | bytes 4194304 | tf_op jit(solution)/shard_map/pallas_call | solution.py:834
  57.6 13.4 %collective-permute-start.6 = (f32[88,128]{1,0:T(8,128)S(1)}, f32[88,128]{1,0:T(8,128)S(1)}, u32[]{:S(2)}, u32[]{:S(2)}) collective-permute-start(f32[88,128]{1,0:T(8,128)S(1)} %get-tuple-element.37), channel_id=1, source_target_pairs={{0,1},{1,0},{2,3},{3,2},{4,5},{5,4},{6,7},{7,6},{8,9},{9,8},{10,11... | collective-permute-start | bytes 135176 | tf_op jit(solution)/shard_map/ppermute | solution.py:841
  71.0 1.9 %collective-permute-start.7 = (f32[152,128]{1,0:T(8,128)S(1)}, f32[152,128]{1,0:T(8,128)S(1)}, u32[]{:S(2)}, u32[]{:S(2)}) collective-permute-start(f32[152,128]{1,0:T(8,128)S(1)} %get-tuple-element.39), channel_id=1, source_target_pairs={{0,16},{16,32},{32,48},{48,64},{64,80},{80,96},{96,112},{112,128},... | collective-permute-start | bytes 233480 | tf_op jit(solution)/shard_map/ppermute | solution.py:842
  72.9 7.8 %collective-permute-start.8 = (f32[152,128]{1,0:T(8,128)S(1)}, f32[152,128]{1,0:T(8,128)S(1)}, u32[]{:S(2)}, u32[]{:S(2)}) collective-permute-start(f32[152,128]{1,0:T(8,128)S(1)} %get-tuple-element.40), channel_id=1, source_target_pairs={{16,0},{32,16},{48,32},{64,48},{80,64},{96,80},{112,96},{128,112},... | collective-permute-start | bytes 233480 | tf_op jit(solution)/shard_map/ppermute | solution.py:843
  80.8 0.0 collective-permute-done.6.far_ref
  80.8 12.3 %shard_map.51.main_ref = f32[4,40,8,128]{3,2,1,0:T(8,128)S(1)} custom-call(s32[2]{0:T(128)S(1)} %pad_add_fusion.flag_ref, f32[5432,128]{1,0:T(8,128)S(1)} %get-tuple-element.36.frame_ref.frame_in, f32[88,128]{1,0:T(8,128)S(1)} %collective-permute-done.6.far_ref, f32[32,128]{1,0:T(8,128)S(1)} %broadcast_in_dim.2.rate_ref, ...), custom_call_target="tpu_custom_call" | custom-call | flops 1000000000 | bytes 4194304 | tf_op jit(solution)/shard_map/pallas_call | solution.py:845
  93.1 0.0 collective-permute-done.7.east_ref
  93.1 0.0 collective-permute-done.8.west_ref
  93.1 15.1 %shard_map.52 = f32[4,40,8,128]{3,2,1,0:T(8,128)} custom-call(s32[2]{0:T(128)S(1)} %pad_add_fusion.flag_ref, f32[5432,128]{1,0:T(8,128)S(1)} %get-tuple-element.36.frame_ref.frame_in, f32[88,128]{1,0:T(8,128)S(1)} %collective-permute-done.6.far_ref, f32[32,128]{1,0:T(8,128)S(1)} %broadcast_in_dim.2.rate_ref, f32[5432,128]{1,0:T(8,128)S(1)} %get-tuple-element.38.side_in, ...), custom_call_target="tpu_custom_call" | custom-call | flops 1000000000 | bytes 4194304 | tf_op jit(solution)/shard_map/pallas_call | solution.py:846
Async XLA Ops:
  0.0 29.2 %copy-start.3 = (s32[32]{0:T(128)S(1)}, s32[32]{0:T(128)}, u32[]{:S(2)}) copy-start(s32[32]{0:T(128)} %constant.39) | copy-start | bytes 388
  0.0 29.3 %copy-start.4 = (s32[32]{0:T(128)S(1)}, s32[32]{0:T(128)}, u32[]{:S(2)}) copy-start(s32[32]{0:T(128)} %constant.34.clone) | copy-start | bytes 388
  0.1 1.1 %copy-start = (f32[4,40,8,128]{3,2,1,0:T(8,128)S(1)}, f32[4,40,8,128]{3,2,1,0:T(8,128)}, u32[]{:S(2)}) copy-start(f32[4,40,8,128]{3,2,1,0:T(8,128)} %param.4) | copy-start | bytes 1966084
  1.2 0.9 copy-start.1
  2.1 0.7 copy-start.2
  4.1 13.2 %collective-permute-start = (f32[1608,128]{1,0:T(8,128)S(1)}, f32[1608,128]{1,0:T(8,128)S(1)}, u32[]{:S(2)}, u32[]{:S(2)}) collective-permute-start(f32[1608,128]{1,0:T(8,128)S(1)} %get-tuple-element.26.x_ref), channel_id=1, source_target_pairs={{0,1},{1,0},{2,3},{3,2},{4,5},{5,4},{6,7},{7,6},{8,9},{9,8},{10,11... | collective-permute-start | bytes 2469896 | tf_op jit(solution)/shard_map/ppermute | solution.py:815
  6.0 47.3 %collective-permute-start.1 = (f32[744,128]{1,0:T(8,128)S(1)}, f32[744,128]{1,0:T(8,128)S(1)}, u32[]{:S(2)}, u32[]{:S(2)}) collective-permute-start(f32[744,128]{1,0:T(8,128)S(1)} %get-tuple-element.29), channel_id=1, source_target_pairs={{1,2},{2,1},{3,4},{4,3},{5,6},{6,5},{7,8},{8,7},{9,10},{10,9},{11,... | collective-permute-start | bytes 1142792 | tf_op jit(solution)/shard_map/ppermute | solution.py:814
  19.2 20.8 %collective-permute-start.4 = (f32[272,128]{1,0:T(8,128)S(1)}, f32[272,128]{1,0:T(8,128)S(1)}, u32[]{:S(2)}, u32[]{:S(2)}) collective-permute-start(f32[272,128]{1,0:T(8,128)S(1)} %get-tuple-element.33), channel_id=1, source_target_pairs={{0,16},{16,32},{32,48},{48,64},{64,80},{80,96},{96,112},{112,128},... | collective-permute-start | bytes 417800 | tf_op jit(solution)/shard_map/ppermute | solution.py:825
  22.6 20.4 %collective-permute-start.5 = (f32[272,128]{1,0:T(8,128)S(1)}, f32[272,128]{1,0:T(8,128)S(1)}, u32[]{:S(2)}, u32[]{:S(2)}) collective-permute-start(f32[272,128]{1,0:T(8,128)S(1)} %get-tuple-element.34), channel_id=1, source_target_pairs={{16,0},{32,16},{48,32},{64,48},{80,64},{96,80},{112,96},{128,112},... | collective-permute-start | bytes 417800 | tf_op jit(solution)/shard_map/ppermute | solution.py:826
  29.3 24.0 %collective-permute-start.3 = (f32[144,128]{1,0:T(8,128)S(1)}, f32[144,128]{1,0:T(8,128)S(1)}, u32[]{:S(2)}, u32[]{:S(2)}) collective-permute-start(f32[144,128]{1,0:T(8,128)S(1)} %get-tuple-element.31), channel_id=1, source_target_pairs={{15,15},{31,511},{47,495},{63,479},{79,463},{95,447},{111,431},{12... | collective-permute-start | bytes 221192 | tf_op jit(solution)/shard_map/ppermute | solution.py:828
  30.0 25.9 %collective-permute-start.2 = (f32[888,128]{1,0:T(8,128)S(1)}, f32[888,128]{1,0:T(8,128)S(1)}, u32[]{:S(2)}, u32[]{:S(2)}) collective-permute-start(f32[888,128]{1,0:T(8,128)S(1)} %get-tuple-element.30), channel_id=1, source_target_pairs={{1,2},{2,1},{3,4},{4,3},{5,6},{6,5},{7,8},{8,7},{9,10},{10,9},{11,... | collective-permute-start | bytes 1363976 | tf_op jit(solution)/shard_map/ppermute | solution.py:827
  57.6 23.2 %collective-permute-start.6 = (f32[88,128]{1,0:T(8,128)S(1)}, f32[88,128]{1,0:T(8,128)S(1)}, u32[]{:S(2)}, u32[]{:S(2)}) collective-permute-start(f32[88,128]{1,0:T(8,128)S(1)} %get-tuple-element.37), channel_id=1, source_target_pairs={{0,1},{1,0},{2,3},{3,2},{4,5},{5,4},{6,7},{7,6},{8,9},{9,8},{10,11... | collective-permute-start | bytes 135176 | tf_op jit(solution)/shard_map/ppermute | solution.py:841
  71.0 22.1 %collective-permute-start.7 = (f32[152,128]{1,0:T(8,128)S(1)}, f32[152,128]{1,0:T(8,128)S(1)}, u32[]{:S(2)}, u32[]{:S(2)}) collective-permute-start(f32[152,128]{1,0:T(8,128)S(1)} %get-tuple-element.39), channel_id=1, source_target_pairs={{0,16},{16,32},{32,48},{48,64},{64,80},{80,96},{96,112},{112,128},... | collective-permute-start | bytes 233480 | tf_op jit(solution)/shard_map/ppermute | solution.py:842
  72.9 20.1 %collective-permute-start.8 = (f32[152,128]{1,0:T(8,128)S(1)}, f32[152,128]{1,0:T(8,128)S(1)}, u32[]{:S(2)}, u32[]{:S(2)}) collective-permute-start(f32[152,128]{1,0:T(8,128)S(1)} %get-tuple-element.40), channel_id=1, source_target_pairs={{16,0},{32,16},{48,32},{64,48},{80,64},{96,80},{112,96},{128,112},... | collective-permute-start | bytes 233480 | tf_op jit(solution)/shard_map/ppermute | solution.py:843

commit v5 on v4

--- a/solution.py
+++ b/solution.py
@@ -73,6 +73,7 @@
 SM = pl.BlockSpec(memory_space=pltpu.SMEM)
 LIMIT = 32 * 1024 * 1024
 UNROLL = {"column": 8}
+TOGETHER = {"explicit": 0, "lateral": 0}
 
 
 def call(body, outs, ins, flops, scratch=()):
@@ -81,7 +82,7 @@
         out_shape=tuple(jax.ShapeDtypeStruct(s, jnp.float32) for s in outs),
         in_specs=ins,
         out_specs=tuple(VM for _ in outs),
-        scratch_shapes=[pltpu.VMEM(s, jnp.float32) if isinstance(s, tuple) else s for s in scratch],
+        scratch_shapes=[pltpu.VMEM(s, jnp.float32) for s in scratch],
         compiler_params=pltpu.CompilerParams(vmem_limit_bytes=LIMIT),
         cost_estimate=pl.CostEstimate(flops=flops, bytes_accessed=4 * 1024 * 1024, transcendentals=0),
     )
@@ -141,15 +142,7 @@
     lax.fori_loop(0, rows // 8, one, 0, unroll=8)
 
 
-def own_body(
-    flag_ref, state_in, mixing_in, wet_in, x_ref, a_ref, b_ref, full_ref, state_ref, mixing_ref, wet_ref, arrived
-):
-    pairs = ((wet_in, wet_ref), (mixing_in, mixing_ref), (state_in, state_ref))
-    copies = [pltpu.make_async_copy(source, out, arrived.at[n]) for n, (source, out) in enumerate(pairs)]
-    for copy in copies:
-        copy.start()
-    for copy in copies:
-        copy.wait()
+def own_body(flag_ref, state_ref, mixing_ref, wet_ref, x_ref, a_ref, b_ref, full_ref):
     levels = rows_of().astype(jnp.float32)
     odd = flag_ref[0] == 1
     fold = flag_ref[1] == 1
@@ -230,17 +223,17 @@
         west_ref[strips.wet + t : strips.wet + t + 8, :] = add_strip(zero, tile, 0, 0)
 
 
-def early_frame_body(flag_ref, x_ref, y_ref, b_in, b_ref, c_ref, frame_ref, east_ref, west_ref, full_ref):
+def early_frame_body(
+    flag_ref, x_ref, y_ref, a_in, b_in, b_ref, fold_a_ref, fold_b_ref, frame_ref, east_ref, west_ref, full_ref
+):
     fold = flag_ref[1] == 1
-    b_ref[0:HALF, :] = b_in[...]
 
     @pl.when(jnp.logical_not(fold))
     def _():
         for k in (TEMP, SALT):
             copy_blocks(b_ref, HALF + k * LEV, y_ref, (k * 8 + 7) * LEV, 1)
-        b_ref[HALF + 2 * LEV : HALF + 2 * LEV + 8, :] = spread(y_ref, OWN_WET + 7)
-        b_ref[HALF + 2 * LEV + 8 : HALF + MORE, :] = jnp.zeros((MORE - 2 * LEV - 8, 128), jnp.float32)
-        c_ref[...] = jnp.zeros((MORE, 128), jnp.float32)
+        b_ref[HALF + 2 * LEV : HALF + FAR, :] = spread(y_ref, OWN_WET + 7)
+        b_ref[0:HALF, :] = b_in[...]
 
     @pl.when(fold)
     def _():
@@ -258,7 +251,9 @@
             copy_block(full_ref, n * LEV, source, (k * 8 + row) * LEV, change)
         wet = jnp.where(rows_of() == 0, spread(y_ref, OWN_WET + 7), spread(y_ref, OWN_WET + 6))
         full_ref[MORE_WET : MORE_WET + 8, :] = mirror(wet)
-        split_halves(full_ref, c_ref, b_ref.at[HALF : HALF + MORE], MORE)
+        split_halves(full_ref, fold_a_ref.at[HALF : HALF + MORE], fold_b_ref.at[HALF : HALF + MORE], MORE)
+        fold_a_ref[0:HALF, :] = a_in[...]
+        fold_b_ref[0:HALF, :] = b_in[...]
 
     for k in range(5):
         copy_blocks(frame_ref, block_at(k, PLACE_NEAR[0]), x_ref, k * 8 * LEV, 8)
@@ -272,7 +267,7 @@
 
 
 def frame_body(
-    flag_ref, early_ref, a_ref, b_ref, c_ref, main_early, side_early, frame_ref, far_ref, east_ref, west_ref, full_ref, more_ref
+    flag_ref, early_ref, a_ref, b_ref, fold_a_ref, fold_b_ref, main_early, side_early, frame_ref, far_ref, east_ref, west_ref, full_ref, more_ref
 ):
     fold = flag_ref[1] == 1
 
@@ -304,8 +299,8 @@
 
     @pl.when(fold)
     def _():
-        join_halves(full_ref, a_ref, b_ref, HALF)
-        join_halves(more_ref, c_ref, b_ref.at[HALF : HALF + MORE], MORE)
+        join_halves(full_ref, fold_a_ref.at[0:HALF], fold_b_ref.at[0:HALF], HALF)
+        join_halves(more_ref, fold_a_ref.at[HALF : HALF + MORE], fold_b_ref.at[HALF : HALF + MORE], MORE)
         for k in range(5):
             bulk(k, 0, 0, COUNT[k])
         for r in range(8):
@@ -497,7 +492,7 @@
 
             return [work(row) for row in sorted({*span_a, *span_f})]
 
-        in_turn(piece(False, near_a, near_f) + piece(True, far_a, far_f))
+        return piece(False, near_a, near_f) + piece(True, far_a, far_f)
 
     def lateral(step, g):
         near_f, far_f = spans[step][2:4]
@@ -566,7 +561,7 @@
 
             return [work(row) for row in sorted(span_f)]
 
-        in_turn(piece(False, near_f) + piece(True, far_f))
+        return piece(False, near_f) + piece(True, far_f)
 
     for step in range(len(spans)):
         source = frame_ref if step == 0 else f_ref
@@ -582,17 +577,20 @@
 
         lax.fori_loop(0, LEV, weigh, (zero,) * len(weights), unroll=UNROLL["column"])
 
-        def explicit_group(g, c):
-            explicit(step, g)
-            return c
-
-        def lateral_group(g, c):
-            lateral(step, g)
-            return c
-
-        lax.fori_loop(0, GROUPS, explicit_group, 0)
+        def by_groups(make, together):
+            def one(g, c):
+                in_turn(make(step, g))
+                return c
+
+            if not together:
+                lax.fori_loop(0, GROUPS, one, 0)
+                return
+            for n in range(0, GROUPS, together):
+                in_turn([job for g in range(n, min(n + together, GROUPS)) for job in make(step, g)])
+
+        by_groups(explicit, TOGETHER["explicit"])
         after(step, "adv")
-        lax.fori_loop(0, GROUPS, lateral_group, 0)
+        by_groups(lateral, TOGETHER["lateral"])
 
         def down(l, carry):
             loads = [(eight(coef_ref, 0, t, l), eight(coef_ref, 1, t, l), [eight(rhs_ref, k, t, l) for k in range(4)]) for t in tiles]
@@ -799,33 +797,28 @@
     x, a, b = call(
         own_body,
         [(OWN, 128), half, half],
-        [SM] + [pl.BlockSpec(memory_space=pltpu.HBM)] * 3,
+        [SM] + [VM] * 3,
         10**6,
-        [
-            (2 * HALF, 128),
-            (4 * LEV * 8, 128),
-            (LEV * 8, 128),
-            pltpu.VMEM(wet_levels.shape, wet_levels.dtype),
-            pltpu.SemaphoreType.DMA((3,)),
-        ],
+        [(2 * HALF, 128)],
     )(
         flags, state.reshape(4 * LEV * 8, 128), mixing.reshape(LEV * 8, 128), wet_levels
     )
-    a = lax.ppermute(a, both, cross + fold_a)
+    far_a = lax.ppermute(a, both, cross)
     y = lax.ppermute(x, both, pairs)
     to_east_pairs = [(i, (i + 1) % lons) for i in range(lons)]
     to_west_pairs = [((i + 1) % lons, i) for i in range(lons)]
-    b, c, early_frame, to_east, to_west = call(
+    b, beyond_a, beyond_b, early_frame, to_east, to_west = call(
         early_frame_body,
-        [(HALF + MORE, 128), (MORE, 128), (FRAME, 128), EARLY.shape, EARLY.shape],
-        [SM, VM, VM, VM],
+        [(HALF + FAR, 128), (HALF + MORE, 128), (HALF + MORE, 128), (FRAME, 128), EARLY.shape, EARLY.shape],
+        [SM] + [VM] * 4,
         10**6,
         [(2 * MORE, 128)],
-    )(flags, x, y, b)
+    )(flags, x, y, a, b)
     from_west = lax.ppermute(to_east, "lon", to_east_pairs)
     from_east = lax.ppermute(to_west, "lon", to_west_pairs)
-    b = lax.ppermute(b, both, cross + fold_b)
-    c = lax.ppermute(c, both, fold_a)
+    far_b = lax.ppermute(b, both, cross)
+    beyond_a = lax.ppermute(beyond_a, both, fold_a)
+    beyond_b = lax.ppermute(beyond_b, both, fold_b)
     wet = (32, 128)
     main_early = call(early_main_body, HANDED_SHAPES, [SM, VM, VM], 10**9, [wet] + WORK)(flags, early_frame, rate)
     side_frame, *side_early = call(
@@ -834,10 +827,10 @@
     frame, far, to_east, to_west = call(
         frame_body,
         [(FRAME, 128), (FAR, 128), LATE.shape, LATE.shape],
-        [SM] + [VM] * 4 + [pl.BlockSpec(memory_space=pl.ANY)] * 2,
+        [SM] + [VM] * 5 + [pl.BlockSpec(memory_space=pl.ANY)] * 2,
         10**6,
         [(2 * HALF, 128), (2 * MORE, 128)],
-    )(flags, early_frame, a, b, c, main_early[0], side_early[0])
+    )(flags, early_frame, far_a, far_b, beyond_a, beyond_b, main_early[0], side_early[0])
     far = lax.ppermute(far, both, pairs)
     from_west = lax.ppermute(to_east, "lon", to_east_pairs)
     from_east = lax.ppermute(to_west, "lon", to_west_pairs)

time: 109 us -> 107 us (0.982)
  waiting for transfers between devices: 5.58 us -> 4.22 us
    ppermute x1, starting transfers between devices: 13.4 us -> 10.8 us  [local(): far = lax.ppermute(far, both, pairs)]
    ppermute x2, starting transfers between devices: 14.5 us -> 16.7 us  [local(): from_east = lax.ppermute(to_west, 'lon', to_west_pairs)]
    ppermute x2, waiting for transfers between devices: 2.97 us -> 1.64 us  [local(): from_east = lax.ppermute(to_west, 'lon', to_west_pairs)]
    ppermute x3 -> x4, starting transfers between devices: 13.9 us -> 14.6 us  [the longest x1 11.3 us: local(): far_a = lax.ppermute(a, both, cross)]
    ppermute x3 -> x4, waiting for transfers between devices: 2.6 us -> 2.57 us  [the longest x1 2.56 us: local(): far_b = lax.ppermute(b, both, cross)]
  transfers between devices with their start and end apart: 9 -> 10, of which waited for: 2 -> 2; matrix products, arithmetic and copies ran while one was open for 0% -> 0% of each run, Pallas kernels for 30% -> 30%
where the time goes in v5:
time: 107 us
  Pallas kernels  50.1 us (47%)
  starting transfers between devices  49.3 us (46%)
  waiting for transfers between devices  4.22 us (4%)
  local copies, waits for them, and re-layouts  2.77 us (3%)
    ppermute x2, starting transfers between devices, local(): from_east = lax.ppermute(to_west, 'lon', to_west_pairs)  16.7 us
    pallas_call x1, Pallas kernels, local(): call(late_side_body, [state.shape], [SM] + [VM] * 11, 10 ** 9, work)  15.1 us
    pallas_call x1, Pallas kernels, local(): call(late_main_body, [state.shape], [SM] + [VM] * 7, 10 ** 9, [wet] + WORK)  12.3 us
    ppermute x1, starting transfers between devices, local(): far_a = lax.ppermute(a, both, cross)  11.3 us
    ppermute x1, starting transfers between devices, local(): far = lax.ppermute(far, both, pairs)  10.8 us
    pallas_call x1, Pallas kernels, local(): call(early_side_body, [(FRAME, 128)] + HANDED_SHAPES, [SM] + [VM] * 4, 10...  10.3 us
    pallas_call x1, Pallas kernels, local(): call(early_main_body, HANDED_SHAPES, [SM, VM, VM], 10 ** 9, [wet] + WORK)  8.03 us
    ppermute x2, starting transfers between devices, local(): from_west = lax.ppermute(to_east, 'lon', to_east_pairs)  5.3 us
  transfers between devices with their start and end apart: 10, of which 2 were waited for; matrix products, arithmetic and copies ran while one was open for 0% of the time, Pallas kernels for 30%

profile of v5, /device:TPU:6, one launch (start us, length us, event | category | flops | bytes accessed | tf_op | source)
XLA Modules:
  0.0 106.6 jit_solution(2562176023206303210)
XLA Ops:
  0.0 0.0 copy-start.3
  0.0 0.0 copy-start.4
  0.0 0.1 pad_add_fusion.flag_ref
  0.1 0.0 copy-start
  0.1 1.1 %copy-done = f32[4,40,8,128]{3,2,1,0:T(8,128)S(1)} copy-done((f32[4,40,8,128]{3,2,1,0:T(8,128)S(1)}, f32[4,40,8,128]{3,2,1,0:T(8,128)}, u32[]{:S(2)}) %copy-start) | copy-done | bytes 655384
  1.2 0.0 copy-start.1
  1.2 0.9 copy-done.1
  2.1 0.0 copy-start.2
  2.1 0.7 copy-done.2
  2.8 0.9 shard_map.46
  3.6 1.9 %collective-permute-start = (f32[1608,128]{1,0:T(8,128)S(1)}, f32[1608,128]{1,0:T(8,128)S(1)}, u32[]{:S(2)}, u32[]{:S(2)}) collective-permute-start(f32[1608,128]{1,0:T(8,128)S(1)} %get-tuple-element.27.x_ref), channel_id=1, source_target_pairs={{0,1},{1,0},{2,3},{3,2},{4,5},{5,4},{6,7},{7,6},{8,9},{9,8},{10,11... | collective-permute-start | bytes 2469896 | tf_op jit(solution)/shard_map/ppermute | solution.py:807
  5.6 11.3 %collective-permute-start.1 = (f32[744,128]{1,0:T(8,128)S(1)}, f32[744,128]{1,0:T(8,128)S(1)}, u32[]{:S(2)}, u32[]{:S(2)}) collective-permute-start(f32[744,128]{1,0:T(8,128)S(1)} %get-tuple-element.28.a_in), channel_id=1, source_target_pairs={{1,2},{2,1},{3,4},{4,3},{5,6},{6,5},{7,8},{8,7},{9,10},{10,9},{11,... | collective-permute-start | bytes 1142792 | tf_op jit(solution)/shard_map/ppermute | solution.py:806
  16.9 0.0 collective-permute-done.y_ref
  16.9 1.9 %shard_map.47 = (f32[832,128]{1,0:T(8,128)S(1)}, f32[888,128]{1,0:T(8,128)S(1)}, f32[888,128]{1,0:T(8,128)S(1)}, f32[5432,128]{1,0:T(8,128)S(1)}, f32[272,128]{1,0:T(8,128)S(1)}, /*index=5*/f32[272,128]{1,0:T(8,128)S(1)}) custom-call(s32[2]{0:T(128)S(1)} %pad_add_fusion.flag_ref, f32[1608,128]{1,0:T(8,128)S(1)} %get-tuple-element.27.x_ref, ...), custom_call_target="tpu_custom_call" | custom-call | flops 1000000 | bytes 4194304 | tf_op jit(solution)/shard_map/pallas_call | solution.py:810
  18.8 3.4 %collective-permute-start.5 = (f32[272,128]{1,0:T(8,128)S(1)}, f32[272,128]{1,0:T(8,128)S(1)}, u32[]{:S(2)}, u32[]{:S(2)}) collective-permute-start(f32[272,128]{1,0:T(8,128)S(1)} %get-tuple-element.35), channel_id=1, source_target_pairs={{0,16},{16,32},{32,48},{48,64},{64,80},{80,96},{96,112},{112,128},... | collective-permute-start | bytes 417800 | tf_op jit(solution)/shard_map/ppermute | solution.py:817
  22.1 6.6 %collective-permute-start.6 = (f32[272,128]{1,0:T(8,128)S(1)}, f32[272,128]{1,0:T(8,128)S(1)}, u32[]{:S(2)}, u32[]{:S(2)}) collective-permute-start(f32[272,128]{1,0:T(8,128)S(1)} %get-tuple-element.36), channel_id=1, source_target_pairs={{16,0},{32,16},{48,32},{64,48},{80,64},{96,80},{112,96},{128,112},... | collective-permute-start | bytes 417800 | tf_op jit(solution)/shard_map/ppermute | solution.py:818
  28.8 0.0 copy-done.3
  28.8 0.0 copy-done.4
  28.8 0.1 broadcast_select_fusion
  28.9 1.9 %collective-permute-start.2 = (f32[832,128]{1,0:T(8,128)S(1)}, f32[832,128]{1,0:T(8,128)S(1)}, u32[]{:S(2)}, u32[]{:S(2)}) collective-permute-start(f32[832,128]{1,0:T(8,128)S(1)} %get-tuple-element.31), channel_id=1, source_target_pairs={{1,2},{2,1},{3,4},{4,3},{5,6},{6,5},{7,8},{8,7},{9,10},{10,9},{11,... | collective-permute-start | bytes 1277960 | tf_op jit(solution)/shard_map/ppermute | solution.py:819
  30.8 0.7 collective-permute-start.3
  31.5 0.1 broadcast_in_dim.2.rate_ref
  31.6 8.0 %shard_map.48 = (f32[448,128]{1,0:T(8,128)S(1)}, f32[1600,128]{1,0:T(8,128)S(1)}, f32[448,128]{1,0:T(8,128)S(1)}, f32[640,128]{1,0:T(8,128)S(1)}) custom-call(s32[2]{0:T(128)S(1)} %pad_add_fusion.flag_ref, f32[5432,128]{1,0:T(8,128)S(1)} %get-tuple-element.30.frame_ref.early_ref, f32[32,128]{1,0:T(8,128)S(1)} %broadcast_in_dim.2.rate_ref), custom_call_target="tpu_custom_call" | custom-call | flops 1000000000 | bytes 4194304 | tf_op jit(solution)/shard_map/pallas_call | solution.py:823
  39.6 0.0 collective-permute-done.5.east_ref
  39.6 0.7 collective-permute-start.4
  40.3 1.6 %collective-permute-done.6.west_ref = f32[272,128]{1,0:T(8,128)S(1)} collective-permute-done((f32[272,128]{1,0:T(8,128)S(1)}, f32[272,128]{1,0:T(8,128)S(1)}, u32[]{:S(2)}, u32[]{:S(2)}) %collective-permute-start.6) | collective-permute-done | bytes 139296 | tf_op jit(solution)/shard_map/ppermute | solution.py:818
  42.0 10.3 %shard_map.49 = (f32[5432,128]{1,0:T(8,128)S(1)}, f32[448,128]{1,0:T(8,128)S(1)}, f32[1600,128]{1,0:T(8,128)S(1)}, f32[448,128]{1,0:T(8,128)S(1)}, f32[640,128]{1,0:T(8,128)S(1)}) custom-call(s32[2]{0:T(128)S(1)} %pad_add_fusion.flag_ref, f32[5432,128]{1,0:T(8,128)S(1)} %get-tuple-element.30.frame_ref.early_ref, f32[32,128]{1,0:T(8,128)S(1)} %broadcast_in_dim.2.rate_ref, ...), custom_call_target="tpu_custom_call" | custom-call | flops 99999997952 | bytes 4194304 | tf_op jit(solution)/shard_map/pallas_call | solution.py:824
  52.2 0.0 collective-permute-done.1.a_ref
  52.3 2.6 %collective-permute-done.2.b_ref = f32[832,128]{1,0:T(8,128)S(1)} collective-permute-done((f32[832,128]{1,0:T(8,128)S(1)}, f32[832,128]{1,0:T(8,128)S(1)}, u32[]{:S(2)}, u32[]{:S(2)}) %collective-permute-start.2) | collective-permute-done | bytes 426016 | tf_op jit(solution)/shard_map/ppermute | solution.py:819
  54.8 0.0 collective-permute-done.3.fold_a_ref
  54.8 0.0 collective-permute-done.4.fold_b_ref
  54.8 1.7 %shard_map.50 = (f32[5432,128]{1,0:T(8,128)S(1)}, f32[88,128]{1,0:T(8,128)S(1)}, f32[152,128]{1,0:T(8,128)S(1)}, f32[152,128]{1,0:T(8,128)S(1)}) custom-call(s32[2]{0:T(128)S(1)} %pad_add_fusion.flag_ref, f32[5432,128]{1,0:T(8,128)S(1)} %get-tuple-element.30.frame_ref.early_ref, f32[744,128]{1,0:T(8,128)S(1)} %collective-permute-done.1.a_ref, ...), custom_call_target="tpu_custom_call" | custom-call | flops 1000000 | bytes 4194304 | tf_op jit(solution)/shard_map/pallas_call | solution.py:827
  56.5 10.8 %collective-permute-start.7 = (f32[88,128]{1,0:T(8,128)S(1)}, f32[88,128]{1,0:T(8,128)S(1)}, u32[]{:S(2)}, u32[]{:S(2)}) collective-permute-start(f32[88,128]{1,0:T(8,128)S(1)} %get-tuple-element.39), channel_id=1, source_target_pairs={{0,1},{1,0},{2,3},{3,2},{4,5},{5,4},{6,7},{7,6},{8,9},{9,8},{10,11... | collective-permute-start | bytes 135176 | tf_op jit(solution)/shard_map/ppermute | solution.py:834
  67.3 1.9 %collective-permute-start.8 = (f32[152,128]{1,0:T(8,128)S(1)}, f32[152,128]{1,0:T(8,128)S(1)}, u32[]{:S(2)}, u32[]{:S(2)}) collective-permute-start(f32[152,128]{1,0:T(8,128)S(1)} %get-tuple-element.41), channel_id=1, source_target_pairs={{0,16},{16,32},{32,48},{48,64},{64,80},{80,96},{96,112},{112,128},... | collective-permute-start | bytes 233480 | tf_op jit(solution)/shard_map/ppermute | solution.py:835
  69.2 10.0 %collective-permute-start.9 = (f32[152,128]{1,0:T(8,128)S(1)}, f32[152,128]{1,0:T(8,128)S(1)}, u32[]{:S(2)}, u32[]{:S(2)}) collective-permute-start(f32[152,128]{1,0:T(8,128)S(1)} %get-tuple-element.42), channel_id=1, source_target_pairs={{16,0},{32,16},{48,32},{64,48},{80,64},{96,80},{112,96},{128,112},... | collective-permute-start | bytes 233480 | tf_op jit(solution)/shard_map/ppermute | solution.py:836
  79.3 0.0 collective-permute-done.7.far_ref
  79.3 12.3 %shard_map.51.main_ref = f32[4,40,8,128]{3,2,1,0:T(8,128)S(1)} custom-call(s32[2]{0:T(128)S(1)} %pad_add_fusion.flag_ref, f32[5432,128]{1,0:T(8,128)S(1)} %get-tuple-element.38.frame_ref.frame_in, f32[88,128]{1,0:T(8,128)S(1)} %collective-permute-done.7.far_ref, f32[32,128]{1,0:T(8,128)S(1)} %broadcast_in_dim.2.rate_ref, ...), custom_call_target="tpu_custom_call" | custom-call | flops 1000000000 | bytes 4194304 | tf_op jit(solution)/shard_map/pallas_call | solution.py:838
  91.5 0.0 collective-permute-done.8.east_ref
  91.6 0.0 collective-permute-done.9.west_ref
  91.6 15.1 %shard_map.52 = f32[4,40,8,128]{3,2,1,0:T(8,128)} custom-call(s32[2]{0:T(128)S(1)} %pad_add_fusion.flag_ref, f32[5432,128]{1,0:T(8,128)S(1)} %get-tuple-element.38.frame_ref.frame_in, f32[88,128]{1,0:T(8,128)S(1)} %collective-permute-done.7.far_ref, f32[32,128]{1,0:T(8,128)S(1)} %broadcast_in_dim.2.rate_ref, f32[5432,128]{1,0:T(8,128)S(1)} %get-tuple-element.40.side_in, ...), custom_call_target="tpu_custom_call" | custom-call | flops 1000000000 | bytes 4194304 | tf_op jit(solution)/shard_map/pallas_call | solution.py:839
Async XLA Ops:
  0.0 28.8 %copy-start.3 = (s32[32]{0:T(128)S(1)}, s32[32]{0:T(128)}, u32[]{:S(2)}) copy-start(s32[32]{0:T(128)} %constant.39) | copy-start | bytes 388
  0.0 28.8 %copy-start.4 = (s32[32]{0:T(128)S(1)}, s32[32]{0:T(128)}, u32[]{:S(2)}) copy-start(s32[32]{0:T(128)} %constant.34.clone) | copy-start | bytes 388
  0.1 1.1 %copy-start = (f32[4,40,8,128]{3,2,1,0:T(8,128)S(1)}, f32[4,40,8,128]{3,2,1,0:T(8,128)}, u32[]{:S(2)}) copy-start(f32[4,40,8,128]{3,2,1,0:T(8,128)} %param.4) | copy-start | bytes 1966084
  1.2 0.9 copy-start.1
  2.1 0.7 copy-start.2
  3.6 13.2 %collective-permute-start = (f32[1608,128]{1,0:T(8,128)S(1)}, f32[1608,128]{1,0:T(8,128)S(1)}, u32[]{:S(2)}, u32[]{:S(2)}) collective-permute-start(f32[1608,128]{1,0:T(8,128)S(1)} %get-tuple-element.27.x_ref), channel_id=1, source_target_pairs={{0,1},{1,0},{2,3},{3,2},{4,5},{5,4},{6,7},{7,6},{8,9},{9,8},{10,11... | collective-permute-start | bytes 2469896 | tf_op jit(solution)/shard_map/ppermute | solution.py:807
  5.6 46.7 %collective-permute-start.1 = (f32[744,128]{1,0:T(8,128)S(1)}, f32[744,128]{1,0:T(8,128)S(1)}, u32[]{:S(2)}, u32[]{:S(2)}) collective-permute-start(f32[744,128]{1,0:T(8,128)S(1)} %get-tuple-element.28.a_in), channel_id=1, source_target_pairs={{1,2},{2,1},{3,4},{4,3},{5,6},{6,5},{7,8},{8,7},{9,10},{10,9},{11,... | collective-permute-start | bytes 1142792 | tf_op jit(solution)/shard_map/ppermute | solution.py:806
  18.8 20.8 %collective-permute-start.5 = (f32[272,128]{1,0:T(8,128)S(1)}, f32[272,128]{1,0:T(8,128)S(1)}, u32[]{:S(2)}, u32[]{:S(2)}) collective-permute-start(f32[272,128]{1,0:T(8,128)S(1)} %get-tuple-element.35), channel_id=1, source_target_pairs={{0,16},{16,32},{32,48},{48,64},{64,80},{80,96},{96,112},{112,128},... | collective-permute-start | bytes 417800 | tf_op jit(solution)/shard_map/ppermute | solution.py:817
  22.1 19.8 %collective-permute-start.6 = (f32[272,128]{1,0:T(8,128)S(1)}, f32[272,128]{1,0:T(8,128)S(1)}, u32[]{:S(2)}, u32[]{:S(2)}) collective-permute-start(f32[272,128]{1,0:T(8,128)S(1)} %get-tuple-element.36), channel_id=1, source_target_pairs={{16,0},{32,16},{48,32},{64,48},{80,64},{96,80},{112,96},{128,112},... | collective-permute-start | bytes 417800 | tf_op jit(solution)/shard_map/ppermute | solution.py:818
  28.9 25.9 %collective-permute-start.2 = (f32[832,128]{1,0:T(8,128)S(1)}, f32[832,128]{1,0:T(8,128)S(1)}, u32[]{:S(2)}, u32[]{:S(2)}) collective-permute-start(f32[832,128]{1,0:T(8,128)S(1)} %get-tuple-element.31), channel_id=1, source_target_pairs={{1,2},{2,1},{3,4},{4,3},{5,6},{6,5},{7,8},{8,7},{9,10},{10,9},{11,... | collective-permute-start | bytes 1277960 | tf_op jit(solution)/shard_map/ppermute | solution.py:819
  30.8 24.0 %collective-permute-start.3 = (f32[888,128]{1,0:T(8,128)S(1)}, f32[888,128]{1,0:T(8,128)S(1)}, u32[]{:S(2)}, u32[]{:S(2)}) collective-permute-start(f32[888,128]{1,0:T(8,128)S(1)} %get-tuple-element.32), channel_id=1, source_target_pairs={{15,15},{31,511},{47,495},{63,479},{79,463},{95,447},{111,431},{12... | collective-permute-start | bytes 1363976 | tf_op jit(solution)/shard_map/ppermute | solution.py:820
  39.6 15.2 %collective-permute-start.4 = (f32[888,128]{1,0:T(8,128)S(1)}, f32[888,128]{1,0:T(8,128)S(1)}, u32[]{:S(2)}, u32[]{:S(2)}) collective-permute-start(f32[888,128]{1,0:T(8,128)S(1)} %get-tuple-element.33), channel_id=1, source_target_pairs={{15,511},{31,495},{47,479},{63,463},{79,447},{95,431},{111,415},{1... | collective-permute-start | bytes 1363976 | tf_op jit(solution)/shard_map/ppermute | solution.py:821
  56.5 22.8 %collective-permute-start.7 = (f32[88,128]{1,0:T(8,128)S(1)}, f32[88,128]{1,0:T(8,128)S(1)}, u32[]{:S(2)}, u32[]{:S(2)}) collective-permute-start(f32[88,128]{1,0:T(8,128)S(1)} %get-tuple-element.39), channel_id=1, source_target_pairs={{0,1},{1,0},{2,3},{3,2},{4,5},{5,4},{6,7},{7,6},{8,9},{9,8},{10,11... | collective-permute-start | bytes 135176 | tf_op jit(solution)/shard_map/ppermute | solution.py:834
  67.3 24.3 %collective-permute-start.8 = (f32[152,128]{1,0:T(8,128)S(1)}, f32[152,128]{1,0:T(8,128)S(1)}, u32[]{:S(2)}, u32[]{:S(2)}) collective-permute-start(f32[152,128]{1,0:T(8,128)S(1)} %get-tuple-element.41), channel_id=1, source_target_pairs={{0,16},{16,32},{32,48},{48,64},{64,80},{80,96},{96,112},{112,128},... | collective-permute-start | bytes 233480 | tf_op jit(solution)/shard_map/ppermute | solution.py:835
  69.2 22.4 %collective-permute-start.9 = (f32[152,128]{1,0:T(8,128)S(1)}, f32[152,128]{1,0:T(8,128)S(1)}, u32[]{:S(2)}, u32[]{:S(2)}) collective-permute-start(f32[152,128]{1,0:T(8,128)S(1)} %get-tuple-element.42), channel_id=1, source_target_pairs={{16,0},{32,16},{48,32},{64,48},{80,64},{96,80},{112,96},{128,112},... | collective-permute-start | bytes 233480 | tf_op jit(solution)/shard_map/ppermute | solution.py:836

commit v6 on v5

--- a/solution.py
+++ b/solution.py
@@ -76,14 +76,14 @@
 TOGETHER = {"explicit": 0, "lateral": 0}
 
 
-def call(body, outs, ins, flops, scratch=()):
+def call(body, outs, ins, flops, scratch=(), limit=LIMIT):
     return pl.pallas_call(
         body,
         out_shape=tuple(jax.ShapeDtypeStruct(s, jnp.float32) for s in outs),
         in_specs=ins,
         out_specs=tuple(VM for _ in outs),
         scratch_shapes=[pltpu.VMEM(s, jnp.float32) for s in scratch],
-        compiler_params=pltpu.CompilerParams(vmem_limit_bytes=LIMIT),
+        compiler_params=pltpu.CompilerParams(vmem_limit_bytes=limit),
         cost_estimate=pl.CostEstimate(flops=flops, bytes_accessed=4 * 1024 * 1024, transcendentals=0),
     )
 
@@ -800,6 +800,7 @@
         [SM] + [VM] * 3,
         10**6,
         [(2 * HALF, 128)],
+        limit=63 * 1024 * 1024,
     )(
         flags, state.reshape(4 * LEV * 8, 128), mixing.reshape(LEV * 8, 128), wet_levels
     )

time: 107 us -> 113 us (1.056)
  the two profiles are of different devices: /device:TPU:6 before, /device:TPU:334 now
where the time goes in v6:
time: 113 us; the launch traced here: 112 us
  Pallas kernels  51.9 us (46%)
  starting transfers between devices  42.2 us (37%)
  waiting for transfers between devices  13.3 us (12%)
  local copies, waits for them, and re-layouts  3.84 us (3%)
    ppermute x1, starting transfers between devices, local(): far = lax.ppermute(far, both, pairs)  17.4 us
    pallas_call x1, Pallas kernels, local(): call(late_side_body, [state.shape], [SM] + [VM] * 11, 10 ** 9, work)  15.1 us
    pallas_call x1, Pallas kernels, local(): call(late_main_body, [state.shape], [SM] + [VM] * 7, 10 ** 9, [wet] + WORK)  12.3 us
    pallas_call x1, Pallas kernels, local(): call(early_side_body, [(FRAME, 128)] + HANDED_SHAPES, [SM] + [VM] * 4, 10...  10.3 us
    pallas_call x1, Pallas kernels, local(): call(early_main_body, HANDED_SHAPES, [SM, VM, VM], 10 ** 9, [wet] + WORK)  8.03 us
    ppermute x1, waiting for transfers between devices, local(): far_b = lax.ppermute(b, both, cross)  6.82 us
    ppermute x1, starting transfers between devices, local(): far_b = lax.ppermute(b, both, cross)  6.78 us
    ppermute x2, starting transfers between devices, local(): from_east = lax.ppermute(to_west, 'lon', to_west_pairs)  6.38 us
  transfers between devices with their start and end apart: 10, of which 3 were waited for; matrix products, arithmetic and copies ran while one was open for 0% of the time, Pallas kernels for 29%

profile of v6, /device:TPU:334, one launch (start us, length us, event | category | flops | bytes accessed | tf_op | source)
XLA Modules:
  0.0 112.1 jit_solution(4247674840233695572)
XLA Ops:
  0.0 0.0 copy-start.4
  0.0 0.0 copy-start.5
  0.0 0.6 pad_add_fusion.flag_ref
  0.6 2.7 %shard_map.46 = (f32[1608,128]{1,0:T(8,128)}, f32[744,128]{1,0:T(8,128)}, f32[744,128]{1,0:T(8,128)}) custom-call(s32[2]{0:T(128)} %pad_add_fusion.flag_ref, f32[1280,128]{1,0:T(8,128)} %bitcast.4, f32[320,128]{1,0:T(8,128)} %bitcast.5, s32[8,128]{1,0:T(8,128)} %wet_ref.1), custom_call_target="tpu_custom_call" | custom-call | flops 1000000 | bytes 4194304 | tf_op jit(solution)/shard_map/pallas_call | solution.py:797
  3.3 3.1 %collective-permute-start = (f32[1608,128]{1,0:T(8,128)}, f32[1608,128]{1,0:T(8,128)S(1)}, u32[]{:S(2)}, u32[]{:S(2)}) collective-permute-start(f32[1608,128]{1,0:T(8,128)} %get-tuple-element.27.x_ref), channel_id=1, source_target_pairs={{0,1},{1,0},{2,3},{3,2},{4,5},{5,4},{6,7},{7,6},{8,9},{9,8},{10,11... | collective-permute-start | bytes 2469896 | tf_op jit(solution)/shard_map/ppermute | solution.py:808
  6.4 1.9 %collective-permute-start.1 = (f32[744,128]{1,0:T(8,128)}, f32[744,128]{1,0:T(8,128)S(1)}, u32[]{:S(2)}, u32[]{:S(2)}) collective-permute-start(f32[744,128]{1,0:T(8,128)} %get-tuple-element.28.a_in), channel_id=1, source_target_pairs={{1,2},{2,1},{3,4},{4,3},{5,6},{6,5},{7,8},{8,7},{9,10},{10,9},{11,... | collective-permute-start | bytes 1142792 | tf_op jit(solution)/shard_map/ppermute | solution.py:807
  8.3 0.2 collective-permute-done.y_ref
  8.5 0.0 copy-start
  8.5 1.1 %copy-done = f32[1608,128]{1,0:T(8,128)S(1)} copy-done((f32[1608,128]{1,0:T(8,128)S(1)}, f32[1608,128]{1,0:T(8,128)}, u32[]{:S(2)}) %copy-start) | copy-done | bytes 823320
  9.7 0.0 copy-start.1
  9.7 1.0 copy-done.1
  10.7 0.0 copy-start.2
  10.7 1.0 copy-done.2
  11.6 0.0 copy-start.3
  11.6 0.6 copy-done.3
  12.3 1.9 %shard_map.47 = (f32[832,128]{1,0:T(8,128)S(1)}, f32[888,128]{1,0:T(8,128)S(1)}, f32[888,128]{1,0:T(8,128)S(1)}, f32[5432,128]{1,0:T(8,128)S(1)}, f32[272,128]{1,0:T(8,128)S(1)}, /*index=5*/f32[272,128]{1,0:T(8,128)S(1)}) custom-call(s32[2]{0:T(128)S(1)} %copy-done.3, f32[1608,128]{1,0:T(8,128)S(1)} %copy-done, f32[1608,128]{1,0:T(8,128)S(1)} %collective-permute-done.y_ref, ...), custom_call_target="tpu_custom_call" | custom-call | flops 1000000 | bytes 4194304 | tf_op jit(solution)/shard_map/pallas_call | solution.py:811
  14.2 3.4 %collective-permute-start.5 = (f32[272,128]{1,0:T(8,128)S(1)}, f32[272,128]{1,0:T(8,128)S(1)}, u32[]{:S(2)}, u32[]{:S(2)}) collective-permute-start(f32[272,128]{1,0:T(8,128)S(1)} %get-tuple-element.35), channel_id=1, source_target_pairs={{0,16},{16,32},{32,48},{48,64},{64,80},{80,96},{96,112},{112,128},... | collective-permute-start | bytes 417800 | tf_op jit(solution)/shard_map/ppermute | solution.py:818
  17.5 2.5 %collective-permute-start.6 = (f32[272,128]{1,0:T(8,128)S(1)}, f32[272,128]{1,0:T(8,128)S(1)}, u32[]{:S(2)}, u32[]{:S(2)}) collective-permute-start(f32[272,128]{1,0:T(8,128)S(1)} %get-tuple-element.36), channel_id=1, source_target_pairs={{16,0},{32,16},{48,32},{64,48},{80,64},{96,80},{112,96},{128,112},... | collective-permute-start | bytes 417800 | tf_op jit(solution)/shard_map/ppermute | solution.py:819
  20.0 0.0 copy-done.4
  20.0 0.0 copy-done.5
  20.0 0.1 broadcast_select_fusion
  20.1 6.8 %collective-permute-start.2 = (f32[832,128]{1,0:T(8,128)S(1)}, f32[832,128]{1,0:T(8,128)S(1)}, u32[]{:S(2)}, u32[]{:S(2)}) collective-permute-start(f32[832,128]{1,0:T(8,128)S(1)} %get-tuple-element.31), channel_id=1, source_target_pairs={{1,2},{2,1},{3,4},{4,3},{5,6},{6,5},{7,8},{8,7},{9,10},{10,9},{11,... | collective-permute-start | bytes 1277960 | tf_op jit(solution)/shard_map/ppermute | solution.py:820
  26.9 0.7 collective-permute-start.3
  27.6 0.1 broadcast_in_dim.2.rate_ref
  27.6 8.0 %shard_map.48 = (f32[448,128]{1,0:T(8,128)S(1)}, f32[1600,128]{1,0:T(8,128)S(1)}, f32[448,128]{1,0:T(8,128)S(1)}, f32[640,128]{1,0:T(8,128)S(1)}) custom-call(s32[2]{0:T(128)S(1)} %copy-done.3, f32[5432,128]{1,0:T(8,128)S(1)} %get-tuple-element.30.frame_ref.early_ref, f32[32,128]{1,0:T(8,128)S(1)} %broadcast_in_dim.2.rate_ref), custom_call_target="tpu_custom_call" | custom-call | flops 1000000000 | bytes 4194304 | tf_op jit(solution)/shard_map/pallas_call | solution.py:824
  35.7 6.2 %collective-permute-done.5.east_ref = f32[272,128]{1,0:T(8,128)S(1)} collective-permute-done((f32[272,128]{1,0:T(8,128)S(1)}, f32[272,128]{1,0:T(8,128)S(1)}, u32[]{:S(2)}, u32[]{:S(2)}) %collective-permute-start.5) | collective-permute-done | bytes 139296 | tf_op jit(solution)/shard_map/ppermute | solution.py:818
  41.9 0.7 collective-permute-start.4
  42.6 0.0 collective-permute-done.6.west_ref
  42.6 10.3 %shard_map.49 = (f32[5432,128]{1,0:T(8,128)S(1)}, f32[448,128]{1,0:T(8,128)S(1)}, f32[1600,128]{1,0:T(8,128)S(1)}, f32[448,128]{1,0:T(8,128)S(1)}, f32[640,128]{1,0:T(8,128)S(1)}) custom-call(s32[2]{0:T(128)S(1)} %copy-done.3, f32[5432,128]{1,0:T(8,128)S(1)} %get-tuple-element.30.frame_ref.early_ref, f32[32,128]{1,0:T(8,128)S(1)} %broadcast_in_dim.2.rate_ref, ...), custom_call_target="tpu_custom_call" | custom-call | flops 99999997952 | bytes 4194304 | tf_op jit(solution)/shard_map/pallas_call | solution.py:825
  52.9 0.0 collective-permute-done.1.a_ref
  52.9 6.8 %collective-permute-done.2.b_ref = f32[832,128]{1,0:T(8,128)S(1)} collective-permute-done((f32[832,128]{1,0:T(8,128)S(1)}, f32[832,128]{1,0:T(8,128)S(1)}, u32[]{:S(2)}, u32[]{:S(2)}) %collective-permute-start.2) | collective-permute-done | bytes 426016 | tf_op jit(solution)/shard_map/ppermute | solution.py:820
  59.7 0.0 collective-permute-done.3.fold_a_ref
  59.7 0.0 collective-permute-done.4.fold_b_ref
  59.7 1.7 %shard_map.50 = (f32[5432,128]{1,0:T(8,128)S(1)}, f32[88,128]{1,0:T(8,128)S(1)}, f32[152,128]{1,0:T(8,128)S(1)}, f32[152,128]{1,0:T(8,128)S(1)}) custom-call(s32[2]{0:T(128)S(1)} %copy-done.3, f32[5432,128]{1,0:T(8,128)S(1)} %get-tuple-element.30.frame_ref.early_ref, f32[744,128]{1,0:T(8,128)S(1)} %collective-permute-done.1.a_ref, ...), custom_call_target="tpu_custom_call" | custom-call | flops 1000000 | bytes 4194304 | tf_op jit(solution)/shard_map/pallas_call | solution.py:828
  61.4 17.4 %collective-permute-start.7 = (f32[88,128]{1,0:T(8,128)S(1)}, f32[88,128]{1,0:T(8,128)S(1)}, u32[]{:S(2)}, u32[]{:S(2)}) collective-permute-start(f32[88,128]{1,0:T(8,128)S(1)} %get-tuple-element.39), channel_id=1, source_target_pairs={{0,1},{1,0},{2,3},{3,2},{4,5},{5,4},{6,7},{7,6},{8,9},{9,8},{10,11... | collective-permute-start | bytes 135176 | tf_op jit(solution)/shard_map/ppermute | solution.py:835
  78.8 1.9 %collective-permute-start.8 = (f32[152,128]{1,0:T(8,128)S(1)}, f32[152,128]{1,0:T(8,128)S(1)}, u32[]{:S(2)}, u32[]{:S(2)}) collective-permute-start(f32[152,128]{1,0:T(8,128)S(1)} %get-tuple-element.41), channel_id=1, source_target_pairs={{0,16},{16,32},{32,48},{48,64},{64,80},{80,96},{96,112},{112,128},... | collective-permute-start | bytes 233480 | tf_op jit(solution)/shard_map/ppermute | solution.py:836
  80.8 3.9 %collective-permute-start.9 = (f32[152,128]{1,0:T(8,128)S(1)}, f32[152,128]{1,0:T(8,128)S(1)}, u32[]{:S(2)}, u32[]{:S(2)}) collective-permute-start(f32[152,128]{1,0:T(8,128)S(1)} %get-tuple-element.42), channel_id=1, source_target_pairs={{16,0},{32,16},{48,32},{64,48},{80,64},{96,80},{112,96},{128,112},... | collective-permute-start | bytes 233480 | tf_op jit(solution)/shard_map/ppermute | solution.py:837
  84.7 0.0 collective-permute-done.7.far_ref
  84.7 12.3 %shard_map.51.main_ref = f32[4,40,8,128]{3,2,1,0:T(8,128)S(1)} custom-call(s32[2]{0:T(128)S(1)} %copy-done.3, f32[5432,128]{1,0:T(8,128)S(1)} %get-tuple-element.38.frame_ref.frame_in, f32[88,128]{1,0:T(8,128)S(1)} %collective-permute-done.7.far_ref, f32[32,128]{1,0:T(8,128)S(1)} %broadcast_in_dim.2.rate_ref, ...), custom_call_target="tpu_custom_call" | custom-call | flops 1000000000 | bytes 4194304 | tf_op jit(solution)/shard_map/pallas_call | solution.py:839
  97.0 0.0 collective-permute-done.8.east_ref
  97.0 0.0 collective-permute-done.9.west_ref
  97.0 15.1 %shard_map.52 = f32[4,40,8,128]{3,2,1,0:T(8,128)} custom-call(s32[2]{0:T(128)S(1)} %copy-done.3, f32[5432,128]{1,0:T(8,128)S(1)} %get-tuple-element.38.frame_ref.frame_in, f32[88,128]{1,0:T(8,128)S(1)} %collective-permute-done.7.far_ref, f32[32,128]{1,0:T(8,128)S(1)} %broadcast_in_dim.2.rate_ref, f32[5432,128]{1,0:T(8,128)S(1)} %get-tuple-element.40.side_in, ...), custom_call_target="tpu_custom_call" | custom-call | flops 1000000000 | bytes 4194304 | tf_op jit(solution)/shard_map/pallas_call | solution.py:840
Async XLA Ops:
  0.0 20.0 %copy-start.4 = (s32[32]{0:T(128)S(1)}, s32[32]{0:T(128)}, u32[]{:S(2)}) copy-start(s32[32]{0:T(128)} %constant.39) | copy-start | bytes 388
  0.0 20.0 %copy-start.5 = (s32[32]{0:T(128)S(1)}, s32[32]{0:T(128)}, u32[]{:S(2)}) copy-start(s32[32]{0:T(128)} %constant.34.clone) | copy-start | bytes 388
  3.3 5.2 %collective-permute-start = (f32[1608,128]{1,0:T(8,128)}, f32[1608,128]{1,0:T(8,128)S(1)}, u32[]{:S(2)}, u32[]{:S(2)}) collective-permute-start(f32[1608,128]{1,0:T(8,128)} %get-tuple-element.27.x_ref), channel_id=1, source_target_pairs={{0,1},{1,0},{2,3},{3,2},{4,5},{5,4},{6,7},{7,6},{8,9},{9,8},{10,11... | collective-permute-start | bytes 2469896 | tf_op jit(solution)/shard_map/ppermute | solution.py:808
  6.4 46.5 %collective-permute-start.1 = (f32[744,128]{1,0:T(8,128)}, f32[744,128]{1,0:T(8,128)S(1)}, u32[]{:S(2)}, u32[]{:S(2)}) collective-permute-start(f32[744,128]{1,0:T(8,128)} %get-tuple-element.28.a_in), channel_id=1, source_target_pairs={{1,2},{2,1},{3,4},{4,3},{5,6},{6,5},{7,8},{8,7},{9,10},{10,9},{11,... | collective-permute-start | bytes 1142792 | tf_op jit(solution)/shard_map/ppermute | solution.py:807
  8.5 1.1 %copy-start = (f32[1608,128]{1,0:T(8,128)S(1)}, f32[1608,128]{1,0:T(8,128)}, u32[]{:S(2)}) copy-start(f32[1608,128]{1,0:T(8,128)} %get-tuple-element.27.x_ref) | copy-start | bytes 2469892
  9.7 1.0 copy-start.1
  10.7 1.0 copy-start.2
  11.6 0.6 copy-start.3
  14.2 27.7 %collective-permute-start.5 = (f32[272,128]{1,0:T(8,128)S(1)}, f32[272,128]{1,0:T(8,128)S(1)}, u32[]{:S(2)}, u32[]{:S(2)}) collective-permute-start(f32[272,128]{1,0:T(8,128)S(1)} %get-tuple-element.35), channel_id=1, source_target_pairs={{0,16},{16,32},{32,48},{48,64},{64,80},{80,96},{96,112},{112,128},... | collective-permute-start | bytes 417800 | tf_op jit(solution)/shard_map/ppermute | solution.py:818
  17.5 25.0 %collective-permute-start.6 = (f32[272,128]{1,0:T(8,128)S(1)}, f32[272,128]{1,0:T(8,128)S(1)}, u32[]{:S(2)}, u32[]{:S(2)}) collective-permute-start(f32[272,128]{1,0:T(8,128)S(1)} %get-tuple-element.36), channel_id=1, source_target_pairs={{16,0},{32,16},{48,32},{64,48},{80,64},{96,80},{112,96},{128,112},... | collective-permute-start | bytes 417800 | tf_op jit(solution)/shard_map/ppermute | solution.py:819
  20.1 39.6 %collective-permute-start.2 = (f32[832,128]{1,0:T(8,128)S(1)}, f32[832,128]{1,0:T(8,128)S(1)}, u32[]{:S(2)}, u32[]{:S(2)}) collective-permute-start(f32[832,128]{1,0:T(8,128)S(1)} %get-tuple-element.31), channel_id=1, source_target_pairs={{1,2},{2,1},{3,4},{4,3},{5,6},{6,5},{7,8},{8,7},{9,10},{10,9},{11,... | collective-permute-start | bytes 1277960 | tf_op jit(solution)/shard_map/ppermute | solution.py:820
  26.9 32.9 %collective-permute-start.3 = (f32[888,128]{1,0:T(8,128)S(1)}, f32[888,128]{1,0:T(8,128)S(1)}, u32[]{:S(2)}, u32[]{:S(2)}) collective-permute-start(f32[888,128]{1,0:T(8,128)S(1)} %get-tuple-element.32), channel_id=1, source_target_pairs={{15,15},{31,511},{47,495},{63,479},{79,463},{95,447},{111,431},{12... | collective-permute-start | bytes 1363976 | tf_op jit(solution)/shard_map/ppermute | solution.py:821
  41.9 17.8 %collective-permute-start.4 = (f32[888,128]{1,0:T(8,128)S(1)}, f32[888,128]{1,0:T(8,128)S(1)}, u32[]{:S(2)}, u32[]{:S(2)}) collective-permute-start(f32[888,128]{1,0:T(8,128)S(1)} %get-tuple-element.33), channel_id=1, source_target_pairs={{15,511},{31,495},{47,479},{63,463},{79,447},{95,431},{111,415},{1... | collective-permute-start | bytes 1363976 | tf_op jit(solution)/shard_map/ppermute | solution.py:822
  61.4 23.3 %collective-permute-start.7 = (f32[88,128]{1,0:T(8,128)S(1)}, f32[88,128]{1,0:T(8,128)S(1)}, u32[]{:S(2)}, u32[]{:S(2)}) collective-permute-start(f32[88,128]{1,0:T(8,128)S(1)} %get-tuple-element.39), channel_id=1, source_target_pairs={{0,1},{1,0},{2,3},{3,2},{4,5},{5,4},{6,7},{7,6},{8,9},{9,8},{10,11... | collective-permute-start | bytes 135176 | tf_op jit(solution)/shard_map/ppermute | solution.py:835
  78.8 18.1 %collective-permute-start.8 = (f32[152,128]{1,0:T(8,128)S(1)}, f32[152,128]{1,0:T(8,128)S(1)}, u32[]{:S(2)}, u32[]{:S(2)}) collective-permute-start(f32[152,128]{1,0:T(8,128)S(1)} %get-tuple-element.41), channel_id=1, source_target_pairs={{0,16},{16,32},{32,48},{48,64},{64,80},{80,96},{96,112},{112,128},... | collective-permute-start | bytes 233480 | tf_op jit(solution)/shard_map/ppermute | solution.py:836
  80.8 16.2 %collective-permute-start.9 = (f32[152,128]{1,0:T(8,128)S(1)}, f32[152,128]{1,0:T(8,128)S(1)}, u32[]{:S(2)}, u32[]{:S(2)}) collective-permute-start(f32[152,128]{1,0:T(8,128)S(1)} %get-tuple-element.42), channel_id=1, source_target_pairs={{16,0},{32,16},{48,32},{64,48},{80,64},{96,80},{112,96},{128,112},... | collective-permute-start | bytes 233480 | tf_op jit(solution)/shard_map/ppermute | solution.py:837

commit v7 on v5

--- a/solution.py
+++ b/solution.py
@@ -72,7 +72,7 @@
 VM = pl.BlockSpec(memory_space=pltpu.VMEM)
 SM = pl.BlockSpec(memory_space=pltpu.SMEM)
 LIMIT = 32 * 1024 * 1024
-UNROLL = {"column": 8}
+UNROLL = {"column": 4}
 TOGETHER = {"explicit": 0, "lateral": 0}
 
 

time: 107 us -> 108 us (level)
  Pallas kernels: 50.1 us -> 51.2 us
  transfers between devices with their start and end apart: 10 -> 10, of which waited for: 2 -> 2; matrix products, arithmetic and copies ran while one was open for 0% -> 0% of each run, Pallas kernels for 30% -> 31%
where the time goes in v7:
time: 108 us; the launch traced here: 107 us
  Pallas kernels  51.2 us (47%)
  starting transfers between devices  49.3 us (46%)
  waiting for transfers between devices  3.92 us (4%)
  local copies, waits for them, and re-layouts  2.77 us (3%)
    ppermute x2, starting transfers between devices, local(): from_east = lax.ppermute(to_west, 'lon', to_west_pairs)  16.7 us
    pallas_call x1, Pallas kernels, local(): call(late_side_body, [state.shape], [SM] + [VM] * 11, 10 ** 9, work)  15.7 us
    pallas_call x1, Pallas kernels, local(): call(late_main_body, [state.shape], [SM] + [VM] * 7, 10 ** 9, [wet] + WORK)  12.5 us
    ppermute x1, starting transfers between devices, local(): far_a = lax.ppermute(a, both, cross)  11.3 us
    ppermute x1, starting transfers between devices, local(): far = lax.ppermute(far, both, pairs)  10.8 us
    pallas_call x1, Pallas kernels, local(): call(early_side_body, [(FRAME, 128)] + HANDED_SHAPES, [SM] + [VM] * 4, 10...  10.4 us
    pallas_call x1, Pallas kernels, local(): call(early_main_body, HANDED_SHAPES, [SM, VM, VM], 10 ** 9, [wet] + WORK)  8.17 us
    ppermute x2, starting transfers between devices, local(): from_west = lax.ppermute(to_east, 'lon', to_east_pairs)  5.3 us
  transfers between devices with their start and end apart: 10, of which 2 were waited for; matrix products, arithmetic and copies ran while one was open for 0% of the time, Pallas kernels for 31%

profile of v7, /device:TPU:6, one launch (start us, length us, event | category | flops | bytes accessed | tf_op | source)
XLA Modules:
  0.0 107.5 jit_solution(3773613499402906688)
XLA Ops:
  0.0 0.0 copy-start.3
  0.0 0.0 copy-start.4
  0.0 0.1 pad_add_fusion.flag_ref
  0.1 0.0 copy-start
  0.1 1.1 %copy-done = f32[4,40,8,128]{3,2,1,0:T(8,128)S(1)} copy-done((f32[4,40,8,128]{3,2,1,0:T(8,128)S(1)}, f32[4,40,8,128]{3,2,1,0:T(8,128)}, u32[]{:S(2)}) %copy-start) | copy-done | bytes 655384
  1.2 0.0 copy-start.1
  1.2 0.9 copy-done.1
  2.1 0.0 copy-start.2
  2.1 0.7 copy-done.2
  2.8 0.9 shard_map.46
  3.6 1.9 %collective-permute-start = (f32[1608,128]{1,0:T(8,128)S(1)}, f32[1608,128]{1,0:T(8,128)S(1)}, u32[]{:S(2)}, u32[]{:S(2)}) collective-permute-start(f32[1608,128]{1,0:T(8,128)S(1)} %get-tuple-element.27.x_ref), channel_id=1, source_target_pairs={{0,1},{1,0},{2,3},{3,2},{4,5},{5,4},{6,7},{7,6},{8,9},{9,8},{10,11... | collective-permute-start | bytes 2469896 | tf_op jit(solution)/shard_map/ppermute | solution.py:807
  5.6 11.3 %collective-permute-start.1 = (f32[744,128]{1,0:T(8,128)S(1)}, f32[744,128]{1,0:T(8,128)S(1)}, u32[]{:S(2)}, u32[]{:S(2)}) collective-permute-start(f32[744,128]{1,0:T(8,128)S(1)} %get-tuple-element.28.a_in), channel_id=1, source_target_pairs={{1,2},{2,1},{3,4},{4,3},{5,6},{6,5},{7,8},{8,7},{9,10},{10,9},{11,... | collective-permute-start | bytes 1142792 | tf_op jit(solution)/shard_map/ppermute | solution.py:806
  16.9 0.0 collective-permute-done.y_ref
  16.9 1.9 %shard_map.47 = (f32[832,128]{1,0:T(8,128)S(1)}, f32[888,128]{1,0:T(8,128)S(1)}, f32[888,128]{1,0:T(8,128)S(1)}, f32[5432,128]{1,0:T(8,128)S(1)}, f32[272,128]{1,0:T(8,128)S(1)}, /*index=5*/f32[272,128]{1,0:T(8,128)S(1)}) custom-call(s32[2]{0:T(128)S(1)} %pad_add_fusion.flag_ref, f32[1608,128]{1,0:T(8,128)S(1)} %get-tuple-element.27.x_ref, ...), custom_call_target="tpu_custom_call" | custom-call | flops 1000000 | bytes 4194304 | tf_op jit(solution)/shard_map/pallas_call | solution.py:810
  18.8 3.4 %collective-permute-start.5 = (f32[272,128]{1,0:T(8,128)S(1)}, f32[272,128]{1,0:T(8,128)S(1)}, u32[]{:S(2)}, u32[]{:S(2)}) collective-permute-start(f32[272,128]{1,0:T(8,128)S(1)} %get-tuple-element.35), channel_id=1, source_target_pairs={{0,16},{16,32},{32,48},{48,64},{64,80},{80,96},{96,112},{112,128},... | collective-permute-start | bytes 417800 | tf_op jit(solution)/shard_map/ppermute | solution.py:817
  22.1 6.6 %collective-permute-start.6 = (f32[272,128]{1,0:T(8,128)S(1)}, f32[272,128]{1,0:T(8,128)S(1)}, u32[]{:S(2)}, u32[]{:S(2)}) collective-permute-start(f32[272,128]{1,0:T(8,128)S(1)} %get-tuple-element.36), channel_id=1, source_target_pairs={{16,0},{32,16},{48,32},{64,48},{80,64},{96,80},{112,96},{128,112},... | collective-permute-start | bytes 417800 | tf_op jit(solution)/shard_map/ppermute | solution.py:818
  28.8 0.0 copy-done.3
  28.8 0.0 copy-done.4
  28.8 0.1 broadcast_select_fusion
  28.9 1.9 %collective-permute-start.2 = (f32[832,128]{1,0:T(8,128)S(1)}, f32[832,128]{1,0:T(8,128)S(1)}, u32[]{:S(2)}, u32[]{:S(2)}) collective-permute-start(f32[832,128]{1,0:T(8,128)S(1)} %get-tuple-element.31), channel_id=1, source_target_pairs={{1,2},{2,1},{3,4},{4,3},{5,6},{6,5},{7,8},{8,7},{9,10},{10,9},{11,... | collective-permute-start | bytes 1277960 | tf_op jit(solution)/shard_map/ppermute | solution.py:819
  30.8 0.7 collective-permute-start.3
  31.5 0.1 broadcast_in_dim.2.rate_ref
  31.6 8.2 %shard_map.48 = (f32[448,128]{1,0:T(8,128)S(1)}, f32[1600,128]{1,0:T(8,128)S(1)}, f32[448,128]{1,0:T(8,128)S(1)}, f32[640,128]{1,0:T(8,128)S(1)}) custom-call(s32[2]{0:T(128)S(1)} %pad_add_fusion.flag_ref, f32[5432,128]{1,0:T(8,128)S(1)} %get-tuple-element.30.frame_ref.early_ref, f32[32,128]{1,0:T(8,128)S(1)} %broadcast_in_dim.2.rate_ref), custom_call_target="tpu_custom_call" | custom-call | flops 1000000000 | bytes 4194304 | tf_op jit(solution)/shard_map/pallas_call | solution.py:823
  39.7 0.0 collective-permute-done.5.east_ref
  39.8 0.7 collective-permute-start.4
  40.5 1.5 %collective-permute-done.6.west_ref = f32[272,128]{1,0:T(8,128)S(1)} collective-permute-done((f32[272,128]{1,0:T(8,128)S(1)}, f32[272,128]{1,0:T(8,128)S(1)}, u32[]{:S(2)}, u32[]{:S(2)}) %collective-permute-start.6) | collective-permute-done | bytes 139296 | tf_op jit(solution)/shard_map/ppermute | solution.py:818
  42.0 10.4 %shard_map.49 = (f32[5432,128]{1,0:T(8,128)S(1)}, f32[448,128]{1,0:T(8,128)S(1)}, f32[1600,128]{1,0:T(8,128)S(1)}, f32[448,128]{1,0:T(8,128)S(1)}, f32[640,128]{1,0:T(8,128)S(1)}) custom-call(s32[2]{0:T(128)S(1)} %pad_add_fusion.flag_ref, f32[5432,128]{1,0:T(8,128)S(1)} %get-tuple-element.30.frame_ref.early_ref, f32[32,128]{1,0:T(8,128)S(1)} %broadcast_in_dim.2.rate_ref, ...), custom_call_target="tpu_custom_call" | custom-call | flops 99999997952 | bytes 4194304 | tf_op jit(solution)/shard_map/pallas_call | solution.py:824
  52.4 0.0 collective-permute-done.1.a_ref
  52.4 2.4 %collective-permute-done.2.b_ref = f32[832,128]{1,0:T(8,128)S(1)} collective-permute-done((f32[832,128]{1,0:T(8,128)S(1)}, f32[832,128]{1,0:T(8,128)S(1)}, u32[]{:S(2)}, u32[]{:S(2)}) %collective-permute-start.2) | collective-permute-done | bytes 426016 | tf_op jit(solution)/shard_map/ppermute | solution.py:819
  54.8 0.0 collective-permute-done.3.fold_a_ref
  54.8 0.0 collective-permute-done.4.fold_b_ref
  54.8 1.7 %shard_map.50 = (f32[5432,128]{1,0:T(8,128)S(1)}, f32[88,128]{1,0:T(8,128)S(1)}, f32[152,128]{1,0:T(8,128)S(1)}, f32[152,128]{1,0:T(8,128)S(1)}) custom-call(s32[2]{0:T(128)S(1)} %pad_add_fusion.flag_ref, f32[5432,128]{1,0:T(8,128)S(1)} %get-tuple-element.30.frame_ref.early_ref, f32[744,128]{1,0:T(8,128)S(1)} %collective-permute-done.1.a_ref, ...), custom_call_target="tpu_custom_call" | custom-call | flops 1000000 | bytes 4194304 | tf_op jit(solution)/shard_map/pallas_call | solution.py:827
  56.5 10.8 %collective-permute-start.7 = (f32[88,128]{1,0:T(8,128)S(1)}, f32[88,128]{1,0:T(8,128)S(1)}, u32[]{:S(2)}, u32[]{:S(2)}) collective-permute-start(f32[88,128]{1,0:T(8,128)S(1)} %get-tuple-element.39), channel_id=1, source_target_pairs={{0,1},{1,0},{2,3},{3,2},{4,5},{5,4},{6,7},{7,6},{8,9},{9,8},{10,11... | collective-permute-start | bytes 135176 | tf_op jit(solution)/shard_map/ppermute | solution.py:834
  67.3 1.9 %collective-permute-start.8 = (f32[152,128]{1,0:T(8,128)S(1)}, f32[152,128]{1,0:T(8,128)S(1)}, u32[]{:S(2)}, u32[]{:S(2)}) collective-permute-start(f32[152,128]{1,0:T(8,128)S(1)} %get-tuple-element.41), channel_id=1, source_target_pairs={{0,16},{16,32},{32,48},{48,64},{64,80},{80,96},{96,112},{112,128},... | collective-permute-start | bytes 233480 | tf_op jit(solution)/shard_map/ppermute | solution.py:835
  69.2 10.1 %collective-permute-start.9 = (f32[152,128]{1,0:T(8,128)S(1)}, f32[152,128]{1,0:T(8,128)S(1)}, u32[]{:S(2)}, u32[]{:S(2)}) collective-permute-start(f32[152,128]{1,0:T(8,128)S(1)} %get-tuple-element.42), channel_id=1, source_target_pairs={{16,0},{32,16},{48,32},{64,48},{80,64},{96,80},{112,96},{128,112},... | collective-permute-start | bytes 233480 | tf_op jit(solution)/shard_map/ppermute | solution.py:836
  79.3 0.0 collective-permute-done.7.far_ref
  79.3 12.5 %shard_map.51.main_ref = f32[4,40,8,128]{3,2,1,0:T(8,128)S(1)} custom-call(s32[2]{0:T(128)S(1)} %pad_add_fusion.flag_ref, f32[5432,128]{1,0:T(8,128)S(1)} %get-tuple-element.38.frame_ref.frame_in, f32[88,128]{1,0:T(8,128)S(1)} %collective-permute-done.7.far_ref, f32[32,128]{1,0:T(8,128)S(1)} %broadcast_in_dim.2.rate_ref, ...), custom_call_target="tpu_custom_call" | custom-call | flops 1000000000 | bytes 4194304 | tf_op jit(solution)/shard_map/pallas_call | solution.py:838
  91.8 0.0 collective-permute-done.8.east_ref
  91.8 0.0 collective-permute-done.9.west_ref
  91.8 15.7 %shard_map.52 = f32[4,40,8,128]{3,2,1,0:T(8,128)} custom-call(s32[2]{0:T(128)S(1)} %pad_add_fusion.flag_ref, f32[5432,128]{1,0:T(8,128)S(1)} %get-tuple-element.38.frame_ref.frame_in, f32[88,128]{1,0:T(8,128)S(1)} %collective-permute-done.7.far_ref, f32[32,128]{1,0:T(8,128)S(1)} %broadcast_in_dim.2.rate_ref, f32[5432,128]{1,0:T(8,128)S(1)} %get-tuple-element.40.side_in, ...), custom_call_target="tpu_custom_call" | custom-call | flops 1000000000 | bytes 4194304 | tf_op jit(solution)/shard_map/pallas_call | solution.py:839
Async XLA Ops:
  0.0 28.8 %copy-start.3 = (s32[32]{0:T(128)S(1)}, s32[32]{0:T(128)}, u32[]{:S(2)}) copy-start(s32[32]{0:T(128)} %constant.39) | copy-start | bytes 388
  0.0 28.8 %copy-start.4 = (s32[32]{0:T(128)S(1)}, s32[32]{0:T(128)}, u32[]{:S(2)}) copy-start(s32[32]{0:T(128)} %constant.34.clone) | copy-start | bytes 388
  0.1 1.1 %copy-start = (f32[4,40,8,128]{3,2,1,0:T(8,128)S(1)}, f32[4,40,8,128]{3,2,1,0:T(8,128)}, u32[]{:S(2)}) copy-start(f32[4,40,8,128]{3,2,1,0:T(8,128)} %param.4) | copy-start | bytes 1966084
  1.2 0.9 copy-start.1
  2.1 0.7 copy-start.2
  3.6 13.2 %collective-permute-start = (f32[1608,128]{1,0:T(8,128)S(1)}, f32[1608,128]{1,0:T(8,128)S(1)}, u32[]{:S(2)}, u32[]{:S(2)}) collective-permute-start(f32[1608,128]{1,0:T(8,128)S(1)} %get-tuple-element.27.x_ref), channel_id=1, source_target_pairs={{0,1},{1,0},{2,3},{3,2},{4,5},{5,4},{6,7},{7,6},{8,9},{9,8},{10,11... | collective-permute-start | bytes 2469896 | tf_op jit(solution)/shard_map/ppermute | solution.py:807
  5.6 46.8 %collective-permute-start.1 = (f32[744,128]{1,0:T(8,128)S(1)}, f32[744,128]{1,0:T(8,128)S(1)}, u32[]{:S(2)}, u32[]{:S(2)}) collective-permute-start(f32[744,128]{1,0:T(8,128)S(1)} %get-tuple-element.28.a_in), channel_id=1, source_target_pairs={{1,2},{2,1},{3,4},{4,3},{5,6},{6,5},{7,8},{8,7},{9,10},{10,9},{11,... | collective-permute-start | bytes 1142792 | tf_op jit(solution)/shard_map/ppermute | solution.py:806
  18.8 21.0 %collective-permute-start.5 = (f32[272,128]{1,0:T(8,128)S(1)}, f32[272,128]{1,0:T(8,128)S(1)}, u32[]{:S(2)}, u32[]{:S(2)}) collective-permute-start(f32[272,128]{1,0:T(8,128)S(1)} %get-tuple-element.35), channel_id=1, source_target_pairs={{0,16},{16,32},{32,48},{48,64},{64,80},{80,96},{96,112},{112,128},... | collective-permute-start | bytes 417800 | tf_op jit(solution)/shard_map/ppermute | solution.py:817
  22.1 19.8 %collective-permute-start.6 = (f32[272,128]{1,0:T(8,128)S(1)}, f32[272,128]{1,0:T(8,128)S(1)}, u32[]{:S(2)}, u32[]{:S(2)}) collective-permute-start(f32[272,128]{1,0:T(8,128)S(1)} %get-tuple-element.36), channel_id=1, source_target_pairs={{16,0},{32,16},{48,32},{64,48},{80,64},{96,80},{112,96},{128,112},... | collective-permute-start | bytes 417800 | tf_op jit(solution)/shard_map/ppermute | solution.py:818
  28.9 25.9 %collective-permute-start.2 = (f32[832,128]{1,0:T(8,128)S(1)}, f32[832,128]{1,0:T(8,128)S(1)}, u32[]{:S(2)}, u32[]{:S(2)}) collective-permute-start(f32[832,128]{1,0:T(8,128)S(1)} %get-tuple-element.31), channel_id=1, source_target_pairs={{1,2},{2,1},{3,4},{4,3},{5,6},{6,5},{7,8},{8,7},{9,10},{10,9},{11,... | collective-permute-start | bytes 1277960 | tf_op jit(solution)/shard_map/ppermute | solution.py:819
  30.8 24.0 %collective-permute-start.3 = (f32[888,128]{1,0:T(8,128)S(1)}, f32[888,128]{1,0:T(8,128)S(1)}, u32[]{:S(2)}, u32[]{:S(2)}) collective-permute-start(f32[888,128]{1,0:T(8,128)S(1)} %get-tuple-element.32), channel_id=1, source_target_pairs={{15,15},{31,511},{47,495},{63,479},{79,463},{95,447},{111,431},{12... | collective-permute-start | bytes 1363976 | tf_op jit(solution)/shard_map/ppermute | solution.py:820
  39.8 15.1 %collective-permute-start.4 = (f32[888,128]{1,0:T(8,128)S(1)}, f32[888,128]{1,0:T(8,128)S(1)}, u32[]{:S(2)}, u32[]{:S(2)}) collective-permute-start(f32[888,128]{1,0:T(8,128)S(1)} %get-tuple-element.33), channel_id=1, source_target_pairs={{15,511},{31,495},{47,479},{63,463},{79,447},{95,431},{111,415},{1... | collective-permute-start | bytes 1363976 | tf_op jit(solution)/shard_map/ppermute | solution.py:821
  56.5 22.8 %collective-permute-start.7 = (f32[88,128]{1,0:T(8,128)S(1)}, f32[88,128]{1,0:T(8,128)S(1)}, u32[]{:S(2)}, u32[]{:S(2)}) collective-permute-start(f32[88,128]{1,0:T(8,128)S(1)} %get-tuple-element.39), channel_id=1, source_target_pairs={{0,1},{1,0},{2,3},{3,2},{4,5},{5,4},{6,7},{7,6},{8,9},{9,8},{10,11... | collective-permute-start | bytes 135176 | tf_op jit(solution)/shard_map/ppermute | solution.py:834
  67.3 24.6 %collective-permute-start.8 = (f32[152,128]{1,0:T(8,128)S(1)}, f32[152,128]{1,0:T(8,128)S(1)}, u32[]{:S(2)}, u32[]{:S(2)}) collective-permute-start(f32[152,128]{1,0:T(8,128)S(1)} %get-tuple-element.41), channel_id=1, source_target_pairs={{0,16},{16,32},{32,48},{48,64},{64,80},{80,96},{96,112},{112,128},... | collective-permute-start | bytes 233480 | tf_op jit(solution)/shard_map/ppermute | solution.py:835
  69.2 22.6 %collective-permute-start.9 = (f32[152,128]{1,0:T(8,128)S(1)}, f32[152,128]{1,0:T(8,128)S(1)}, u32[]{:S(2)}, u32[]{:S(2)}) collective-permute-start(f32[152,128]{1,0:T(8,128)S(1)} %get-tuple-element.42), channel_id=1, source_target_pairs={{16,0},{32,16},{48,32},{64,48},{80,64},{96,80},{112,96},{128,112},... | collective-permute-start | bytes 233480 | tf_op jit(solution)/shard_map/ppermute | solution.py:836
